TPU v7x, 256 devices: a whole 4x4x8 slice. The times are simulated.
256 devices in a mesh: queue: 128 (over y, z, x_lo, core), heads: 2 (over x_hi).
Axes of the slice: x: 4 (x_hi: 2, x_lo: 2; x = x_hi * 2 + x_lo), y: 4, z: 8, core: 2. Of those that a mesh axis runs over, the one named last changes fastest.
Arguments:
- frames: bfloat16 [32768, 1536], P('queue', 'heads'), may hold values from -6 to 6
- fresh_groups: bfloat16 [3, 256, 1536], P(None, None, 'heads'), may hold values from -6 to 6
- level_index: int32 [128], replicated, may hold values from 0 to 63, as said below
- window_start: int32 [128], replicated, may hold values from 0 to 128
- mod_shift: bfloat16 [64, 1536], P(None, 'heads'), may hold values from -3 to 3
- mod_scale: bfloat16 [64, 1536], P(None, 'heads'), may hold values from -1.796875 to 1.796875
- mod_gate: bfloat16 [64, 1536], P(None, 'heads'), may hold values from -10 to 10
- w_qkv: bfloat16 [1536, 3, 1536], P(None, None, 'heads'), may hold values from -1 to 1
- q_gain: float32 [1536], P('heads'), may hold values from 0.5 to 5
- k_gain: float32 [1536], P('heads'), may hold values from 0.5 to 5
- w_out: bfloat16 [1536, 1536], P('heads'), may hold values from -0.5 to 0.5
Outputs:
- queue_state: bfloat16 [32768, 1536], P('queue', 'heads')
- last_velocity: bfloat16 [32768, 1536], P('queue', 'heads')
Inputs may be any that keep to these rules, and one draw needn't show every extreme that they name: `level_index`: never falls from slot to slot; the first slot holds 0 and the last 63.
All inputs are finite; a program needn't handle non-finite values.
Results may differ from a plain program's by a relative error of at most 0.04.
Values may be sent and summed in bfloat16 or wider, within the bound.
No kernel may reach another device: no remote copies, remote signals or barrier semaphores. Data moves between devices by JAX's collectives and lax.ppermute only.
A program may use at most 128 MiB of HBM per device.

v0:
```python
import jax
import jax.numpy as jnp
from jax import lax
from jax.sharding import PartitionSpec as P

HD = 128
STEPS = 3
LEVELS = 64


def shifted(block, axis, distance):
    devices = range(lax.axis_size(axis))
    route = [(i - distance, i) for i in devices if i - distance in devices]
    return lax.ppermute(block, axis, route)


def modulate(group, table):
    values = group.astype(jnp.float32)
    spread = jnp.sqrt(jnp.mean(values * values, axis=-1, keepdims=True) + 1e-06)
    return (
        values / spread * (1.0 + table[1].astype(jnp.float32)) + table[0].astype(jnp.float32)
    ).astype(jnp.bfloat16)


def head_norm(block, gain):
    shaped = block.reshape(block.shape[0], -1, HD)
    spread = jnp.sqrt(jnp.mean(shaped * shaped, axis=-1, keepdims=True) + 1e-06)
    return ((shaped / spread).reshape(block.shape) * gain).astype(jnp.bfloat16)


def attend(query, keys, values, near_keys, near_values, start, alive):
    rows = query.shape[0]
    heads = query.shape[1] // HD
    qh = query.reshape(rows, heads, HD)
    scale = 1.0 / jnp.sqrt(jnp.float32(HD))
    own = (
        jnp.einsum(
            "rhe,she->hrs", qh, keys.reshape(rows, heads, HD), preferred_element_type=jnp.float32
        )
        * scale
    )
    near = (
        jnp.einsum(
            "rhe,she->hrs",
            qh,
            near_keys.reshape(rows, heads, HD),
            preferred_element_type=jnp.float32,
        )
        * scale
    )
    visible = (jnp.arange(rows, dtype=jnp.int32) >= start) & alive
    near = jnp.where(visible[None, None, :], near, jnp.float32(-1e30))
    top = jnp.maximum(jnp.max(own, axis=-1, keepdims=True), jnp.max(near, axis=-1, keepdims=True))
    own_exp = jnp.exp(own - top)
    near_exp = jnp.exp(near - top)
    total = jnp.sum(own_exp, axis=-1, keepdims=True) + jnp.sum(near_exp, axis=-1, keepdims=True)
    own_w = (own_exp / total).astype(jnp.bfloat16)
    near_w = (near_exp / total).astype(jnp.bfloat16)
    out = jnp.einsum(
        "hrs,she->rhe", own_w, values.reshape(rows, heads, HD), preferred_element_type=jnp.float32
    )
    out = out + jnp.einsum(
        "hrs,she->rhe",
        near_w,
        near_values.reshape(rows, heads, HD),
        preferred_element_type=jnp.float32,
    )
    return out.reshape(rows, heads * HD).astype(jnp.bfloat16)


def on_device(
    frames,
    fresh_groups,
    level_index,
    window_start,
    mod_shift,
    mod_scale,
    mod_gate,
    w_qkv,
    q_gain,
    k_gain,
    w_out,
):
    position = lax.axis_index("queue")
    slot_count = lax.axis_size("queue")
    level = level_index[position]
    below = level_index[jnp.maximum(position - 1, 0)]
    t_cur = (level.astype(jnp.float32) + 1.0) / LEVELS
    t_next = jnp.where(position > 0, (below.astype(jnp.float32) + 1.0) / LEVELS, jnp.float32(0.0))
    step_size = t_next - t_cur
    start = window_start[position]
    alive = position > 0
    width = w_qkv.shape[2]
    flat_weights = w_qkv.reshape(w_qkv.shape[0], 3 * width)
    own_rows = jnp.stack([mod_shift[level], mod_scale[level]])
    gate_row = mod_gate[level].astype(jnp.float32)
    state = frames
    velocity = jnp.zeros(frames.shape, jnp.float32)
    near_keys = None
    near_values = None
    for step in range(STEPS):
        whole, table = (
            lax.all_gather(state, "heads", axis=1, tiled=True),
            lax.all_gather(own_rows, "heads", axis=1, tiled=True),
        )
        moved = modulate(whole, table)
        qkv = jnp.dot(moved, flat_weights, preferred_element_type=jnp.float32).reshape(
            moved.shape[0], 3, width
        )
        query = head_norm(qkv[:, 0], q_gain)
        keys = head_norm(qkv[:, 1], k_gain)
        values = qkv[:, 2].astype(jnp.bfloat16)
        near_keys, near_values = shifted((keys, values), "queue", 1)
        attended = attend(query, keys, values, near_keys, near_values, start, alive)
        term = jnp.dot(attended, w_out, preferred_element_type=jnp.float32)
        product = lax.psum_scatter(
            term.astype(jnp.bfloat16), "heads", scatter_dimension=1, tiled=True
        ).astype(jnp.float32)
        velocity = gate_row * product
        updated = (state.astype(jnp.float32) + step_size * velocity).astype(jnp.bfloat16)
        advanced = shifted(updated, "queue", -1)
        state = jnp.where(position == slot_count - 1, fresh_groups[step], advanced)
    return (state, velocity.astype(jnp.bfloat16))


def solution(mesh):
    placed = (
        P("queue", "heads"),
        P(None, None, "heads"),
        P(),
        P(),
        P(None, "heads"),
        P(None, "heads"),
        P(None, "heads"),
        P(None, None, "heads"),
        P("heads"),
        P("heads"),
        P("heads", None),
    )
    return jax.shard_map(
        on_device,
        mesh=mesh,
        in_specs=placed,
        out_specs=(P("queue", "heads"), P("queue", "heads")),
        check_vma=False,
    )
```

profile of v0, /device:TPU:12, one launch (start us, length us, event | category | flops | bytes accessed | tf_op | source)
XLA Modules:
  0.0 310.4 jit_solution(15246833195985867280)
XLA Ops:
  11.4 5.8 %all_gather.15 = bf16[2,1536]{1,0:T(2,128)(2,1)S(1)} all-gather(bf16[2,768]{1,0:T(2,128)(2,1)S(1)} %pad_maximum_fusion), channel_id=1, replica_groups=mesh['queue'=128,'heads'=2] {'heads'}, dimensions={1}, use_global_device_ids=true | all-gather | bytes 9216 | tf_op jit(solution)/shard_map/all_gather | solution.py:104
  17.3 12.1 %all_gather.14 = bf16[256,1536]{1,0:T(8,128)(2,1)S(1)} all-gather(bf16[256,768]{1,0:T(8,128)(2,1)} %param.11), channel_id=1, replica_groups=mesh['queue'=128,'heads'=2] {'heads'}, dimensions={1}, use_global_device_ids=true | all-gather | bytes 1179648 | tf_op jit(solution)/shard_map/all_gather | solution.py:103
  29.6 10.3 %copy.37 = bf16[1536,3,768]{0,2,1:T(8,128)(2,1)} copy(bf16[1536,3,768]{2,0,1:T(8,128)(2,1)} %param.18) | data formatting | bytes 14155776 | tf_op args[7]
  39.9 5.1 %fusion.4 = f32[256,3,768]{2,0,1:T(8,128)S(1)} fusion(bf16[1536,3,768]{0,2,1:T(8,128)(2,1)} %copy.37, bf16[256,1536]{1,0:T(8,128)(2,1)S(1)} %all_gather.14, f32[1536]{0:T(1024)S(1)} %get-tuple-element.9, f32[1536]{0:T(1024)S(1)} %get-tuple-element.8, f32[256]{0:T(256)S(1)} %add_sqrt_fusion.8), kind=kOutput, calls=%fused_computation.4 | convolution fusion | flops 1813905408 | bytes 10236928 | tf_op jit(solution)/shard_map/dot_general | solution.py:107
  51.6 2.3 copy.43
  53.9 2.2 fusion.38
  56.1 3.2 %collective-permute-start = (bf16[256,768]{1,0:T(8,128)(2,1)}, bf16[256,768]{1,0:T(8,128)(2,1)}, u32[]{:S(2)}, u32[]{:S(2)}) collective-permute-start(bf16[256,768]{1,0:T(8,128)(2,1)} %fusion.38), channel_id=1, source_target_pairs={{0,2},{2,4},{4,6},{6,8},{8,10},{10,12},{12,14},{14,16},{16,18},{18... | collective-permute-start | bytes 1179656 | tf_op jit(solution)/shard_map/ppermute | solution.py:14
  62.1 2.3 copy.39
  66.2 3.0 fusion.68
  76.2 2.0 fusion.24
  82.1 22.5 %reduce-scatter.4.cloned.1.call-done = bf16[256,768]{1,0:T(8,128)(2,1)} async-done(((bf16[256,1536]{1,0:T(8,128)(2,1)}), bf16[256,768]{1,0:T(8,128)(2,1)}) %reduce-scatter.4.cloned.1.call-update) | async-done | bytes 393232 | tf_op jit(solution)/shard_map/reduce_scatter | solution.py:116
  105.7 6.1 %collective-permute-start.2 = (bf16[256,768]{1,0:T(8,128)(2,1)S(1)}, bf16[256,768]{1,0:T(8,128)(2,1)S(1)}, u32[]{:S(2)}, u32[]{:S(2)}) collective-permute-start(bf16[256,768]{1,0:T(8,128)(2,1)S(1)} %add_convert_fusion.2), channel_id=1, source_target_pairs={{2,0},{4,2},{6,4},{8,6},{10,8},{12,10},{14,12},{16,14},{18,16},{20... | collective-permute-start | bytes 1179656 | tf_op jit(solution)/shard_map/ppermute | solution.py:14
  111.9 5.2 %collective-permute-done.2 = bf16[256,768]{1,0:T(8,128)(2,1)S(1)} collective-permute-done((bf16[256,768]{1,0:T(8,128)(2,1)S(1)}, bf16[256,768]{1,0:T(8,128)(2,1)S(1)}, u32[]{:S(2)}, u32[]{:S(2)}) %collective-permute-start.2) | collective-permute-done | bytes 393248 | tf_op jit(solution)/shard_map/ppermute | solution.py:14
  118.1 11.3 %all_gather.16 = bf16[256,1536]{1,0:T(8,128)(2,1)S(1)} all-gather(bf16[256,768]{1,0:T(8,128)(2,1)S(1)} %bitcast_select_fusion), channel_id=1, replica_groups=mesh['queue'=128,'heads'=2] {'heads'}, dimensions={1}, use_global_device_ids=true | all-gather | bytes 1179648 | tf_op jit(solution)/shard_map/all_gather | solution.py:103
  129.7 5.1 %fusion.2 = f32[256,3,768]{2,0,1:T(8,128)S(1)} fusion(bf16[1536,3,768]{0,2,1:T(8,128)(2,1)} %copy.37, bf16[256,1536]{1,0:T(8,128)(2,1)S(1)} %all_gather.16, f32[256]{0:T(256)S(1)} %add_sqrt_fusion.7, f32[1536]{0:T(1024)S(1)} %copy-done.25, f32[1536]{0:T(1024)S(1)} %copy-done.22), kind=kOutput, calls=%fused_computation.2 | convolution fusion | flops 1813905408 | bytes 10236928 | tf_op jit(solution)/shard_map/dot_general | solution.py:107
  142.0 2.3 copy.52
  147.1 2.3 copy.55
  151.0 2.1 collective-permute-start.3
  155.0 8.2 %collective-permute-done.3 = bf16[256,768]{1,0:T(8,128)(2,1)} collective-permute-done((bf16[256,768]{1,0:T(8,128)(2,1)S(1)}, bf16[256,768]{1,0:T(8,128)(2,1)}, u32[]{:S(2)}, u32[]{:S(2)}) %collective-permute-start.3) | collective-permute-done | bytes 393248 | tf_op jit(solution)/shard_map/ppermute | solution.py:14
  170.7 2.0 fusion.25
  174.5 22.2 %reduce-scatter.6.cloned.1.call-done = bf16[256,768]{1,0:T(8,128)(2,1)} async-done(((bf16[256,1536]{1,0:T(8,128)(2,1)}), bf16[256,768]{1,0:T(8,128)(2,1)}) %reduce-scatter.6.cloned.1.call-update) | async-done | bytes 393232 | tf_op jit(solution)/shard_map/reduce_scatter | solution.py:116
  197.9 6.3 %collective-permute-start.5 = (bf16[256,768]{1,0:T(8,128)(2,1)S(1)}, bf16[256,768]{1,0:T(8,128)(2,1)S(1)}, u32[]{:S(2)}, u32[]{:S(2)}) collective-permute-start(bf16[256,768]{1,0:T(8,128)(2,1)S(1)} %add_convert_fusion.1), channel_id=1, source_target_pairs={{2,0},{4,2},{6,4},{8,6},{10,8},{12,10},{14,12},{16,14},{18,16},{20... | collective-permute-start | bytes 1179656 | tf_op jit(solution)/shard_map/ppermute | solution.py:14
  204.1 5.3 %collective-permute-done.5 = bf16[256,768]{1,0:T(8,128)(2,1)S(1)} collective-permute-done((bf16[256,768]{1,0:T(8,128)(2,1)S(1)}, bf16[256,768]{1,0:T(8,128)(2,1)S(1)}, u32[]{:S(2)}, u32[]{:S(2)}) %collective-permute-start.5) | collective-permute-done | bytes 393248 | tf_op jit(solution)/shard_map/ppermute | solution.py:14
  210.5 11.3 %all_gather.17 = bf16[256,1536]{1,0:T(8,128)(2,1)S(1)} all-gather(bf16[256,768]{1,0:T(8,128)(2,1)S(1)} %bitcast_select_fusion.1), channel_id=1, replica_groups=mesh['queue'=128,'heads'=2] {'heads'}, dimensions={1}, use_global_device_ids=true | all-gather | bytes 1179648 | tf_op jit(solution)/shard_map/all_gather | solution.py:103
  222.0 5.1 %fusion = f32[256,3,768]{2,0,1:T(8,128)S(1)} fusion(bf16[1536,3,768]{0,2,1:T(8,128)(2,1)} %copy.37, bf16[256,1536]{1,0:T(8,128)(2,1)S(1)} %all_gather.17, f32[256]{0:T(256)S(1)} %add_sqrt_fusion.6, f32[1536]{0:T(1024)S(1)} %copy-done.26, f32[1536]{0:T(1024)S(1)} %copy-done.23), kind=kOutput, calls=%fused_computation | convolution fusion | flops 1813905408 | bytes 10236928 | tf_op jit(solution)/shard_map/dot_general | solution.py:107
  234.3 2.3 copy.64
  239.3 2.3 copy.67
  247.0 8.4 %collective-permute-done.6 = bf16[256,768]{1,0:T(8,128)(2,1)} collective-permute-done((bf16[256,768]{1,0:T(8,128)(2,1)S(1)}, bf16[256,768]{1,0:T(8,128)(2,1)}, u32[]{:S(2)}, u32[]{:S(2)}) %collective-permute-start.6) | collective-permute-done | bytes 393248 | tf_op jit(solution)/shard_map/ppermute | solution.py:14
  262.8 2.0 fusion.26
  266.6 22.2 %reduce-scatter.8.cloned.1.call-done = bf16[256,768]{1,0:T(8,128)(2,1)} async-done(((bf16[256,1536]{1,0:T(8,128)(2,1)}), bf16[256,768]{1,0:T(8,128)(2,1)}) %reduce-scatter.8.cloned.1.call-update) | async-done | bytes 393232 | tf_op jit(solution)/shard_map/reduce_scatter | solution.py:116
  290.7 6.1 %collective-permute-start.8 = (bf16[256,768]{1,0:T(8,128)(2,1)S(1)}, bf16[256,768]{1,0:T(8,128)(2,1)S(1)}, u32[]{:S(2)}, u32[]{:S(2)}) collective-permute-start(bf16[256,768]{1,0:T(8,128)(2,1)S(1)} %get-tuple-element.17), channel_id=1, source_target_pairs={{2,0},{4,2},{6,4},{8,6},{10,8},{12,10},{14,12},{16,14},{18,16},{20... | collective-permute-start | bytes 1179656 | tf_op jit(solution)/shard_map/ppermute | solution.py:14
  296.8 5.3 %collective-permute-done.8 = bf16[256,768]{1,0:T(8,128)(2,1)S(1)} collective-permute-done((bf16[256,768]{1,0:T(8,128)(2,1)S(1)}, bf16[256,768]{1,0:T(8,128)(2,1)S(1)}, u32[]{:S(2)}, u32[]{:S(2)}) %collective-permute-start.8) | collective-permute-done | bytes 393248 | tf_op jit(solution)/shard_map/ppermute | solution.py:14
  (159 shorter events, 78.4 us)
Async XLA Ops:
  7.2 71.1 %copy-start = (bf16[768,1536]{1,0:T(8,128)(2,1)S(1)}, bf16[768,1536]{1,0:T(8,128)(2,1)}, u32[]{:S(2)}) copy-start(bf16[768,1536]{1,0:T(8,128)(2,1)} %param.21) | copy-start | bytes 7077892
  7.2 97.4 %reduce-scatter.4.cloned.1.call-start = ((), (), s32[]{:S(2)}) async-start(), calls=%async_computation.3 | async-start | bytes 1179648 | tf_op jit(solution)/shard_map/reduce_scatter | solution.py:116
  17.3 22.6 %copy-start.21 = (f32[1536]{0:T(1024)}, f32[1536]{0:T(1024)S(1)}, u32[]{:S(2)}) copy-start(f32[1536]{0:T(1024)S(1)} %get-tuple-element.8) | copy-start | bytes 18436
  17.3 22.6 %copy-start.24 = (f32[1536]{0:T(1024)}, f32[1536]{0:T(1024)S(1)}, u32[]{:S(2)}) copy-start(f32[1536]{0:T(1024)S(1)} %get-tuple-element.9) | copy-start | bytes 18436
  45.0 4.1 %copy-start.2 = (f32[256,3,768]{2,0,1:T(8,128)}, f32[256,3,768]{2,0,1:T(8,128)S(1)}, u32[]{:S(2)}) copy-start(f32[256,3,768]{2,0,1:T(8,128)S(1)} %fusion.4) | copy-start | bytes 7077892
  45.9 29.1 %collective-permute-start.1 = (bf16[256,768]{1,0:T(8,128)(2,1)}, bf16[256,768]{1,0:T(8,128)(2,1)}, u32[]{:S(2)}, u32[]{:S(2)}) collective-permute-start(bf16[256,768]{1,0:T(8,128)(2,1)} %slice_bitcast_fusion), channel_id=1, source_target_pairs={{0,2},{2,4},{4,6},{6,8},{8,10},{10,12},{12,14},{14,16},{16,18},{18... | collective-permute-start | bytes 1179656 | tf_op jit(solution)/shard_map/ppermute | solution.py:14
  50.5 3.4 %copy-start.16 = (f32[768]{0:T(1024)S(1)}, f32[768]{0:T(1024)}, u32[]{:S(2)}) copy-start(f32[768]{0:T(1024)} %param.20) | copy-start | bytes 9220
  53.9 6.6 %copy-start.32 = (s32[128]{0:T(128)S(1)}, s32[128]{0:T(128)}, u32[]{:S(2)}) copy-start(s32[128]{0:T(128)} %param.14) | copy-start | bytes 1540
  56.1 13.2 %collective-permute-start = (bf16[256,768]{1,0:T(8,128)(2,1)}, bf16[256,768]{1,0:T(8,128)(2,1)}, u32[]{:S(2)}, u32[]{:S(2)}) collective-permute-start(bf16[256,768]{1,0:T(8,128)(2,1)} %fusion.38), channel_id=1, source_target_pairs={{0,2},{2,4},{4,6},{6,8},{8,10},{10,12},{12,14},{14,16},{16,18},{18... | collective-permute-start | bytes 1179656 | tf_op jit(solution)/shard_map/ppermute | solution.py:14
  61.2 5.1 %copy-start.29 = (f32[768]{0:T(1024)S(1)}, f32[768]{0:T(1024)}, u32[]{:S(2)}) copy-start(f32[768]{0:T(1024)} %param.19) | copy-start | bytes 9220
  66.2 4.2 %copy-start.33 = (pred[256]{0:T(512)(128)(4,1)}, pred[256]{0:T(512)(128)(4,1)S(1)}, u32[]{:S(2)}) copy-start(pred[256]{0:T(512)(128)(4,1)S(1)} %compare_and_fusion) | copy-start | bytes 772
  78.2 26.3 %copy-start.12 = (bf16[256,768]{1,0:T(8,128)(2,1)S(1)}, bf16[256,768]{1,0:T(8,128)(2,1)}, u32[]{:S(2)}) copy-start(bf16[256,768]{1,0:T(8,128)(2,1)} %param.11) | copy-start | bytes 1179652
  80.0 116.7 %reduce-scatter.6.cloned.1.call-start = ((), (), s32[]{:S(2)}) async-start(), calls=%async_computation.4 | async-start | bytes 1179648 | tf_op jit(solution)/shard_map/reduce_scatter | solution.py:116
  105.7 11.4 %collective-permute-start.2 = (bf16[256,768]{1,0:T(8,128)(2,1)S(1)}, bf16[256,768]{1,0:T(8,128)(2,1)S(1)}, u32[]{:S(2)}, u32[]{:S(2)}) collective-permute-start(bf16[256,768]{1,0:T(8,128)(2,1)S(1)} %add_convert_fusion.2), channel_id=1, source_target_pairs={{2,0},{4,2},{6,4},{8,6},{10,8},{12,10},{14,12},{16,14},{18,16},{20... | collective-permute-start | bytes 1179656 | tf_op jit(solution)/shard_map/ppermute | solution.py:14
  111.8 17.9 %copy-start.22 = (f32[1536]{0:T(1024)S(1)}, f32[1536]{0:T(1024)}, u32[]{:S(2)}) copy-start(f32[1536]{0:T(1024)} %copy-done.21) | copy-start | bytes 18436
  111.8 17.9 %copy-start.25 = (f32[1536]{0:T(1024)S(1)}, f32[1536]{0:T(1024)}, u32[]{:S(2)}) copy-start(f32[1536]{0:T(1024)} %copy-done.24) | copy-start | bytes 18436
  138.6 31.0 %collective-permute-start.4 = (bf16[256,768]{1,0:T(8,128)(2,1)}, bf16[256,768]{1,0:T(8,128)(2,1)}, u32[]{:S(2)}, u32[]{:S(2)}) collective-permute-start(bf16[256,768]{1,0:T(8,128)(2,1)} %slice_bitcast_fusion.1), channel_id=1, source_target_pairs={{0,2},{2,4},{4,6},{6,8},{8,10},{10,12},{12,14},{14,16},{16,18},{18... | collective-permute-start | bytes 1179656 | tf_op jit(solution)/shard_map/ppermute | solution.py:14
  149.4 3.7 %copy-start.4 = (f32[256,1,768]{0,2,1:T(8,128)S(1)}, f32[256,1,768]{0,2,1:T(8,128)}, u32[]{:S(2)}) copy-start(f32[256,1,768]{0,2,1:T(8,128)} %copy.52) | copy-start | bytes 2359300
  149.4 3.7 %copy-start.18 = (f32[256,6]{0,1:T(8,128)S(1)}, f32[256,6]{0,1:T(8,128)}, u32[]{:S(2)}) copy-start(f32[256,6]{0,1:T(8,128)} %copy-done.17) | copy-start | bytes 18436
  149.4 3.7 %copy-start.30 = (f32[768]{0:T(1024)S(1)}, f32[768]{0:T(1024)}, u32[]{:S(2)}) copy-start(f32[768]{0:T(1024)} %param.19) | copy-start | bytes 9220
  151.0 12.2 %collective-permute-start.3 = (bf16[256,768]{1,0:T(8,128)(2,1)S(1)}, bf16[256,768]{1,0:T(8,128)(2,1)}, u32[]{:S(2)}, u32[]{:S(2)}) collective-permute-start(bf16[256,768]{1,0:T(8,128)(2,1)S(1)} %fusion.36), channel_id=1, source_target_pairs={{0,2},{2,4},{4,6},{6,8},{8,10},{10,12},{12,14},{14,16},{16,18},{18... | collective-permute-start | bytes 1179656 | tf_op jit(solution)/shard_map/ppermute | solution.py:14
  153.1 1.9 copy-start.28
  174.5 114.3 %reduce-scatter.8.cloned.1.call-start = ((), (), s32[]{:S(2)}) async-start(), calls=%async_computation.5 | async-start | bytes 1179648 | tf_op jit(solution)/shard_map/reduce_scatter | solution.py:116
  197.8 24.2 %copy-start.23 = (f32[1536]{0:T(1024)S(1)}, f32[1536]{0:T(1024)}, u32[]{:S(2)}) copy-start(f32[1536]{0:T(1024)} %copy-done.21) | copy-start | bytes 18436
  197.8 24.2 %copy-start.26 = (f32[1536]{0:T(1024)S(1)}, f32[1536]{0:T(1024)}, u32[]{:S(2)}) copy-start(f32[1536]{0:T(1024)} %copy-done.24) | copy-start | bytes 18436
  197.9 11.5 %collective-permute-start.5 = (bf16[256,768]{1,0:T(8,128)(2,1)S(1)}, bf16[256,768]{1,0:T(8,128)(2,1)S(1)}, u32[]{:S(2)}, u32[]{:S(2)}) collective-permute-start(bf16[256,768]{1,0:T(8,128)(2,1)S(1)} %add_convert_fusion.1), channel_id=1, source_target_pairs={{2,0},{4,2},{6,4},{8,6},{10,8},{12,10},{14,12},{16,14},{18,16},{20... | collective-permute-start | bytes 1179656 | tf_op jit(solution)/shard_map/ppermute | solution.py:14
  230.9 30.8 %collective-permute-start.7 = (bf16[256,768]{1,0:T(8,128)(2,1)}, bf16[256,768]{1,0:T(8,128)(2,1)}, u32[]{:S(2)}, u32[]{:S(2)}) collective-permute-start(bf16[256,768]{1,0:T(8,128)(2,1)} %slice_bitcast_fusion.2), channel_id=1, source_target_pairs={{0,2},{2,4},{4,6},{6,8},{8,10},{10,12},{12,14},{14,16},{16,18},{18... | collective-permute-start | bytes 1179656 | tf_op jit(solution)/shard_map/ppermute | solution.py:14
  241.6 3.5 %copy-start.5 = (f32[256,1,768]{0,2,1:T(8,128)S(1)}, f32[256,1,768]{0,2,1:T(8,128)}, u32[]{:S(2)}) copy-start(f32[256,1,768]{0,2,1:T(8,128)} %copy.64) | copy-start | bytes 2359300
  241.6 3.5 %copy-start.20 = (f32[256,6]{0,1:T(8,128)S(1)}, f32[256,6]{0,1:T(8,128)}, u32[]{:S(2)}) copy-start(f32[256,6]{0,1:T(8,128)} %copy-done.19) | copy-start | bytes 18436
  241.6 3.5 %copy-start.31 = (f32[768]{0:T(1024)S(1)}, f32[768]{0:T(1024)}, u32[]{:S(2)}) copy-start(f32[768]{0:T(1024)} %param.19) | copy-start | bytes 9220
  243.2 12.2 %collective-permute-start.6 = (bf16[256,768]{1,0:T(8,128)(2,1)S(1)}, bf16[256,768]{1,0:T(8,128)(2,1)}, u32[]{:S(2)}, u32[]{:S(2)}) collective-permute-start(bf16[256,768]{1,0:T(8,128)(2,1)S(1)} %fusion.34), channel_id=1, source_target_pairs={{0,2},{2,4},{4,6},{6,8},{8,10},{10,12},{12,14},{14,16},{16,18},{18... | collective-permute-start | bytes 1179656 | tf_op jit(solution)/shard_map/ppermute | solution.py:14
  290.7 11.4 %collective-permute-start.8 = (bf16[256,768]{1,0:T(8,128)(2,1)S(1)}, bf16[256,768]{1,0:T(8,128)(2,1)S(1)}, u32[]{:S(2)}, u32[]{:S(2)}) collective-permute-start(bf16[256,768]{1,0:T(8,128)(2,1)S(1)} %get-tuple-element.17), channel_id=1, source_target_pairs={{2,0},{4,2},{6,4},{8,6},{10,8},{12,10},{14,12},{16,14},{18,16},{20... | collective-permute-start | bytes 1179656 | tf_op jit(solution)/shard_map/ppermute | solution.py:14
  (14 other events, 19.0 us)
Sparse Core Ops, SparseCore 0:
  80.1 24.4 reduce-scatter.3
  174.6 22.0 reduce-scatter.5
  266.7 22.0 reduce-scatter.7
where the time goes:
time: 314 us; the launch traced here: 310 us
  waiting for transfers between devices  99.2 us (32%)
  local copies, waits for them, and re-layouts  58 us (18%)
  matrix products  42.6 us (14%)
  blocking collectives  40.6 us (13%)
  starting transfers between devices  31.6 us (10%)
  other arithmetic  20.7 us (7%)
  between operations  17.7 us (6%)
    reduce_scatter x3, waiting for transfers between devices, on_device(): lax.psum_scatter(term.astype(jnp.bfloat16), 'heads', scatter_dimension=1,...  66.8 us
    all_gather x3, blocking collectives, on_device(): lax.all_gather(state, 'heads', axis=1, tiled=True)  34.7 us
    ppermute x9, waiting for transfers between devices, shifted(): return lax.ppermute(block, axis, route)  32.3 us
    ppermute x9, starting transfers between devices, shifted(): return lax.ppermute(block, axis, route)  31.5 us
    unnamed x69, local copies, waits for them, and re-layouts  15.4 us
    dot_general x3, matrix products, on_device(): jnp.dot(moved, flat_weights, preferred_element_type=jnp.float32)  15.3 us
    div x6, local copies, waits for them, and re-layouts, head_norm(): return ((shaped / spread).reshape(block.shape) * gain).astype(jnp.bfloat16)  9.78 us
    slice x6, local copies, waits for them, and re-layouts, on_device(): query = head_norm(qkv[:, 0], q_gain)  8.88 us
  transfers between devices with their start and end apart: 12, of which 8 were waited for; matrix products, arithmetic and copies ran while one was open for 19% of the time, Pallas kernels for 0%

commit v1 on v0

v1 whole, which is shorter than its diff:
```python
import functools

import jax
import jax.numpy as jnp
from jax import lax
from jax.experimental import pallas as pl
from jax.experimental.pallas import tpu as pltpu
from jax.sharding import PartitionSpec as P

HD = 128
STEPS = 3
LEVELS = 64
EPS = 1e-06
AXES = ("queue", "heads")
VMEM_LIMIT = 56 * 1024 * 1024


def routed(block, target):
    slots, halves = lax.axis_size("queue"), lax.axis_size("heads")
    pairs = []
    for q in range(slots):
        for h in range(halves):
            q2, h2 = target(q, h)
            if 0 <= q2 < slots:
                pairs.append((q * halves + h, q2 * halves + h2))
    return lax.ppermute(block, AXES, pairs)


def modulated(x, shift, scale):
    values = x.astype(jnp.float32)
    mean = jnp.mean(values * values, axis=-1, keepdims=True)
    return (values * lax.rsqrt(mean + EPS) * (1.0 + scale) + shift).astype(jnp.bfloat16)


def normed(block, gain):
    mean = jnp.mean(block * block, axis=-1, keepdims=True)
    return (block * lax.rsqrt(mean + EPS) * gain).astype(jnp.bfloat16)


def dot(a, b):
    return jnp.dot(a, b, preferred_element_type=jnp.float32)


def dot_t(a, b):
    return lax.dot_general(a, b, (((1,), (1,)), ((), ())), preferred_element_type=jnp.float32)


def near_kernel(x, table, w, k_gain, keys, values):
    width = w.shape[2]
    moved = modulated(x[...], table[3:4, :], table[4:5, :])
    raw = dot(moved, w[1])
    for a in range(0, width, HD):
        keys[:, a : a + HD] = normed(raw[:, a : a + HD], k_gain[:, a : a + HD])
    values[...] = dot(moved, w[2]).astype(jnp.bfloat16)


def own_kernel(start, x, table, w, w_out, q_gain, k_gain, near_keys, near_values, term, attended):
    rows = x.shape[0]
    width = w.shape[2]
    moved = modulated(x[...], table[0:1, :], table[1:2, :])
    visible = lax.broadcasted_iota(jnp.int32, (1, rows), 1) >= start[0]
    factor = 1.4426950408889634 / (HD**0.5)
    query_raw = dot(moved, w[0])
    key_raw = dot(moved, w[1])
    value = dot(moved, w[2]).astype(jnp.bfloat16)
    for a in range(0, width, HD):
        part = slice(a, a + HD)
        query = normed(query_raw[:, part], q_gain[:, part])
        key = normed(key_raw[:, part], k_gain[:, part])
        own = dot_t(query, key)
        near = jnp.where(visible, dot_t(query, near_keys[:, part]), jnp.float32(-1e30))
        top = jnp.maximum(
            jnp.max(own, axis=-1, keepdims=True), jnp.max(near, axis=-1, keepdims=True)
        )
        own = jnp.exp2((own - top) * factor)
        near = jnp.exp2((near - top) * factor)
        total = jnp.sum(own, axis=-1, keepdims=True) + jnp.sum(near, axis=-1, keepdims=True)
        out = dot(own.astype(jnp.bfloat16), value[:, part])
        out = out + dot(near.astype(jnp.bfloat16), near_values[:, part])
        attended[:, part] = (out / total).astype(jnp.bfloat16)
    term[...] = dot(attended[...], w_out[...]).astype(jnp.bfloat16)


def whole_specs(count):
    return [pl.BlockSpec(memory_space=pltpu.VMEM)] * count


def near_call(x, table, w, k_gain):
    rows, width = x.shape[0], w.shape[2]
    out = jax.ShapeDtypeStruct((rows, width), jnp.bfloat16)
    return pl.pallas_call(
        near_kernel,
        out_shape=(out, out),
        in_specs=whole_specs(4),
        out_specs=tuple(whole_specs(2)),
        compiler_params=pltpu.CompilerParams(vmem_limit_bytes=VMEM_LIMIT),
    )(x, table, w, k_gain)


def own_call(start, x, table, w, w_out, q_gain, k_gain, near_keys, near_values):
    rows, width = x.shape[0], w.shape[2]
    return pl.pallas_call(
        own_kernel,
        out_shape=jax.ShapeDtypeStruct((rows, w_out.shape[1]), jnp.bfloat16),
        in_specs=[pl.BlockSpec(memory_space=pltpu.SMEM)] + whole_specs(8),
        out_specs=whole_specs(1)[0],
        scratch_shapes=[pltpu.VMEM((rows, width), jnp.bfloat16)],
        compiler_params=pltpu.CompilerParams(vmem_limit_bytes=VMEM_LIMIT),
    )(start, x, table, w, w_out, q_gain, k_gain, near_keys, near_values)


def on_device(
    frames,
    fresh_groups,
    level_index,
    window_start,
    mod_shift,
    mod_scale,
    mod_gate,
    w_qkv,
    q_gain,
    k_gain,
    w_out,
):
    position = lax.axis_index("queue")
    half = lax.axis_index("heads")
    slot_count = lax.axis_size("queue")
    rows = frames.shape[0]
    features = frames.shape[1]
    level = level_index[position]
    below = level_index[jnp.maximum(position - 1, 0)]
    t_cur = (level.astype(jnp.float32) + 1.0) / LEVELS
    t_next = jnp.where(position > 0, (below.astype(jnp.float32) + 1.0) / LEVELS, jnp.float32(0.0))
    step_size = t_next - t_cur
    start = jnp.where(position > 0, window_start[position], rows).astype(jnp.int32).reshape(1)
    w = jnp.transpose(w_qkv, (1, 0, 2))
    q_gain = q_gain.reshape(1, -1)
    k_gain = k_gain.reshape(1, -1)

    def swap(block):
        return routed(block, lambda q, h: (q, 1 - h))

    def up(block):
        return routed(block, lambda q, h: (q + 1, h))

    def down(block):
        return routed(block, lambda q, h: (q - 1, h))

    def both(mine, other):
        return jnp.where(
            half == 0,
            jnp.concatenate([mine, other], axis=-1),
            jnp.concatenate([other, mine], axis=-1),
        )

    table_rows = [mod_shift[level], mod_scale[level], mod_gate[level], mod_shift[below], mod_scale[below]]
    my_rows = jnp.stack(table_rows + [jnp.zeros_like(table_rows[0])] * 11)
    near_mine = up(frames)
    send = jnp.concatenate([frames, my_rows], axis=0)
    received = swap(send)
    near_other = up(received[:rows])
    state = both(frames, received[:rows])
    table = both(my_rows, received[rows:]).astype(jnp.float32)
    near = both(near_mine, near_other)
    last = slot_count - 1
    fresh_sent = fresh_groups[: STEPS - 1]
    fresh_other = lax.ppermute(fresh_sent, AXES, [(2 * last, 2 * last + 1), (2 * last + 1, 2 * last)])
    fresh = both(fresh_sent, fresh_other)
    gate = table[2:3]
    for step in range(STEPS):
        near_keys, near_values = near_call(near, table, w, k_gain)
        term = own_call(start, state, table, w, w_out, q_gain, k_gain, near_keys, near_values)
        if step < STEPS - 1:
            other = swap(term)
            velocity = gate * (term.astype(jnp.float32) + other.astype(jnp.float32))
            near = (state.astype(jnp.float32) + step_size * velocity).astype(jnp.bfloat16)
            advanced = down(near)
            state = jnp.where(position == last, fresh[step], advanced)
        else:
            low, high = term[:, :features], term[:, features:]
            other = swap(jnp.where(half == 0, high, low))
            mine = jnp.where(half == 0, low, high)
            gate = my_rows[2:3].astype(jnp.float32)
            velocity = gate * (mine.astype(jnp.float32) + other.astype(jnp.float32))
            held = jnp.where(half == 0, state[:, :features], state[:, features:])
            updated = (held.astype(jnp.float32) + step_size * velocity).astype(jnp.bfloat16)
            advanced = down(updated)
            state = jnp.where(position == last, fresh_groups[step], advanced)
    return (state, velocity.astype(jnp.bfloat16))


def solution(mesh):
    placed = (
        P("queue", "heads"),
        P(None, None, "heads"),
        P(),
        P(),
        P(None, "heads"),
        P(None, "heads"),
        P(None, "heads"),
        P(None, None, "heads"),
        P("heads"),
        P("heads"),
        P("heads", None),
    )
    return jax.shard_map(
        on_device,
        mesh=mesh,
        in_specs=placed,
        out_specs=(P("queue", "heads"), P("queue", "heads")),
        check_vma=False,
    )
```

time: 314 us -> 174 us (0.55)
  local copies, waits for them, and re-layouts: 58 us -> 8.9 us
  Pallas kernels: 0 us -> 46 us
  matrix products: 42.6 us -> 0 us
  blocking collectives: 40.6 us -> 0 us
  waiting for transfers between devices: 99.2 us -> 70.3 us
  between operations: 17.7 us -> 6.26 us
  starting transfers between devices: 31.6 us -> 26.1 us
  other arithmetic: 20.7 us -> 15.5 us
    reduce_scatter x3 -> x0, waiting for transfers between devices: 66.8 us -> none  [on_device(): lax.psum_scatter(term.astype(jnp.bfloat16), 'heads', scatter_dimension=1,...]
    pallas_call x0 -> x6, Pallas kernels: none -> 46 us  [the longest x3 29.2 us: own_call(): pl.pallas_call(own_kernel, out_shape=jax.ShapeDtypeStruct((rows, w_out.sh...]
    dot_general x18 -> x0, matrix products: 42.6 us -> none  [the longest x3 15.3 us: on_device(): jnp.dot(moved, flat_weights, preferred_element_type=jnp.float32)]
    all_gather x4 -> x0, blocking collectives: 40.6 us -> none  [the longest x3 34.7 us: on_device(): lax.all_gather(state, 'heads', axis=1, tiled=True)]
    ppermute x9 -> x10, waiting for transfers between devices: 32.3 us -> 70.3 us  [the longest x9 70.3 us: routed(): return lax.ppermute(block, AXES, pairs)]
    unnamed x69 -> x16, local copies, waits for them, and re-layouts: 15.4 us -> 0.03 us
    slice x12 -> x4, local copies, waits for them, and re-layouts: 16.1 us -> 0.9 us  [the longest x1 0.82 us: on_device(): gate = table[2:3]]
    div x6 -> x0, local copies, waits for them, and re-layouts: 9.78 us -> none  [head_norm(): return ((shaped / spread).reshape(block.shape) * gain).astype(jnp.bfloat16)]
  transfers between devices with their start and end apart: 12 -> 10, of which waited for: 8 -> 8; matrix products, arithmetic and copies ran while one was open for 19% -> 6% of each run, Pallas kernels for 0% -> 6%
where the time goes in v1:
time: 174 us; the launch traced here: 173 us
  waiting for transfers between devices  70.3 us (40%)
  Pallas kernels  46 us (26%)
  starting transfers between devices  26.1 us (15%)
  other arithmetic  15.5 us (9%)
  local copies, waits for them, and re-layouts  8.9 us (5%)
  between operations  6.26 us (4%)
    ppermute x9, waiting for transfers between devices, routed(): return lax.ppermute(block, AXES, pairs)  70.3 us
    pallas_call x3, Pallas kernels, own_call(): pl.pallas_call(own_kernel, out_shape=jax.ShapeDtypeStruct((rows, w_out.sh...  29.2 us
    ppermute x9, starting transfers between devices, routed(): return lax.ppermute(block, AXES, pairs)  24.5 us
    pallas_call x3, Pallas kernels, near_call(): pl.pallas_call(near_kernel, out_shape=(out, out), in_specs=whole_specs(4)...  16.8 us
    select_n x3, other arithmetic, both(): jnp.where(half == 0, jnp.concatenate([mine, other], axis=-1), jnp.concate...  3.92 us
  transfers between devices with their start and end apart: 10, of which 8 were waited for; matrix products, arithmetic and copies ran while one was open for 6% of the time, Pallas kernels for 6%

profile of v1, /device:TPU:12, one launch (start us, length us, event | category | flops | bytes accessed | tf_op | source)
XLA Modules:
  0.0 173.1 jit_solution(4246641031070870239)
XLA Ops:
  0.6 1.4 fusion.4
  7.2 1.9 %concatenate.30 = bf16[272,768]{1,0:T(8,128)(2,1)S(1)} concatenate(bf16[256,768]{1,0:T(8,128)(2,1)} %param.11, bf16[1,768]{1,0:T(2,128)(2,1)S(1)} %get-tuple-element.24, bf16[1,768]{1,0:T(2,128)(2,1)S(1)} %get-tuple-element.19, bf16[1,768]{1,0:T(2,128)(2,1)S(1)} %get-tuple-element.15, bf16[1,768]{1,0:T(2,128)(2,1)S(1)} %get-tuple-element.25, ...), dimensions={0} | concatenate | bytes 835584 | tf_op jit(solution)/shard_map/concatenate | solution.py:159
  9.7 1.9 %collective-permute-start.2 = (bf16[256,768]{1,0:T(8,128)(2,1)}, bf16[256,768]{1,0:T(8,128)(2,1)S(1)}, u32[]{:S(2)}, u32[]{:S(2)}) collective-permute-start(bf16[256,768]{1,0:T(8,128)(2,1)} %param.11), channel_id=1, source_target_pairs={{0,2},{1,3},{2,4},{3,5},{4,6},{5,7},{6,8},{7,9},{8,10},{9,11},{10,... | collective-permute-start | bytes 1179656 | tf_op jit(solution)/shard_map/ppermute | solution.py:26
  11.7 1.2 dynamic_slice.31
  12.9 1.3 reshape.15.k_gain
  14.2 1.3 reshape.14.q_gain
  16.1 7.1 %collective-permute-done.1 = bf16[272,768]{1,0:T(8,128)(2,1)S(1)} collective-permute-done((bf16[272,768]{1,0:T(8,128)(2,1)S(1)}, bf16[272,768]{1,0:T(8,128)(2,1)S(1)}, u32[]{:S(2)}, u32[]{:S(2)}) %collective-permute-start.1) | collective-permute-done | bytes 417824 | tf_op jit(solution)/shard_map/ppermute | solution.py:26
  23.3 1.9 %collective-permute-start.3 = (bf16[256,768]{1,0:T(8,128)(2,1)S(1)}, bf16[256,768]{1,0:T(8,128)(2,1)S(1)}, u32[]{:S(2)}, u32[]{:S(2)}) collective-permute-start(bf16[256,768]{1,0:T(8,128)(2,1)S(1)} %slice.47), channel_id=1, source_target_pairs={{0,2},{1,3},{2,4},{3,5},{4,6},{5,7},{6,8},{7,9},{8,10},{9,11},{10,... | collective-permute-start | bytes 1179656 | tf_op jit(solution)/shard_map/ppermute | solution.py:26
  25.8 1.1 maximum_select_fusion.1.x
  27.0 11.7 %collective-permute-done.3 = bf16[256,768]{1,0:T(8,128)(2,1)S(1)} collective-permute-done((bf16[256,768]{1,0:T(8,128)(2,1)S(1)}, bf16[256,768]{1,0:T(8,128)(2,1)S(1)}, u32[]{:S(2)}, u32[]{:S(2)}) %collective-permute-start.3) | collective-permute-done | bytes 393248 | tf_op jit(solution)/shard_map/ppermute | solution.py:26
  39.8 5.6 %shard_map.122 = (bf16[256,768]{1,0:T(8,128)(2,1)}, bf16[256,768]{1,0:T(8,128)(2,1)}) custom-call(bf16[256,1536]{1,0:T(8,128)(2,1)} %maximum_select_fusion.2.x, f32[16,1536]{1,0:T(8,128)} %fusion.3.table, bf16[3,1536,768]{2,1,0:T(8,128)(2,1)} %bitcast.15, f32[1,768]{1,0:T(1,128)} %reshape.15.k_gain), custom_call_target="tpu_custom_call" | custom-call | tf_op jit(solution)/shard_map/pallas_call | solution.py:91
  45.4 9.7 %shard_map.123 = bf16[256,1536]{1,0:T(8,128)(2,1)} custom-call(s32[1]{0:T(128)} %bitcast.6.start, bf16[256,1536]{1,0:T(8,128)(2,1)} %maximum_select_fusion.1.x, f32[16,1536]{1,0:T(8,128)} %fusion.3.table, bf16[3,1536,768]{2,1,0:T(8,128)(2,1)} %bitcast.16, bf16[768,1536]{1,0:T(8,128)(2,1)} %w_out.5, f32[1,768]{1,0:T(1,128)} %reshape.14.q_gain, ...), custom_call_target="tpu_custom_call" | custom-call | tf_op jit(solution)/shard_map/pallas_call | solution.py:102
  56.0 1.6 collective-permute-start
  59.6 12.4 %collective-permute-done.4 = bf16[256,1536]{1,0:T(8,128)(2,1)} collective-permute-done((bf16[256,1536]{1,0:T(8,128)(2,1)}, bf16[256,1536]{1,0:T(8,128)(2,1)}, u32[]{:S(2)}, u32[]{:S(2)}) %collective-permute-start.4) | collective-permute-done | bytes 786464 | tf_op jit(solution)/shard_map/ppermute | solution.py:26
  72.0 1.5 add_convert_fusion.1.x
  73.5 2.1 %collective-permute-start.5 = (bf16[256,1536]{1,0:T(8,128)(2,1)S(1)}, bf16[256,1536]{1,0:T(8,128)(2,1)S(1)}, u32[]{:S(2)}, u32[]{:S(2)}) collective-permute-start(bf16[256,1536]{1,0:T(8,128)(2,1)S(1)} %add_convert_fusion.1.x), channel_id=1, source_target_pairs={{2,0},{3,1},{4,2},{5,3},{6,4},{7,5},{8,6},{9,7},{10,8},{11,9},{12,... | collective-permute-start | bytes 2359304 | tf_op jit(solution)/shard_map/ppermute | solution.py:26
  75.6 1.7 %maximum_select_fusion = bf16[2,256,1536]{2,1,0:T(8,128)(2,1)S(1)} fusion(bf16[2,256,768]{2,1,0:T(8,128)(2,1)} %collective-permute-done, bf16[2,256,768]{2,1,0:T(8,128)(2,1)S(1)} %slice.35, pred[]{:T(512)S(6)} %eq.5), kind=kLoop, calls=%fused_computation | loop fusion | flops 7077888 | bytes 3145729 | tf_op jit(solution)/shard_map/jit(_where)/select_n | solution.py:150
  77.4 5.6 %shard_map.124 = (bf16[256,768]{1,0:T(8,128)(2,1)}, bf16[256,768]{1,0:T(8,128)(2,1)}) custom-call(bf16[256,1536]{1,0:T(8,128)(2,1)} %copy-done.4, f32[16,1536]{1,0:T(8,128)} %fusion.3.table, bf16[3,1536,768]{2,1,0:T(8,128)(2,1)} %bitcast.17, f32[1,768]{1,0:T(1,128)} %reshape.15.k_gain), custom_call_target="tpu_custom_call" | custom-call | tf_op jit(solution)/shard_map/pallas_call | solution.py:91
  83.0 1.9 %collective-permute-done.5 = bf16[256,1536]{1,0:T(8,128)(2,1)S(1)} collective-permute-done((bf16[256,1536]{1,0:T(8,128)(2,1)S(1)}, bf16[256,1536]{1,0:T(8,128)(2,1)S(1)}, u32[]{:S(2)}, u32[]{:S(2)}) %collective-permute-start.5) | collective-permute-done | bytes 786464 | tf_op jit(solution)/shard_map/ppermute | solution.py:26
  85.9 9.7 %shard_map.125 = bf16[256,1536]{1,0:T(8,128)(2,1)} custom-call(s32[1]{0:T(128)} %bitcast.6.start, bf16[256,1536]{1,0:T(8,128)(2,1)} %fusion.x, f32[16,1536]{1,0:T(8,128)} %fusion.3.table, bf16[3,1536,768]{2,1,0:T(8,128)(2,1)} %bitcast.18, bf16[768,1536]{1,0:T(8,128)(2,1)} %w_out.5, f32[1,768]{1,0:T(1,128)} %reshape.14.q_gain, f32[1,768]{1,0:T(1,128)} %reshape.15.k_gain, ...), custom_call_target="tpu_custom_call" | custom-call | tf_op jit(solution)/shard_map/pallas_call | solution.py:102
  96.4 19.8 %collective-permute-done.6 = bf16[256,1536]{1,0:T(8,128)(2,1)S(1)} collective-permute-done((bf16[256,1536]{1,0:T(8,128)(2,1)}, bf16[256,1536]{1,0:T(8,128)(2,1)S(1)}, u32[]{:S(2)}, u32[]{:S(2)}) %collective-permute-start.6) | collective-permute-done | bytes 786464 | tf_op jit(solution)/shard_map/ppermute | solution.py:26
  116.2 1.5 add_convert_fusion.x
  117.7 5.7 %collective-permute-start.7 = (bf16[256,1536]{1,0:T(8,128)(2,1)S(1)}, bf16[256,1536]{1,0:T(8,128)(2,1)S(1)}, u32[]{:S(2)}, u32[]{:S(2)}) collective-permute-start(bf16[256,1536]{1,0:T(8,128)(2,1)S(1)} %add_convert_fusion.x), channel_id=1, source_target_pairs={{2,0},{3,1},{4,2},{5,3},{6,4},{7,5},{8,6},{9,7},{10,8},{11,9},{12,... | collective-permute-start | bytes 2359304 | tf_op jit(solution)/shard_map/ppermute | solution.py:26
  123.4 5.6 %shard_map.126 = (bf16[256,768]{1,0:T(8,128)(2,1)}, bf16[256,768]{1,0:T(8,128)(2,1)}) custom-call(bf16[256,1536]{1,0:T(8,128)(2,1)} %copy-done.5, f32[16,1536]{1,0:T(8,128)} %fusion.3.table, bf16[3,1536,768]{2,1,0:T(8,128)(2,1)} %bitcast.19, f32[1,768]{1,0:T(1,128)} %reshape.15.k_gain), custom_call_target="tpu_custom_call" | custom-call | tf_op jit(solution)/shard_map/pallas_call | solution.py:91
  129.1 3.6 %collective-permute-done.7 = bf16[256,1536]{1,0:T(8,128)(2,1)S(1)} collective-permute-done((bf16[256,1536]{1,0:T(8,128)(2,1)S(1)}, bf16[256,1536]{1,0:T(8,128)(2,1)S(1)}, u32[]{:S(2)}, u32[]{:S(2)}) %collective-permute-start.7) | collective-permute-done | bytes 786464 | tf_op jit(solution)/shard_map/ppermute | solution.py:26
  133.7 9.7 %shard_map.127 = bf16[256,1536]{1,0:T(8,128)(2,1)} custom-call(s32[1]{0:T(128)} %bitcast.6.start, bf16[256,1536]{1,0:T(8,128)(2,1)} %fusion.1.x, f32[16,1536]{1,0:T(8,128)} %fusion.3.table, bf16[3,1536,768]{2,1,0:T(8,128)(2,1)} %bitcast.20, bf16[768,1536]{1,0:T(8,128)(2,1)} %w_out.5, f32[1,768]{1,0:T(1,128)} %reshape.14.q_gain, f32[1,768]{1,0:T(1,128)} %reshape.15.k_gain, ...), custom_call_target="tpu_custom_call" | custom-call | tf_op jit(solution)/shard_map/pallas_call | solution.py:102
  143.4 1.2 broadcast_select_fusion
  145.5 8.5 %collective-permute-done.8 = bf16[256,768]{1,0:T(8,128)(2,1)S(1)} collective-permute-done((bf16[256,768]{1,0:T(8,128)(2,1)S(1)}, bf16[256,768]{1,0:T(8,128)(2,1)S(1)}, u32[]{:S(2)}, u32[]{:S(2)}) %collective-permute-start.8) | collective-permute-done | bytes 393248 | tf_op jit(solution)/shard_map/ppermute | solution.py:26
  154.0 2.2 %fusion.2 = (bf16[256,768]{1,0:T(8,128)(2,1)}, bf16[256,768]{1,0:T(8,128)(2,1)S(1)}) fusion(bf16[256,768]{1,0:T(8,128)(2,1)S(1)} %collective-permute-done.8, f32[768]{0:T(1024)S(1)} %get-tuple-element.14, bf16[256,1536]{1,0:T(8,128)(2,1)} %shard_map.127, pred[]{:T(512)S(6)} %eq.5, f32[]{:T(128)S(6)} %sub.7, bf16[256,1536]{1,0:T(8,128)(2,1)S(1)} %copy-done.1), kind=kLoop, calls=%fused_computation.11 | loop fusion | flops 2162688 | bytes 2755589 | tf_op jit(solution)/shard_map/convert_element_type | solution.py:189
  156.2 9.8 %collective-permute-start.9 = (bf16[256,768]{1,0:T(8,128)(2,1)S(1)}, bf16[256,768]{1,0:T(8,128)(2,1)S(1)}, u32[]{:S(2)}, u32[]{:S(2)}) collective-permute-start(bf16[256,768]{1,0:T(8,128)(2,1)S(1)} %get-tuple-element.17), channel_id=1, source_target_pairs={{2,0},{3,1},{4,2},{5,3},{6,4},{7,5},{8,6},{9,7},{10,8},{11,9},{12,... | collective-permute-start | bytes 1179656 | tf_op jit(solution)/shard_map/ppermute | solution.py:26
  166.0 5.3 %collective-permute-done.9 = bf16[256,768]{1,0:T(8,128)(2,1)S(1)} collective-permute-done((bf16[256,768]{1,0:T(8,128)(2,1)S(1)}, bf16[256,768]{1,0:T(8,128)(2,1)S(1)}, u32[]{:S(2)}, u32[]{:S(2)}) %collective-permute-start.9) | collective-permute-done | bytes 393248 | tf_op jit(solution)/shard_map/ppermute | solution.py:26
  171.3 1.8 %bitcast_select_fusion = bf16[256,768]{1,0:T(8,128)(2,1)} fusion(bf16[256,768]{1,0:T(8,128)(2,1)S(1)} %collective-permute-done.9, bf16[3,256,768]{2,1,0:T(8,128)(2,1)} %param.12, pred[]{:T(512)S(6)} %eq.4), kind=kLoop, calls=%fused_computation.13 | loop fusion | flops 196608 | bytes 1179649 | tf_op jit(solution)/shard_map/jit(_where)/select_n | solution.py:188
  (36 shorter events, 9.3 us)
Async XLA Ops:
  0.6 25.2 %copy-start.6 = (bf16[256,768]{1,0:T(8,128)(2,1)S(1)}, bf16[256,768]{1,0:T(8,128)(2,1)}, u32[]{:S(2)}) copy-start(bf16[256,768]{1,0:T(8,128)(2,1)} %param.11) | copy-start | bytes 1179652
  9.1 14.1 %collective-permute-start.1 = (bf16[272,768]{1,0:T(8,128)(2,1)S(1)}, bf16[272,768]{1,0:T(8,128)(2,1)S(1)}, u32[]{:S(2)}, u32[]{:S(2)}) collective-permute-start(bf16[272,768]{1,0:T(8,128)(2,1)S(1)} %concatenate.30), channel_id=1, source_target_pairs={{0,1},{1,0},{2,3},{3,2},{4,5},{5,4},{6,7},{7,6},{8,9},{9,8},{10,11... | collective-permute-start | bytes 1253384 | tf_op jit(solution)/shard_map/ppermute | solution.py:26
  9.7 17.2 %collective-permute-start.2 = (bf16[256,768]{1,0:T(8,128)(2,1)}, bf16[256,768]{1,0:T(8,128)(2,1)S(1)}, u32[]{:S(2)}, u32[]{:S(2)}) collective-permute-start(bf16[256,768]{1,0:T(8,128)(2,1)} %param.11), channel_id=1, source_target_pairs={{0,2},{1,3},{2,4},{3,5},{4,6},{5,7},{6,8},{7,9},{8,10},{9,11},{10,... | collective-permute-start | bytes 1179656 | tf_op jit(solution)/shard_map/ppermute | solution.py:26
  23.3 15.4 %collective-permute-start.3 = (bf16[256,768]{1,0:T(8,128)(2,1)S(1)}, bf16[256,768]{1,0:T(8,128)(2,1)S(1)}, u32[]{:S(2)}, u32[]{:S(2)}) collective-permute-start(bf16[256,768]{1,0:T(8,128)(2,1)S(1)} %slice.47), channel_id=1, source_target_pairs={{0,2},{1,3},{2,4},{3,5},{4,6},{5,7},{6,8},{7,9},{8,10},{9,11},{10,... | collective-permute-start | bytes 1179656 | tf_op jit(solution)/shard_map/ppermute | solution.py:26
  45.4 10.6 %copy-start.7 = (bf16[3,256,768]{2,1,0:T(8,128)(2,1)S(1)}, bf16[3,256,768]{2,1,0:T(8,128)(2,1)}, u32[]{:S(2)}) copy-start(bf16[3,256,768]{2,1,0:T(8,128)(2,1)} %param.12) | copy-start | bytes 3538948
  55.1 16.9 %copy-start = (bf16[256,1536]{1,0:T(8,128)(2,1)S(1)}, bf16[256,1536]{1,0:T(8,128)(2,1)}, u32[]{:S(2)}) copy-start(bf16[256,1536]{1,0:T(8,128)(2,1)} %maximum_select_fusion.1.x) | copy-start | bytes 2359300
  55.1 16.9 %copy-start.3 = (bf16[256,1536]{1,0:T(8,128)(2,1)S(1)}, bf16[256,1536]{1,0:T(8,128)(2,1)}, u32[]{:S(2)}) copy-start(bf16[256,1536]{1,0:T(8,128)(2,1)} %shard_map.123) | copy-start | bytes 2359300
  55.1 16.9 %collective-permute-start.4 = (bf16[256,1536]{1,0:T(8,128)(2,1)}, bf16[256,1536]{1,0:T(8,128)(2,1)}, u32[]{:S(2)}, u32[]{:S(2)}) collective-permute-start(bf16[256,1536]{1,0:T(8,128)(2,1)} %shard_map.123), channel_id=1, source_target_pairs={{0,1},{1,0},{2,3},{3,2},{4,5},{5,4},{6,7},{7,6},{8,9},{9,8},{10,11... | collective-permute-start | bytes 2359304 | tf_op jit(solution)/shard_map/ppermute | solution.py:26
  56.0 19.6 %collective-permute-start = (bf16[2,256,768]{2,1,0:T(8,128)(2,1)S(1)}, bf16[2,256,768]{2,1,0:T(8,128)(2,1)}, u32[]{:S(2)}, u32[]{:S(2)}) collective-permute-start(bf16[2,256,768]{2,1,0:T(8,128)(2,1)S(1)} %slice.35), channel_id=1, source_target_pairs={{254,255},{255,254}} | collective-permute-start | bytes 2359304 | tf_op jit(solution)/shard_map/ppermute | solution.py:167
  73.5 3.9 %copy-start.4 = (bf16[256,1536]{1,0:T(8,128)(2,1)}, bf16[256,1536]{1,0:T(8,128)(2,1)S(1)}, u32[]{:S(2)}) copy-start(bf16[256,1536]{1,0:T(8,128)(2,1)S(1)} %add_convert_fusion.1.x) | copy-start | bytes 2359300
  73.5 11.4 %collective-permute-start.5 = (bf16[256,1536]{1,0:T(8,128)(2,1)S(1)}, bf16[256,1536]{1,0:T(8,128)(2,1)S(1)}, u32[]{:S(2)}, u32[]{:S(2)}) collective-permute-start(bf16[256,1536]{1,0:T(8,128)(2,1)S(1)} %add_convert_fusion.1.x), channel_id=1, source_target_pairs={{2,0},{3,1},{4,2},{5,3},{6,4},{7,5},{8,6},{9,7},{10,8},{11,9},{12,... | collective-permute-start | bytes 2359304 | tf_op jit(solution)/shard_map/ppermute | solution.py:26
  85.9 30.3 %copy-start.2 = (bf16[256,1536]{1,0:T(8,128)(2,1)S(1)}, bf16[256,1536]{1,0:T(8,128)(2,1)}, u32[]{:S(2)}) copy-start(bf16[256,1536]{1,0:T(8,128)(2,1)} %fusion.x) | copy-start | bytes 2359300
  95.6 20.6 %collective-permute-start.6 = (bf16[256,1536]{1,0:T(8,128)(2,1)}, bf16[256,1536]{1,0:T(8,128)(2,1)S(1)}, u32[]{:S(2)}, u32[]{:S(2)}) collective-permute-start(bf16[256,1536]{1,0:T(8,128)(2,1)} %shard_map.125), channel_id=1, source_target_pairs={{0,1},{1,0},{2,3},{3,2},{4,5},{5,4},{6,7},{7,6},{8,9},{9,8},{10,11... | collective-permute-start | bytes 2359304 | tf_op jit(solution)/shard_map/ppermute | solution.py:26
  117.7 5.7 %copy-start.5 = (bf16[256,1536]{1,0:T(8,128)(2,1)}, bf16[256,1536]{1,0:T(8,128)(2,1)S(1)}, u32[]{:S(2)}) copy-start(bf16[256,1536]{1,0:T(8,128)(2,1)S(1)} %add_convert_fusion.x) | copy-start | bytes 2359300
  117.7 15.0 %collective-permute-start.7 = (bf16[256,1536]{1,0:T(8,128)(2,1)S(1)}, bf16[256,1536]{1,0:T(8,128)(2,1)S(1)}, u32[]{:S(2)}, u32[]{:S(2)}) collective-permute-start(bf16[256,1536]{1,0:T(8,128)(2,1)S(1)} %add_convert_fusion.x), channel_id=1, source_target_pairs={{2,0},{3,1},{4,2},{5,3},{6,4},{7,5},{8,6},{9,7},{10,8},{11,9},{12,... | collective-permute-start | bytes 2359304 | tf_op jit(solution)/shard_map/ppermute | solution.py:26
  143.4 10.6 %copy-start.1 = (bf16[256,1536]{1,0:T(8,128)(2,1)S(1)}, bf16[256,1536]{1,0:T(8,128)(2,1)}, u32[]{:S(2)}) copy-start(bf16[256,1536]{1,0:T(8,128)(2,1)} %fusion.1.x) | copy-start | bytes 2359300
  144.6 9.4 %collective-permute-start.8 = (bf16[256,768]{1,0:T(8,128)(2,1)S(1)}, bf16[256,768]{1,0:T(8,128)(2,1)S(1)}, u32[]{:S(2)}, u32[]{:S(2)}) collective-permute-start(bf16[256,768]{1,0:T(8,128)(2,1)S(1)} %broadcast_select_fusion), channel_id=1, source_target_pairs={{0,1},{1,0},{2,3},{3,2},{4,5},{5,4},{6,7},{7,6},{8,9},{9,8},{10,11... | collective-permute-start | bytes 1179656 | tf_op jit(solution)/shard_map/ppermute | solution.py:26
  156.2 15.1 %collective-permute-start.9 = (bf16[256,768]{1,0:T(8,128)(2,1)S(1)}, bf16[256,768]{1,0:T(8,128)(2,1)S(1)}, u32[]{:S(2)}, u32[]{:S(2)}) collective-permute-start(bf16[256,768]{1,0:T(8,128)(2,1)S(1)} %get-tuple-element.17), channel_id=1, source_target_pairs={{2,0},{3,1},{4,2},{5,3},{6,4},{7,5},{8,6},{9,7},{10,8},{11,9},{12,... | collective-permute-start | bytes 1179656 | tf_op jit(solution)/shard_map/ppermute | solution.py:26

commit v2 on v1

v2 whole, which is shorter than its diff:
```python
import functools

import jax
import jax.numpy as jnp
from jax import lax
from jax.experimental import pallas as pl
from jax.experimental.pallas import tpu as pltpu
from jax.sharding import PartitionSpec as P

HD = 128
STEPS = 3
LEVELS = 64
EPS = 1e-06
AXES = ("queue", "heads")
VMEM_LIMIT = 24 * 1024 * 1024
CHUNKS = 2
SHIFT, SCALE, GATE, NEAR_SHIFT, NEAR_SCALE = range(5)
TABLE_ROWS = 16


def routed(block, target):
    slots, halves = lax.axis_size("queue"), lax.axis_size("heads")
    pairs = []
    for q in range(slots):
        for h in range(halves):
            to = target(q, h)
            if to is not None and 0 <= to[0] < slots:
                pairs.append((q * halves + h, to[0] * halves + to[1]))
    return lax.ppermute(block, AXES, pairs)


def dot(a, b):
    return jnp.dot(a, b, preferred_element_type=jnp.float32)


def dot_t(a, b):
    return lax.dot_general(a, b, (((1,), (1,)), ((), ())), preferred_element_type=jnp.float32)


def modulated(low, high, shift, scale):
    low, high = low.astype(jnp.float32), high.astype(jnp.float32)
    total = jnp.sum(low * low, axis=-1, keepdims=True) + jnp.sum(high * high, axis=-1, keepdims=True)
    factor = lax.rsqrt(total / (2 * low.shape[-1]) + EPS)
    parts = [low, high]
    for n in range(2):
        parts[n] = (parts[n] * factor * (1.0 + scale[n]) + shift[n]).astype(jnp.bfloat16)
    return jnp.concatenate(parts, axis=-1)


def normed(block, gain):
    mean = jnp.mean(block * block, axis=-1, keepdims=True)
    return (block * lax.rsqrt(mean + EPS) * gain).astype(jnp.bfloat16)


def ordered(mine, other):
    first = lax.axis_index("heads") == 0
    return jnp.where(first, mine, other), jnp.where(first, other, mine)


def table_row(rows, n):
    mine, other = (r[n : n + 1, :].astype(jnp.float32) for r in rows)
    return ordered(mine, other)


def halves_of(kind, refs, step, row, count):
    if kind == "pair":
        return ordered(refs[0][row : row + count, :], refs[1][row : row + count, :])
    fresh, fresh_other, *chunks = refs
    size = chunks[0].shape[0]
    wide = [c[...] for c in chunks[row // size : (row + count) // size]]
    wide = wide[0] if len(wide) == 1 else jnp.concatenate(wide, axis=0)
    width = wide.shape[1] // 2
    low, high = wide[:, :width], wide[:, width:]
    if kind == "chunks":
        return low, high
    passed = ordered(fresh[step, row : row + count, :], fresh_other[step, row : row + count, :])
    last = lax.axis_index("queue") == lax.axis_size("queue") - 1
    return jnp.where(last, passed[0], low), jnp.where(last, passed[1], high)


def rows_kernel(levels, shift_hbm, scale_hbm, gate_hbm, rows, shift, scale, gate, arrived):
    tables = ((shift_hbm, shift), (scale_hbm, scale), (gate_hbm, gate))
    copies = [pltpu.make_async_copy(a, b, arrived.at[n]) for n, (a, b) in enumerate(tables)]
    for copy in copies:
        copy.start()
    position = lax.axis_index("queue")
    level = levels[position]
    below = levels[jnp.maximum(position - 1, 0)]
    shape = (TABLE_ROWS, shift.shape[0])
    row = lax.broadcasted_iota(jnp.int32, shape, 0)
    column = lax.broadcasted_iota(jnp.int32, shape, 1)

    def picked(table, own, near):
        chosen = jnp.logical_and(row == own, column == level)
        if near is not None:
            chosen = jnp.logical_or(chosen, jnp.logical_and(row == near, column == below))
        return dot(jnp.where(chosen, 1.0, 0.0).astype(jnp.bfloat16), table[...])

    for copy in copies:
        copy.wait()
    out = picked(shift, SHIFT, NEAR_SHIFT) + picked(scale, SCALE, NEAR_SCALE)
    rows[...] = (out + picked(gate, GATE, None)).astype(jnp.bfloat16)


def rows_call(levels, tables):
    held = [pltpu.VMEM(table.shape, table.dtype) for table in tables]
    return pl.pallas_call(
        rows_kernel,
        out_shape=jax.ShapeDtypeStruct((TABLE_ROWS, tables[0].shape[1]), jnp.bfloat16),
        in_specs=[pl.BlockSpec(memory_space=pltpu.SMEM)] + [pl.BlockSpec(memory_space=pltpu.HBM)] * len(tables),
        out_specs=pl.BlockSpec(memory_space=pltpu.VMEM),
        scratch_shapes=held + [pltpu.SemaphoreType.DMA((len(tables),))],
        compiler_params=pltpu.CompilerParams(vmem_limit_bytes=VMEM_LIMIT),
    )(levels, *(pltpu.with_memory_space_constraint(table, pltpu.HBM) for table in tables))


def stage_kernel(w_hbm, w_out_hbm, q_gain, k_gain, w, w_out, gains, arrived):
    copies = [pltpu.make_async_copy(w_hbm, w, arrived.at[0]), pltpu.make_async_copy(w_out_hbm, w_out, arrived.at[1])]
    for copy in copies:
        copy.start()
    gains[0:1, :] = q_gain[...].reshape(1, -1)
    gains[1:2, :] = k_gain[...].reshape(1, -1)
    for copy in copies:
        copy.wait()


def stage_call(w, w_out, q_gain, k_gain):
    vmem = pl.BlockSpec(memory_space=pltpu.VMEM)
    held = [pltpu.with_memory_space_constraint(a, pltpu.HBM) for a in (w, w_out)]
    return pl.pallas_call(
        stage_kernel,
        out_shape=(
            pltpu.VMEM(w.shape, w.dtype),
            pltpu.VMEM(w_out.shape, w_out.dtype),
            pltpu.VMEM((2, q_gain.shape[0]), q_gain.dtype),
        ),
        in_specs=[pl.BlockSpec(memory_space=pl.ANY)] * 2 + [vmem] * 2,
        out_specs=(vmem, vmem, vmem),
        scratch_shapes=[pltpu.SemaphoreType.DMA((2,))],
        compiler_params=pltpu.CompilerParams(vmem_limit_bytes=VMEM_LIMIT),
    )(*held, q_gain, k_gain)


def near_kernel(kind, rows_mine, rows_other, w, gains, *refs):
    x, (keys, values) = refs[:-2], refs[-2:]
    width = w.shape[2]
    table = (rows_mine, rows_other)
    low, high = halves_of(kind, x, None, 0, keys.shape[0])
    moved = modulated(low, high, table_row(table, NEAR_SHIFT), table_row(table, NEAR_SCALE))
    raw = dot(moved, w[1])
    gain = gains[1:2, :]
    for a in range(0, width, HD):
        keys[:, a : a + HD] = normed(raw[:, a : a + HD], gain[:, a : a + HD])
    values[...] = dot(moved, w[2]).astype(jnp.bfloat16)


def attend(starts, query, key, value, near_key, near_value):
    position = lax.axis_index("queue")
    start = jnp.where(position > 0, starts[position], near_key.shape[0])
    visible = lax.broadcasted_iota(jnp.int32, (1, near_key.shape[0]), 1) >= start
    factor = 1.4426950408889634 / (HD**0.5)
    own = dot_t(query, key)
    near = jnp.where(visible, dot_t(query, near_key), jnp.float32(-1e30))
    top = jnp.maximum(jnp.max(own, axis=-1, keepdims=True), jnp.max(near, axis=-1, keepdims=True))
    own = jnp.exp2((own - top) * factor)
    near = jnp.exp2((near - top) * factor)
    total = jnp.sum(own, axis=-1, keepdims=True) + jnp.sum(near, axis=-1, keepdims=True)
    out = dot(own.astype(jnp.bfloat16), value) + dot(near.astype(jnp.bfloat16), near_value)
    return (out / total).astype(jnp.bfloat16)


def own_kernel(kind, step, count, starts, rows_mine, rows_other, w, gains, near_keys, near_values, *refs):
    x, (attended, queries, keys, values) = refs[:-4], refs[-4:]
    rows = keys.shape[0]
    width = w.shape[2]
    first = attended.shape[0]
    table = (rows_mine, rows_other)
    low, high = halves_of(kind, x, step, 0, rows)
    moved = modulated(low, high, table_row(table, SHIFT), table_row(table, SCALE))
    query_raw = dot(moved, w[0])
    key_raw = dot(moved, w[1])
    value = dot(moved, w[2]).astype(jnp.bfloat16)
    values[...] = value
    q_row, k_row = gains[0:1, :], gains[1:2, :]
    for a in range(0, width, HD):
        part = slice(a, a + HD)
        query = normed(query_raw[:, part], q_row[:, part])
        key = normed(key_raw[:, part], k_row[:, part])
        queries[:, part] = query[first:]
        keys[:, part] = key
        attended[:, part] = attend(
            starts, query[:first], key, value[:, part], near_keys[:, part], near_values[:, part]
        )


def qkv_kernel(kind, rows_mine, rows_other, w, gains, *refs):
    x, (*queries, keys, values) = refs[:2], refs[2:]
    rows = keys.shape[0]
    width = w.shape[2]
    table = (rows_mine, rows_other)
    low, high = halves_of(kind, x, None, 0, rows)
    moved = modulated(low, high, table_row(table, SHIFT), table_row(table, SCALE))
    query_raw = dot(moved, w[0])
    key_raw = dot(moved, w[1])
    values[...] = dot(moved, w[2]).astype(jnp.bfloat16)
    q_row, k_row = gains[0:1, :], gains[1:2, :]
    for a in range(0, width, HD):
        part = slice(a, a + HD)
        query = normed(query_raw[:, part], q_row[:, part])
        keys[:, part] = normed(key_raw[:, part], k_row[:, part])
        for n, chunk in enumerate(queries):
            chunk[:, part] = query[n * chunk.shape[0] : (n + 1) * chunk.shape[0]]


def rest_kernel(starts, queries, keys, values, near_keys, near_values, attended):
    for a in range(0, attended.shape[1], HD):
        part = slice(a, a + HD)
        attended[:, part] = attend(
            starts, queries[:, part], keys[:, part], values[:, part], near_keys[:, part], near_values[:, part]
        )


def step_size_of(levels):
    position = lax.axis_index("queue")
    level = levels[position]
    below = levels[jnp.maximum(position - 1, 0)]
    t_cur = (level.astype(jnp.float32) + 1.0) / LEVELS
    t_next = jnp.where(position > 0, (below.astype(jnp.float32) + 1.0) / LEVELS, jnp.float32(0.0))
    return t_next - t_cur


def project_kernel(kind, step, row, levels, rows_mine, rows_other, w_mine, w_other, a_mine, a_other, *refs):
    x, new = refs[:-1], refs[-1]
    count = new.shape[0]
    width = new.shape[1] // 2
    gate = table_row((rows_mine, rows_other), GATE)
    halves = halves_of(kind, x, step - 1, row, count)
    product = dot(a_mine[...], w_mine[...]) + dot(a_other[...], w_other[...])
    for n in range(2):
        part = slice(n * width, (n + 1) * width)
        velocity = gate[n] * product[:, part]
        value = (halves[n].astype(jnp.float32) + step_size_of(levels) * velocity).astype(jnp.bfloat16)
        new[:, part] = value


def final_kernel(kind, step, row, levels, rows_mine, w_mine, w_other, a_mine, a_other, *refs):
    x, (new, velocity_out) = refs[:-2], refs[-2:]
    count, width = new.shape
    half = lax.axis_index("heads")
    part = pl.ds(pl.multiple_of(half * width, HD), width)
    low, high = halves_of(kind, x, step - 1, row, count)
    held = jnp.where(half == 0, low, high).astype(jnp.float32)
    product = dot(a_mine[...], w_mine[:, part]) + dot(a_other[...], w_other[:, part])
    velocity = rows_mine[GATE : GATE + 1, :].astype(jnp.float32) * product
    velocity_out[...] = velocity.astype(jnp.bfloat16)
    new[...] = (held + step_size_of(levels) * velocity).astype(jnp.bfloat16)


def piece_of(position):
    core = position % 2
    z = (position // 4) % 8
    y = position // 32
    return (y + 2 * z) % 4, core


def gather_kernel(own, back, ahead, across, others, w_other):
    group, core = piece_of(lax.axis_index("queue"))
    size = own.shape[0]
    for n, (block, turn) in enumerate(((own, 0), (back, 3), (ahead, 1), (across, 2))):
        place = (group + turn) % 4 * 2
        w_other[pl.ds(pl.multiple_of((place + core) * size, 16), size), :] = block[...]
        w_other[pl.ds(pl.multiple_of((place + 1 - core) * size, 16), size), :] = others[n]


def kernel_call(kernel, out, scalars, arrays, products=0, exponentials=0, dtype=jnp.bfloat16):
    many = isinstance(out[0], tuple)
    outs = out if many else (out,)
    shapes = tuple(jax.ShapeDtypeStruct(s, dtype) for s in outs)
    size = sum(a.size * a.dtype.itemsize for a in arrays)
    result = pl.pallas_call(
        kernel,
        cost_estimate=pl.CostEstimate(
            flops=2 * products, bytes_accessed=size, transcendentals=exponentials
        ),
        out_shape=shapes,
        in_specs=[pl.BlockSpec(memory_space=pltpu.SMEM)] * len(scalars)
        + [pl.BlockSpec(memory_space=pltpu.VMEM)] * len(arrays),
        out_specs=tuple([pl.BlockSpec(memory_space=pltpu.VMEM)] * len(outs)),
        compiler_params=pltpu.CompilerParams(vmem_limit_bytes=VMEM_LIMIT),
    )(*scalars, *arrays)
    return result if many else result[0]


def after(block, *others):
    return lax.optimization_barrier((block, *others))[0]


def fetched_piece(w_out):
    size = w_out.shape[0] // 8
    group, core = piece_of(lax.axis_index("queue"))
    return lax.dynamic_slice_in_dim(w_out, (group * 2 + core) * size, size, 0)


def other_projection(own, ready, shape):
    def turned(y, z):
        return lambda q, h: ((q // 32 + y) % 4 * 32 + (q // 4 + z) % 8 * 4 + q % 4, h)

    back = routed(own, turned(1, 0))
    ahead = routed(own, turned(-1, 0))
    across = routed(own, turned(0, 1))
    own, back, ahead, across, _ = lax.optimization_barrier((own, back, ahead, across, ready))
    others = routed(jnp.stack([own, back, ahead, across]), lambda q, h: (q ^ 1, h))
    return kernel_call(gather_kernel, shape, (), (own, back, ahead, across, others))


def on_device(
    frames,
    fresh_groups,
    level_index,
    window_start,
    mod_shift,
    mod_scale,
    mod_gate,
    w_qkv,
    q_gain,
    k_gain,
    w_out,
):
    position = lax.axis_index("queue")
    last = lax.axis_size("queue") - 1
    rows, width = frames.shape
    count = rows // CHUNKS
    w = jnp.transpose(w_qkv, (1, 0, 2))
    group_products = rows * w.shape[1] * width
    attention_products = 4 * count * rows * width
    out_products = 2 * count * width * width

    def swap(block):
        return routed(block, lambda q, h: (q, 1 - h))

    def up(block):
        return routed(block, lambda q, h: (q + 1, h))

    def down(block):
        return routed(block, lambda q, h: (q - 1, h))

    w_out_hbm = w_out
    other = swap(frames)
    rows_mine = rows_call(level_index, (mod_shift, mod_scale, mod_gate))
    rows_other = swap(rows_mine)
    w, w_out, gains = stage_call(w, w_out, q_gain, k_gain)
    near_mine = up(frames)
    near_other = up(after(other, rows_other, gains))
    piece = routed(fetched_piece(w_out_hbm), lambda q, h: (q ^ 2, 1 - h))
    table = (rows_mine, rows_other)
    kind, state = "pair", (frames, other)
    near_kind, near = "pair", (near_mine, near_other)
    *queries, keys, values = kernel_call(
        functools.partial(qkv_kernel, kind),
        ((count, width),) * CHUNKS + ((rows, width), (rows, width)),
        (),
        (*table, w, gains, *state),
        3 * group_products,
    )
    fresh_other = routed(
        after(fresh_groups[: STEPS - 1], other),
        lambda q, h: (last, 1 - h) if q == last - 2 else None,
    )
    near = (near_mine, after(near_other, keys, fresh_other))
    for step in range(STEPS):
        near_keys, near_values = kernel_call(
            functools.partial(near_kernel, near_kind),
            ((rows, width), (rows, width)),
            (),
            (*table, w, gains, *near),
            2 * group_products,
        )
        if step == 0:
            parts = []
        else:
            first, *queries, keys, values = kernel_call(
                functools.partial(own_kernel, kind, step - 1, count),
                ((count, width), (rows - count, width), (rows, width), (rows, width)),
                (window_start,),
                (*table, w, gains, near_keys, near_values, *state),
                3 * group_products + attention_products,
                attention_products // HD,
            )
            parts = [first]
        for query in queries:
            part = kernel_call(
                rest_kernel,
                (count, width),
                (window_start,),
                (after(query, *parts), keys, values, near_keys, near_values),
                attention_products,
                attention_products // HD,
            )
            parts.append(part)
        received = [swap(part) for part in parts]
        if step == 0:
            w_other = other_projection(after(piece, other, rows_other, near_mine), near_keys, w_out.shape)
        if step < STEPS - 1:
            new = []
            for n in range(CHUNKS):
                block = kernel_call(
                    functools.partial(project_kernel, kind, step, n * count),
                    (count, 2 * width),
                    (level_index,),
                    (*table, w_out, w_other, parts[n], after(received[n], *new), *state),
                    2 * out_products,
                )
                new.append(block)
            state = (fresh_groups, fresh_other, *[down(block) for block in new])
            near_kind, near = "chunks", (fresh_groups, fresh_other, *(after(block, state[2]) for block in new))
            kind = "fresh"
        else:
            done = []
            for n in range(CHUNKS):
                pair = kernel_call(
                    functools.partial(final_kernel, kind, step, n * count),
                    ((count, width), (count, width)),
                    (level_index,),
                    (rows_mine, w_out, w_other, parts[n], after(received[n], *(p[0] for p in done)), *state),
                    out_products,
                )
                done.append(pair)
            advanced = jnp.concatenate([down(block) for block, _ in done], axis=0)
            velocity = jnp.concatenate([block for _, block in done], axis=0)
            final = jnp.where(position == last, fresh_groups[step], advanced)
    return (final, velocity)


def solution(mesh):
    placed = (
        P("queue", "heads"),
        P(None, None, "heads"),
        P(),
        P(),
        P(None, "heads"),
        P(None, "heads"),
        P(None, "heads"),
        P(None, None, "heads"),
        P("heads"),
        P("heads"),
        P("heads", None),
    )
    return jax.shard_map(
        on_device,
        mesh=mesh,
        in_specs=placed,
        out_specs=(P("queue", "heads"), P("queue", "heads")),
        check_vma=False,
    )
```

time: 174 us -> 133 us (0.76)
  waiting for transfers between devices: 70.3 us -> 41.7 us
  starting transfers between devices: 26.1 us -> 47.5 us
  other arithmetic: 15.5 us -> 1.78 us
  Pallas kernels: 46 us -> 37.9 us
  local copies, waits for them, and re-layouts: 8.9 us -> 2.6 us
  between operations: 6.26 us -> 1.05 us
    ppermute x9 -> x22, waiting for transfers between devices: 70.3 us -> 41.7 us  [routed(): return lax.ppermute(block, AXES, pairs)]
    ppermute x9 -> x22, starting transfers between devices: 24.5 us -> 47.5 us  [routed(): return lax.ppermute(block, AXES, pairs)]
    pallas_call x6 -> x19, Pallas kernels: 46 us -> 37.9 us  [the longest x17 32.5 us: kernel_call(): pl.pallas_call(kernel, cost_estimate=pl.CostEstimate(flops=2 * products,...]
    select_n x7 -> x1, other arithmetic: 8.89 us -> 0.86 us  [on_device(): final = jnp.where(position == last, fresh_groups[step], advanced)]
    convert_element_type x4 -> x0, other arithmetic: 5.85 us -> none  [the longest x2 3.04 us: on_device(): (state.astype(jnp.float32) + step_size * velocity).astype(jnp.bfloat16)]
    reshape x2 -> x0, local copies, waits for them, and re-layouts: 2.56 us -> none  [the longest x1 1.28 us: on_device(): k_gain = k_gain.reshape(1, -1)]
    dynamic_slice x3 -> x1, local copies, waits for them, and re-layouts: 3.44 us -> 0.99 us  [fetched_piece(): return lax.dynamic_slice_in_dim(w_out, (group * 2 + core) * size, size, 0)]
    concatenate x1 -> x0, local copies, waits for them, and re-layouts: 1.91 us -> none  [on_device(): send = jnp.concatenate([frames, my_rows], axis=0)]
  transfers between devices with their start and end apart: 10 -> 22, of which waited for: 8 -> 13; matrix products, arithmetic and copies ran while one was open for 6% -> 2% of each run, Pallas kernels for 6% -> 21%
where the time goes in v2:
time: 133 us
  starting transfers between devices  47.5 us (36%)
  waiting for transfers between devices  41.7 us (31%)
  Pallas kernels  37.9 us (28%)
  local copies, waits for them, and re-layouts  2.6 us (2%)
  other arithmetic  1.78 us (1%)
    ppermute x22, starting transfers between devices, routed(): return lax.ppermute(block, AXES, pairs)  47.5 us
    ppermute x22, waiting for transfers between devices, routed(): return lax.ppermute(block, AXES, pairs)  41.7 us
    pallas_call x17, Pallas kernels, kernel_call(): pl.pallas_call(kernel, cost_estimate=pl.CostEstimate(flops=2 * products,...  32.5 us
    pallas_call x1, Pallas kernels, stage_call(): pl.pallas_call(stage_kernel, out_shape=(pltpu.VMEM(w.shape, w.dtype), plt...  3.7 us
  transfers between devices with their start and end apart: 22, of which 13 were waited for; matrix products, arithmetic and copies ran while one was open for 2% of the time, Pallas kernels for 21%

profile of v2, /device:TPU:12, one launch (start us, length us, event | category | flops | bytes accessed | tf_op | source)
XLA Modules:
  0.0 132.6 jit_solution(233871280409837844)
XLA Ops:
  2.5 10.9 %collective-permute-done.1.refs_1_ = bf16[256,768]{1,0:T(8,128)(2,1)S(1)} collective-permute-done((bf16[256,768]{1,0:T(8,128)(2,1)}, bf16[256,768]{1,0:T(8,128)(2,1)S(1)}, u32[]{:S(2)}, u32[]{:S(2)}) %collective-permute-start.1) | collective-permute-done | bytes 393248 | tf_op jit(solution)/shard_map/ppermute | solution.py:29
  14.0 1.9 %collective-permute-start.3 = (bf16[256,768]{1,0:T(8,128)(2,1)S(1)}, bf16[256,768]{1,0:T(8,128)(2,1)S(1)}, u32[]{:S(2)}, u32[]{:S(2)}) collective-permute-start(bf16[256,768]{1,0:T(8,128)(2,1)S(1)} %copy-done.1), channel_id=1, source_target_pairs={{0,2},{1,3},{2,4},{3,5},{4,6},{5,7},{6,8},{7,9},{8,10},{9,11},{10,... | collective-permute-start | bytes 1179656 | tf_op jit(solution)/shard_map/ppermute | solution.py:29
  17.7 1.7 %shard_map.122.rows_mine = bf16[16,768]{1,0:T(8,128)(2,1)S(1)} custom-call(s32[128]{0:T(128)S(1)} %copy-done.2, bf16[64,768]{1,0:T(8,128)(2,1)} %shift_hbm.1, bf16[64,768]{1,0:T(8,128)(2,1)} %scale_hbm.1, bf16[64,768]{1,0:T(8,128)(2,1)} %gate_hbm.1), custom_call_target="tpu_custom_call" | custom-call | tf_op jit(solution)/shard_map/pallas_call | solution.py:107
  19.4 2.8 %collective-permute-start.2 = (bf16[16,768]{1,0:T(8,128)(2,1)S(1)}, bf16[16,768]{1,0:T(8,128)(2,1)S(1)}, u32[]{:S(2)}, u32[]{:S(2)}) collective-permute-start(bf16[16,768]{1,0:T(8,128)(2,1)S(1)} %shard_map.122.rows_mine), channel_id=1, source_target_pairs={{0,1},{1,0},{2,3},{3,2},{4,5},{5,4},{6,7},{7,6},{8,9},{9,8},{10,11... | collective-permute-start | bytes 73736 | tf_op jit(solution)/shard_map/ppermute | solution.py:29
  22.2 3.7 %shard_map.123 = (bf16[3,1536,768]{2,1,0:T(8,128)(2,1)S(1)}, bf16[768,1536]{1,0:T(8,128)(2,1)S(1)}, f32[2,768]{1,0:T(2,128)S(1)}) custom-call(bf16[3,1536,768]{2,1,0:T(8,128)(2,1)} %bitcast.11, bf16[768,1536]{1,0:T(8,128)(2,1)} %w_out_hbm.1, f32[768]{0:T(1024)S(1)} %copy-done.4, f32[768]{0:T(1024)S(1)} %copy-done.5), custom_call_target="tpu_custom_call" | custom-call | tf_op jit(solution)/shard_map/pallas_call | solution.py:130
  25.9 3.6 %collective-permute-start.7 = (bf16[256,768]{1,0:T(8,128)(2,1)S(1)}, bf16[256,768]{1,0:T(8,128)(2,1)S(1)}, u32[]{:S(2)}, u32[]{:S(2)}) collective-permute-start(bf16[256,768]{1,0:T(8,128)(2,1)S(1)} %collective-permute-done.1.refs_1_), channel_id=1, source_target_pairs={{0,2},{1,3},{2,4},{3,5},{4,6},{5,7},{6,8},{7,9},{8,10},{9,11},{10,... | collective-permute-start | bytes 1179656 | tf_op jit(solution)/shard_map/ppermute | solution.py:29
  29.6 2.0 %collective-permute-start.6 = (bf16[96,1536]{1,0:T(8,128)(2,1)S(1)}, bf16[96,1536]{1,0:T(8,128)(2,1)S(1)}, u32[]{:S(2)}, u32[]{:S(2)}) collective-permute-start(bf16[96,1536]{1,0:T(8,128)(2,1)S(1)} %collective-permute-done.own), channel_id=1, source_target_pairs={{0,8},{1,9},{2,10},{3,11},{4,12},{5,13},{6,14},{7,15},{8,16},{9,17... | collective-permute-start | bytes 884744 | tf_op jit(solution)/shard_map/ppermute | solution.py:29
  33.6 2.3 %shard_map.124 = (bf16[128,768]{1,0:T(8,128)(2,1)S(1)}, bf16[128,768]{1,0:T(8,128)(2,1)S(1)}, bf16[256,768]{1,0:T(8,128)(2,1)S(1)}, bf16[256,768]{1,0:T(8,128)(2,1)S(1)}) custom-call(bf16[16,768]{1,0:T(8,128)(2,1)S(1)} %shard_map.122.rows_mine, bf16[16,768]{1,0:T(8,128)(2,1)S(1)} %collective-permute-done.2.rows_other, ...), custom_call_target="tpu_custom_call" | custom-call | flops 1811939328 | bytes 7919616 | tf_op jit(solution)/shard_map/pallas_call | solution.py:280
  35.9 6.9 %collective-permute-done.7.refs_1_ = bf16[256,768]{1,0:T(8,128)(2,1)S(1)} collective-permute-done((bf16[256,768]{1,0:T(8,128)(2,1)S(1)}, bf16[256,768]{1,0:T(8,128)(2,1)S(1)}, u32[]{:S(2)}, u32[]{:S(2)}) %collective-permute-start.7) | collective-permute-done | bytes 393248 | tf_op jit(solution)/shard_map/ppermute | solution.py:29
  46.5 2.3 %shard_map.127.a_mine = bf16[128,768]{1,0:T(8,128)(2,1)S(1)} custom-call(s32[128]{0:T(128)S(1)} %copy-done.3, bf16[128,768]{1,0:T(8,128)(2,1)S(1)} %get-tuple-element.58.queries, bf16[256,768]{1,0:T(8,128)(2,1)S(1)} %get-tuple-element.50.keys, bf16[256,768]{1,0:T(8,128)(2,1)S(1)} %get-tuple-element.59.values, ...), custom_call_target="tpu_custom_call" | custom-call | flops 201326592 | bytes 1769472 | tf_op jit(solution)/shard_map/pallas_call | solution.py:280
  49.6 2.3 %shard_map.129.a_mine = bf16[128,768]{1,0:T(8,128)(2,1)S(1)} custom-call(s32[128]{0:T(128)S(1)} %copy-done.3, bf16[128,768]{1,0:T(8,128)(2,1)S(1)} %get-tuple-element.63.queries, bf16[256,768]{1,0:T(8,128)(2,1)S(1)} %get-tuple-element.50.keys, bf16[256,768]{1,0:T(8,128)(2,1)S(1)} %get-tuple-element.59.values, ...), custom_call_target="tpu_custom_call" | custom-call | flops 201326592 | bytes 1769472 | tf_op jit(solution)/shard_map/pallas_call | solution.py:280
  51.9 3.0 %collective-permute-start.12 = (bf16[128,768]{1,0:T(8,128)(2,1)S(1)}, bf16[128,768]{1,0:T(8,128)(2,1)S(1)}, u32[]{:S(2)}, u32[]{:S(2)}) collective-permute-start(bf16[128,768]{1,0:T(8,128)(2,1)S(1)} %shard_map.129.a_mine), channel_id=1, source_target_pairs={{0,1},{1,0},{2,3},{3,2},{4,5},{5,4},{6,7},{7,6},{8,9},{9,8},{10,11... | collective-permute-start | bytes 589832 | tf_op jit(solution)/shard_map/ppermute | solution.py:29
  55.0 3.2 %collective-permute-done.10.a_other = bf16[128,768]{1,0:T(8,128)(2,1)S(1)} collective-permute-done((bf16[128,768]{1,0:T(8,128)(2,1)S(1)}, bf16[128,768]{1,0:T(8,128)(2,1)S(1)}, u32[]{:S(2)}, u32[]{:S(2)}) %collective-permute-start.10) | collective-permute-done | bytes 196640 | tf_op jit(solution)/shard_map/ppermute | solution.py:29
  59.7 4.3 %collective-permute-start.11 = (bf16[128,1536]{1,0:T(8,128)(2,1)S(1)}, bf16[128,1536]{1,0:T(8,128)(2,1)S(1)}, u32[]{:S(2)}, u32[]{:S(2)}) collective-permute-start(bf16[128,1536]{1,0:T(8,128)(2,1)S(1)} %shard_map.128.refs_2_), channel_id=1, source_target_pairs={{2,0},{3,1},{4,2},{5,3},{6,4},{7,5},{8,6},{9,7},{10,8},{11,9},{12,... | collective-permute-start | bytes 1179656 | tf_op jit(solution)/shard_map/ppermute | solution.py:29
  65.4 2.8 %collective-permute-start.13 = (bf16[128,1536]{1,0:T(8,128)(2,1)S(1)}, bf16[128,1536]{1,0:T(8,128)(2,1)S(1)}, u32[]{:S(2)}, u32[]{:S(2)}) collective-permute-start(bf16[128,1536]{1,0:T(8,128)(2,1)S(1)} %shard_map.130.refs_3_), channel_id=1, source_target_pairs={{2,0},{3,1},{4,2},{5,3},{6,4},{7,5},{8,6},{9,7},{10,8},{11,9},{12,... | collective-permute-start | bytes 1179656 | tf_op jit(solution)/shard_map/ppermute | solution.py:29
  70.9 2.6 %collective-permute-done.13.refs_3_ = bf16[128,1536]{1,0:T(8,128)(2,1)S(1)} collective-permute-done((bf16[128,1536]{1,0:T(8,128)(2,1)S(1)}, bf16[128,1536]{1,0:T(8,128)(2,1)S(1)}, u32[]{:S(2)}, u32[]{:S(2)}) %collective-permute-start.13) | collective-permute-done | bytes 393248 | tf_op jit(solution)/shard_map/ppermute | solution.py:29
  73.5 4.4 %shard_map.132 = (bf16[128,768]{1,0:T(8,128)(2,1)S(1)}, bf16[128,768]{1,0:T(8,128)(2,1)S(1)}, bf16[256,768]{1,0:T(8,128)(2,1)S(1)}, bf16[256,768]{1,0:T(8,128)(2,1)S(1)}) custom-call(s32[128]{0:T(128)S(1)} %copy-done.3, bf16[16,768]{1,0:T(8,128)(2,1)S(1)} %shard_map.122.rows_mine, bf16[16,768]{1,0:T(8,128)(2,1)S(1)} %collective-permute-done.2.rows_other, ...), custom_call_target="tpu_custom_call" | custom-call | flops 2013265920 | bytes 10672128 | tf_op jit(solution)/shard_map/pallas_call | solution.py:280
  79.5 2.3 %shard_map.134.a_mine = bf16[128,768]{1,0:T(8,128)(2,1)S(1)} custom-call(s32[128]{0:T(128)S(1)} %copy-done.3, bf16[128,768]{1,0:T(8,128)(2,1)S(1)} %get-tuple-element.71.queries, bf16[256,768]{1,0:T(8,128)(2,1)S(1)} %get-tuple-element.72.keys, bf16[256,768]{1,0:T(8,128)(2,1)S(1)} %get-tuple-element.73.values, ...), custom_call_target="tpu_custom_call" | custom-call | flops 201326592 | bytes 1769472 | tf_op jit(solution)/shard_map/pallas_call | solution.py:280
  81.8 2.2 %collective-permute-start.16 = (bf16[128,768]{1,0:T(8,128)(2,1)S(1)}, bf16[128,768]{1,0:T(8,128)(2,1)S(1)}, u32[]{:S(2)}, u32[]{:S(2)}) collective-permute-start(bf16[128,768]{1,0:T(8,128)(2,1)S(1)} %shard_map.134.a_mine), channel_id=1, source_target_pairs={{0,1},{1,0},{2,3},{3,2},{4,5},{5,4},{6,7},{7,6},{8,9},{9,8},{10,11... | collective-permute-start | bytes 589832 | tf_op jit(solution)/shard_map/ppermute | solution.py:29
  83.9 3.4 %collective-permute-done.14.a_other = bf16[128,768]{1,0:T(8,128)(2,1)S(1)} collective-permute-done((bf16[128,768]{1,0:T(8,128)(2,1)S(1)}, bf16[128,768]{1,0:T(8,128)(2,1)S(1)}, u32[]{:S(2)}, u32[]{:S(2)}) %collective-permute-start.14) | collective-permute-done | bytes 196640 | tf_op jit(solution)/shard_map/ppermute | solution.py:29
  88.7 4.6 %collective-permute-start.15 = (bf16[128,1536]{1,0:T(8,128)(2,1)S(1)}, bf16[128,1536]{1,0:T(8,128)(2,1)S(1)}, u32[]{:S(2)}, u32[]{:S(2)}) collective-permute-start(bf16[128,1536]{1,0:T(8,128)(2,1)S(1)} %shard_map.133.refs_2_), channel_id=1, source_target_pairs={{2,0},{3,1},{4,2},{5,3},{6,4},{7,5},{8,6},{9,7},{10,8},{11,9},{12,... | collective-permute-start | bytes 1179656 | tf_op jit(solution)/shard_map/ppermute | solution.py:29
  94.7 2.1 %collective-permute-start.17 = (bf16[128,1536]{1,0:T(8,128)(2,1)S(1)}, bf16[128,1536]{1,0:T(8,128)(2,1)S(1)}, u32[]{:S(2)}, u32[]{:S(2)}) collective-permute-start(bf16[128,1536]{1,0:T(8,128)(2,1)S(1)} %shard_map.135.refs_3_), channel_id=1, source_target_pairs={{2,0},{3,1},{4,2},{5,3},{6,4},{7,5},{8,6},{9,7},{10,8},{11,9},{12,... | collective-permute-start | bytes 1179656 | tf_op jit(solution)/shard_map/ppermute | solution.py:29
  96.8 1.8 %collective-permute-done.15.refs_2_ = bf16[128,1536]{1,0:T(8,128)(2,1)S(1)} collective-permute-done((bf16[128,1536]{1,0:T(8,128)(2,1)S(1)}, bf16[128,1536]{1,0:T(8,128)(2,1)S(1)}, u32[]{:S(2)}, u32[]{:S(2)}) %collective-permute-start.15) | collective-permute-done | bytes 393248 | tf_op jit(solution)/shard_map/ppermute | solution.py:29
  100.2 2.7 %collective-permute-done.17.refs_3_ = bf16[128,1536]{1,0:T(8,128)(2,1)S(1)} collective-permute-done((bf16[128,1536]{1,0:T(8,128)(2,1)S(1)}, bf16[128,1536]{1,0:T(8,128)(2,1)S(1)}, u32[]{:S(2)}, u32[]{:S(2)}) %collective-permute-start.17) | collective-permute-done | bytes 393248 | tf_op jit(solution)/shard_map/ppermute | solution.py:29
  102.8 4.4 %shard_map.137 = (bf16[128,768]{1,0:T(8,128)(2,1)S(1)}, bf16[128,768]{1,0:T(8,128)(2,1)S(1)}, bf16[256,768]{1,0:T(8,128)(2,1)S(1)}, bf16[256,768]{1,0:T(8,128)(2,1)S(1)}) custom-call(s32[128]{0:T(128)S(1)} %copy-done.3, bf16[16,768]{1,0:T(8,128)(2,1)S(1)} %shard_map.122.rows_mine, bf16[16,768]{1,0:T(8,128)(2,1)S(1)} %collective-permute-done.2.rows_other, ...), custom_call_target="tpu_custom_call" | custom-call | flops 2013265920 | bytes 10672128 | tf_op jit(solution)/shard_map/pallas_call | solution.py:280
  107.2 2.6 %collective-permute-start.18 = (bf16[128,768]{1,0:T(8,128)(2,1)S(1)}, bf16[128,768]{1,0:T(8,128)(2,1)S(1)}, u32[]{:S(2)}, u32[]{:S(2)}) collective-permute-start(bf16[128,768]{1,0:T(8,128)(2,1)S(1)} %get-tuple-element.78.a_mine), channel_id=1, source_target_pairs={{0,1},{1,0},{2,3},{3,2},{4,5},{5,4},{6,7},{7,6},{8,9},{9,8},{10,11... | collective-permute-start | bytes 589832 | tf_op jit(solution)/shard_map/ppermute | solution.py:29
  109.8 2.3 %shard_map.139.a_mine = bf16[128,768]{1,0:T(8,128)(2,1)S(1)} custom-call(s32[128]{0:T(128)S(1)} %copy-done.3, bf16[128,768]{1,0:T(8,128)(2,1)S(1)} %get-tuple-element.81.queries, bf16[256,768]{1,0:T(8,128)(2,1)S(1)} %get-tuple-element.82.keys, bf16[256,768]{1,0:T(8,128)(2,1)S(1)} %get-tuple-element.83.values, ...), custom_call_target="tpu_custom_call" | custom-call | flops 201326592 | bytes 1769472 | tf_op jit(solution)/shard_map/pallas_call | solution.py:280
  113.2 3.2 %collective-permute-done.18.a_other = bf16[128,768]{1,0:T(8,128)(2,1)S(1)} collective-permute-done((bf16[128,768]{1,0:T(8,128)(2,1)S(1)}, bf16[128,768]{1,0:T(8,128)(2,1)S(1)}, u32[]{:S(2)}, u32[]{:S(2)}) %collective-permute-start.18) | collective-permute-done | bytes 196640 | tf_op jit(solution)/shard_map/ppermute | solution.py:29
  117.4 1.9 %collective-permute-done.20.a_other = bf16[128,768]{1,0:T(8,128)(2,1)S(1)} collective-permute-done((bf16[128,768]{1,0:T(8,128)(2,1)S(1)}, bf16[128,768]{1,0:T(8,128)(2,1)S(1)}, u32[]{:S(2)}, u32[]{:S(2)}) %collective-permute-start.20) | collective-permute-done | bytes 196640 | tf_op jit(solution)/shard_map/ppermute | solution.py:29
  120.4 6.0 %collective-permute-start.21 = (bf16[128,768]{1,0:T(8,128)(2,1)S(1)}, bf16[128,768]{1,0:T(8,128)(2,1)S(1)}, u32[]{:S(2)}, u32[]{:S(2)}) collective-permute-start(bf16[128,768]{1,0:T(8,128)(2,1)S(1)} %get-tuple-element.85), channel_id=1, source_target_pairs={{2,0},{3,1},{4,2},{5,3},{6,4},{7,5},{8,6},{9,7},{10,8},{11,9},{12,... | collective-permute-start | bytes 589832 | tf_op jit(solution)/shard_map/ppermute | solution.py:29
  126.4 1.9 %collective-permute-start.19 = (bf16[128,768]{1,0:T(8,128)(2,1)S(1)}, bf16[128,768]{1,0:T(8,128)(2,1)S(1)}, u32[]{:S(2)}, u32[]{:S(2)}) collective-permute-start(bf16[128,768]{1,0:T(8,128)(2,1)S(1)} %get-tuple-element.79), channel_id=1, source_target_pairs={{2,0},{3,1},{4,2},{5,3},{6,4},{7,5},{8,6},{9,7},{10,8},{11,9},{12,... | collective-permute-start | bytes 589832 | tf_op jit(solution)/shard_map/ppermute | solution.py:29
  129.6 2.1 %collective-permute-done.19 = bf16[128,768]{1,0:T(8,128)(2,1)S(1)} collective-permute-done((bf16[128,768]{1,0:T(8,128)(2,1)S(1)}, bf16[128,768]{1,0:T(8,128)(2,1)S(1)}, u32[]{:S(2)}, u32[]{:S(2)}) %collective-permute-start.19) | collective-permute-done | bytes 196640 | tf_op jit(solution)/shard_map/ppermute | solution.py:29
  (48 shorter events, 27.3 us)
Async XLA Ops:
  0.6 13.4 %copy-start.1 = (bf16[256,768]{1,0:T(8,128)(2,1)S(1)}, bf16[256,768]{1,0:T(8,128)(2,1)}, u32[]{:S(2)}) copy-start(bf16[256,768]{1,0:T(8,128)(2,1)} %refs_0_.13) | copy-start | bytes 1179652
  0.6 17.0 %copy-start.2 = (s32[128]{0:T(128)S(1)}, s32[128]{0:T(128)}, u32[]{:S(2)}) copy-start(s32[128]{0:T(128)} %levels.13) | copy-start | bytes 1540
  0.7 21.5 %copy-start.5 = (f32[768]{0:T(1024)S(1)}, f32[768]{0:T(1024)}, u32[]{:S(2)}) copy-start(f32[768]{0:T(1024)} %k_gain.1) | copy-start | bytes 9220
  0.7 21.5 %copy-start.4 = (f32[768]{0:T(1024)S(1)}, f32[768]{0:T(1024)}, u32[]{:S(2)}) copy-start(f32[768]{0:T(1024)} %q_gain.1) | copy-start | bytes 9220
  0.7 12.7 %collective-permute-start.1 = (bf16[256,768]{1,0:T(8,128)(2,1)}, bf16[256,768]{1,0:T(8,128)(2,1)S(1)}, u32[]{:S(2)}, u32[]{:S(2)}) collective-permute-start(bf16[256,768]{1,0:T(8,128)(2,1)} %refs_0_.13), channel_id=1, source_target_pairs={{0,1},{1,0},{2,3},{3,2},{4,5},{5,4},{6,7},{7,6},{8,9},{9,8},{10,11... | collective-permute-start | bytes 1179656 | tf_op jit(solution)/shard_map/ppermute | solution.py:29
  13.3 29.5 %collective-permute-start.8 = (bf16[2,256,768]{2,1,0:T(8,128)(2,1)S(1)}, bf16[2,256,768]{2,1,0:T(8,128)(2,1)S(1)}, u32[]{:S(2)}, u32[]{:S(2)}) collective-permute-start(bf16[2,256,768]{2,1,0:T(8,128)(2,1)S(1)} %slice.7), channel_id=1, source_target_pairs={{250,255},{251,254}} | collective-permute-start | bytes 2359304 | tf_op jit(solution)/shard_map/ppermute | solution.py:29
  14.0 15.5 %collective-permute-start.3 = (bf16[256,768]{1,0:T(8,128)(2,1)S(1)}, bf16[256,768]{1,0:T(8,128)(2,1)S(1)}, u32[]{:S(2)}, u32[]{:S(2)}) collective-permute-start(bf16[256,768]{1,0:T(8,128)(2,1)S(1)} %copy-done.1), channel_id=1, source_target_pairs={{0,2},{1,3},{2,4},{3,5},{4,6},{5,7},{6,8},{7,9},{8,10},{9,11},{10,... | collective-permute-start | bytes 1179656 | tf_op jit(solution)/shard_map/ppermute | solution.py:29
  17.0 12.5 %collective-permute-start = (bf16[96,1536]{1,0:T(8,128)(2,1)S(1)}, bf16[96,1536]{1,0:T(8,128)(2,1)S(1)}, u32[]{:S(2)}, u32[]{:S(2)}) collective-permute-start(bf16[96,1536]{1,0:T(8,128)(2,1)S(1)} %constant_dynamic-slice_fusion), channel_id=1, source_target_pairs={{0,5},{1,4},{2,7},{3,6},{4,1},{5,0},{6,3},{7,2},{8,13},{9,12},{10,... | collective-permute-start | bytes 884744 | tf_op jit(solution)/shard_map/ppermute | solution.py:29
  19.4 6.5 %collective-permute-start.2 = (bf16[16,768]{1,0:T(8,128)(2,1)S(1)}, bf16[16,768]{1,0:T(8,128)(2,1)S(1)}, u32[]{:S(2)}, u32[]{:S(2)}) collective-permute-start(bf16[16,768]{1,0:T(8,128)(2,1)S(1)} %shard_map.122.rows_mine), channel_id=1, source_target_pairs={{0,1},{1,0},{2,3},{3,2},{4,5},{5,4},{6,7},{7,6},{8,9},{9,8},{10,11... | collective-permute-start | bytes 73736 | tf_op jit(solution)/shard_map/ppermute | solution.py:29
  25.9 16.9 %collective-permute-start.7 = (bf16[256,768]{1,0:T(8,128)(2,1)S(1)}, bf16[256,768]{1,0:T(8,128)(2,1)S(1)}, u32[]{:S(2)}, u32[]{:S(2)}) collective-permute-start(bf16[256,768]{1,0:T(8,128)(2,1)S(1)} %collective-permute-done.1.refs_1_), channel_id=1, source_target_pairs={{0,2},{1,3},{2,4},{3,5},{4,6},{5,7},{6,8},{7,9},{8,10},{9,11},{10,... | collective-permute-start | bytes 1179656 | tf_op jit(solution)/shard_map/ppermute | solution.py:29
  29.6 14.9 %collective-permute-start.6 = (bf16[96,1536]{1,0:T(8,128)(2,1)S(1)}, bf16[96,1536]{1,0:T(8,128)(2,1)S(1)}, u32[]{:S(2)}, u32[]{:S(2)}) collective-permute-start(bf16[96,1536]{1,0:T(8,128)(2,1)S(1)} %collective-permute-done.own), channel_id=1, source_target_pairs={{0,8},{1,9},{2,10},{3,11},{4,12},{5,13},{6,14},{7,15},{8,16},{9,17... | collective-permute-start | bytes 884744 | tf_op jit(solution)/shard_map/ppermute | solution.py:29
  31.6 12.9 %collective-permute-start.5 = (bf16[96,1536]{1,0:T(8,128)(2,1)S(1)}, bf16[96,1536]{1,0:T(8,128)(2,1)S(1)}, u32[]{:S(2)}, u32[]{:S(2)}) collective-permute-start(bf16[96,1536]{1,0:T(8,128)(2,1)S(1)} %collective-permute-done.own), channel_id=1, source_target_pairs={{0,192},{1,193},{2,194},{3,195},{4,196},{5,197},{6,198},{7,199},{8... | collective-permute-start | bytes 884744 | tf_op jit(solution)/shard_map/ppermute | solution.py:29
  32.0 13.8 %collective-permute-start.4 = (bf16[96,1536]{1,0:T(8,128)(2,1)S(1)}, bf16[96,1536]{1,0:T(8,128)(2,1)S(1)}, u32[]{:S(2)}, u32[]{:S(2)}) collective-permute-start(bf16[96,1536]{1,0:T(8,128)(2,1)S(1)} %collective-permute-done.own), channel_id=1, source_target_pairs={{0,64},{1,65},{2,66},{3,67},{4,68},{5,69},{6,70},{7,71},{8,72},{9,... | collective-permute-start | bytes 884744 | tf_op jit(solution)/shard_map/ppermute | solution.py:29
  45.9 0.7 copy-start.3
  46.0 12.1 %collective-permute-start.9 = (bf16[4,96,1536]{2,1,0:T(8,128)(2,1)S(1)}, bf16[4,96,1536]{2,1,0:T(8,128)(2,1)S(1)}, u32[]{:S(2)}, u32[]{:S(2)}) collective-permute-start(bf16[4,96,1536]{2,1,0:T(8,128)(2,1)S(1)} %pad_maximum_fusion), channel_id=1, source_target_pairs={{0,2},{1,3},{2,0},{3,1},{4,6},{5,7},{6,4},{7,5},{8,10},{9,11},{10,... | collective-permute-start | bytes 3538952 | tf_op jit(solution)/shard_map/ppermute | solution.py:29
  48.8 9.3 %collective-permute-start.10 = (bf16[128,768]{1,0:T(8,128)(2,1)S(1)}, bf16[128,768]{1,0:T(8,128)(2,1)S(1)}, u32[]{:S(2)}, u32[]{:S(2)}) collective-permute-start(bf16[128,768]{1,0:T(8,128)(2,1)S(1)} %shard_map.127.a_mine), channel_id=1, source_target_pairs={{0,1},{1,0},{2,3},{3,2},{4,5},{5,4},{6,7},{7,6},{8,9},{9,8},{10,11... | collective-permute-start | bytes 589832 | tf_op jit(solution)/shard_map/ppermute | solution.py:29
  51.9 12.1 %collective-permute-start.12 = (bf16[128,768]{1,0:T(8,128)(2,1)S(1)}, bf16[128,768]{1,0:T(8,128)(2,1)S(1)}, u32[]{:S(2)}, u32[]{:S(2)}) collective-permute-start(bf16[128,768]{1,0:T(8,128)(2,1)S(1)} %shard_map.129.a_mine), channel_id=1, source_target_pairs={{0,1},{1,0},{2,3},{3,2},{4,5},{5,4},{6,7},{7,6},{8,9},{9,8},{10,11... | collective-permute-start | bytes 589832 | tf_op jit(solution)/shard_map/ppermute | solution.py:29
  59.7 9.6 %copy-start = (bf16[3,256,768]{2,1,0:T(8,128)(2,1)S(1)}, bf16[3,256,768]{2,1,0:T(8,128)(2,1)}, u32[]{:S(2)}) copy-start(bf16[3,256,768]{2,1,0:T(8,128)(2,1)} %refs_0_.21) | copy-start | bytes 3538948
  59.7 9.6 %collective-permute-start.11 = (bf16[128,1536]{1,0:T(8,128)(2,1)S(1)}, bf16[128,1536]{1,0:T(8,128)(2,1)S(1)}, u32[]{:S(2)}, u32[]{:S(2)}) collective-permute-start(bf16[128,1536]{1,0:T(8,128)(2,1)S(1)} %shard_map.128.refs_2_), channel_id=1, source_target_pairs={{2,0},{3,1},{4,2},{5,3},{6,4},{7,5},{8,6},{9,7},{10,8},{11,9},{12,... | collective-permute-start | bytes 1179656 | tf_op jit(solution)/shard_map/ppermute | solution.py:29
  65.4 8.1 %collective-permute-start.13 = (bf16[128,1536]{1,0:T(8,128)(2,1)S(1)}, bf16[128,1536]{1,0:T(8,128)(2,1)S(1)}, u32[]{:S(2)}, u32[]{:S(2)}) collective-permute-start(bf16[128,1536]{1,0:T(8,128)(2,1)S(1)} %shard_map.130.refs_3_), channel_id=1, source_target_pairs={{2,0},{3,1},{4,2},{5,3},{6,4},{7,5},{8,6},{9,7},{10,8},{11,9},{12,... | collective-permute-start | bytes 1179656 | tf_op jit(solution)/shard_map/ppermute | solution.py:29
  78.0 9.4 %collective-permute-start.14 = (bf16[128,768]{1,0:T(8,128)(2,1)S(1)}, bf16[128,768]{1,0:T(8,128)(2,1)S(1)}, u32[]{:S(2)}, u32[]{:S(2)}) collective-permute-start(bf16[128,768]{1,0:T(8,128)(2,1)S(1)} %get-tuple-element.68.a_mine), channel_id=1, source_target_pairs={{0,1},{1,0},{2,3},{3,2},{4,5},{5,4},{6,7},{7,6},{8,9},{9,8},{10,11... | collective-permute-start | bytes 589832 | tf_op jit(solution)/shard_map/ppermute | solution.py:29
  81.8 11.6 %collective-permute-start.16 = (bf16[128,768]{1,0:T(8,128)(2,1)S(1)}, bf16[128,768]{1,0:T(8,128)(2,1)S(1)}, u32[]{:S(2)}, u32[]{:S(2)}) collective-permute-start(bf16[128,768]{1,0:T(8,128)(2,1)S(1)} %shard_map.134.a_mine), channel_id=1, source_target_pairs={{0,1},{1,0},{2,3},{3,2},{4,5},{5,4},{6,7},{7,6},{8,9},{9,8},{10,11... | collective-permute-start | bytes 589832 | tf_op jit(solution)/shard_map/ppermute | solution.py:29
  88.7 9.9 %collective-permute-start.15 = (bf16[128,1536]{1,0:T(8,128)(2,1)S(1)}, bf16[128,1536]{1,0:T(8,128)(2,1)S(1)}, u32[]{:S(2)}, u32[]{:S(2)}) collective-permute-start(bf16[128,1536]{1,0:T(8,128)(2,1)S(1)} %shard_map.133.refs_2_), channel_id=1, source_target_pairs={{2,0},{3,1},{4,2},{5,3},{6,4},{7,5},{8,6},{9,7},{10,8},{11,9},{12,... | collective-permute-start | bytes 1179656 | tf_op jit(solution)/shard_map/ppermute | solution.py:29
  94.7 8.1 %collective-permute-start.17 = (bf16[128,1536]{1,0:T(8,128)(2,1)S(1)}, bf16[128,1536]{1,0:T(8,128)(2,1)S(1)}, u32[]{:S(2)}, u32[]{:S(2)}) collective-permute-start(bf16[128,1536]{1,0:T(8,128)(2,1)S(1)} %shard_map.135.refs_3_), channel_id=1, source_target_pairs={{2,0},{3,1},{4,2},{5,3},{6,4},{7,5},{8,6},{9,7},{10,8},{11,9},{12,... | collective-permute-start | bytes 1179656 | tf_op jit(solution)/shard_map/ppermute | solution.py:29
  107.2 9.2 %collective-permute-start.18 = (bf16[128,768]{1,0:T(8,128)(2,1)S(1)}, bf16[128,768]{1,0:T(8,128)(2,1)S(1)}, u32[]{:S(2)}, u32[]{:S(2)}) collective-permute-start(bf16[128,768]{1,0:T(8,128)(2,1)S(1)} %get-tuple-element.78.a_mine), channel_id=1, source_target_pairs={{0,1},{1,0},{2,3},{3,2},{4,5},{5,4},{6,7},{7,6},{8,9},{9,8},{10,11... | collective-permute-start | bytes 589832 | tf_op jit(solution)/shard_map/ppermute | solution.py:29
  112.1 7.3 %collective-permute-start.20 = (bf16[128,768]{1,0:T(8,128)(2,1)S(1)}, bf16[128,768]{1,0:T(8,128)(2,1)S(1)}, u32[]{:S(2)}, u32[]{:S(2)}) collective-permute-start(bf16[128,768]{1,0:T(8,128)(2,1)S(1)} %shard_map.139.a_mine), channel_id=1, source_target_pairs={{0,1},{1,0},{2,3},{3,2},{4,5},{5,4},{6,7},{7,6},{8,9},{9,8},{10,11... | collective-permute-start | bytes 589832 | tf_op jit(solution)/shard_map/ppermute | solution.py:29
  120.4 9.2 %collective-permute-start.21 = (bf16[128,768]{1,0:T(8,128)(2,1)S(1)}, bf16[128,768]{1,0:T(8,128)(2,1)S(1)}, u32[]{:S(2)}, u32[]{:S(2)}) collective-permute-start(bf16[128,768]{1,0:T(8,128)(2,1)S(1)} %get-tuple-element.85), channel_id=1, source_target_pairs={{2,0},{3,1},{4,2},{5,3},{6,4},{7,5},{8,6},{9,7},{10,8},{11,9},{12,... | collective-permute-start | bytes 589832 | tf_op jit(solution)/shard_map/ppermute | solution.py:29
  126.4 5.3 %collective-permute-start.19 = (bf16[128,768]{1,0:T(8,128)(2,1)S(1)}, bf16[128,768]{1,0:T(8,128)(2,1)S(1)}, u32[]{:S(2)}, u32[]{:S(2)}) collective-permute-start(bf16[128,768]{1,0:T(8,128)(2,1)S(1)} %get-tuple-element.79), channel_id=1, source_target_pairs={{2,0},{3,1},{4,2},{5,3},{6,4},{7,5},{8,6},{9,7},{10,8},{11,9},{12,... | collective-permute-start | bytes 589832 | tf_op jit(solution)/shard_map/ppermute | solution.py:29

commit v3 on v2

--- a/solution.py
+++ b/solution.py
@@ -78,11 +78,13 @@
     return jnp.where(last, passed[0], low), jnp.where(last, passed[1], high)
 
 
-def rows_kernel(levels, shift_hbm, scale_hbm, gate_hbm, rows, shift, scale, gate, arrived):
-    tables = ((shift_hbm, shift), (scale_hbm, scale), (gate_hbm, gate))
+def rows_kernel(levels_hbm, shift_hbm, scale_hbm, gate_hbm, rows, levels, shift, scale, gate, arrived):
+    tables = ((levels_hbm, levels), (shift_hbm, shift), (scale_hbm, scale), (gate_hbm, gate))
     copies = [pltpu.make_async_copy(a, b, arrived.at[n]) for n, (a, b) in enumerate(tables)]
     for copy in copies:
         copy.start()
+    for copy in copies:
+        copy.wait()
     position = lax.axis_index("queue")
     level = levels[position]
     below = levels[jnp.maximum(position - 1, 0)]
@@ -96,8 +98,6 @@
             chosen = jnp.logical_or(chosen, jnp.logical_and(row == near, column == below))
         return dot(jnp.where(chosen, 1.0, 0.0).astype(jnp.bfloat16), table[...])
 
-    for copy in copies:
-        copy.wait()
     out = picked(shift, SHIFT, NEAR_SHIFT) + picked(scale, SCALE, NEAR_SCALE)
     rows[...] = (out + picked(gate, GATE, None)).astype(jnp.bfloat16)
 
@@ -107,38 +107,50 @@
     return pl.pallas_call(
         rows_kernel,
         out_shape=jax.ShapeDtypeStruct((TABLE_ROWS, tables[0].shape[1]), jnp.bfloat16),
-        in_specs=[pl.BlockSpec(memory_space=pltpu.SMEM)] + [pl.BlockSpec(memory_space=pltpu.HBM)] * len(tables),
+        in_specs=[pl.BlockSpec(memory_space=pl.ANY)] * (1 + len(tables)),
         out_specs=pl.BlockSpec(memory_space=pltpu.VMEM),
-        scratch_shapes=held + [pltpu.SemaphoreType.DMA((len(tables),))],
+        scratch_shapes=[pltpu.SMEM(levels.shape, levels.dtype)] + held + [pltpu.SemaphoreType.DMA((1 + len(tables),))],
         compiler_params=pltpu.CompilerParams(vmem_limit_bytes=VMEM_LIMIT),
-    )(levels, *(pltpu.with_memory_space_constraint(table, pltpu.HBM) for table in tables))
-
-
-def stage_kernel(w_hbm, w_out_hbm, q_gain, k_gain, w, w_out, gains, arrived):
-    copies = [pltpu.make_async_copy(w_hbm, w, arrived.at[0]), pltpu.make_async_copy(w_out_hbm, w_out, arrived.at[1])]
+    )(*(pltpu.with_memory_space_constraint(a, pltpu.HBM) for a in (levels, *tables)))
+
+
+def stage_kernel(w_hbm, q_hbm, k_hbm, fresh_hbm, w_out_hbm, w, gains, fresh, w_out, q_gain, k_gain, arrived):
+    moves = (
+        (w_hbm, w),
+        (q_hbm, q_gain),
+        (k_hbm, k_gain),
+        (fresh_hbm.at[0 : STEPS - 1], fresh),
+        (w_out_hbm, w_out),
+    )
+    copies = [pltpu.make_async_copy(a, b, arrived.at[n]) for n, (a, b) in enumerate(moves)]
     for copy in copies:
         copy.start()
+    for copy in copies:
+        copy.wait()
     gains[0:1, :] = q_gain[...].reshape(1, -1)
     gains[1:2, :] = k_gain[...].reshape(1, -1)
-    for copy in copies:
-        copy.wait()
-
-
-def stage_call(w, w_out, q_gain, k_gain):
+
+
+def stage_call(w, q_gain, k_gain, fresh, w_out):
     vmem = pl.BlockSpec(memory_space=pltpu.VMEM)
-    held = [pltpu.with_memory_space_constraint(a, pltpu.HBM) for a in (w, w_out)]
+    held = [pltpu.with_memory_space_constraint(a, pltpu.HBM) for a in (w, q_gain, k_gain, fresh, w_out)]
     return pl.pallas_call(
         stage_kernel,
         out_shape=(
             pltpu.VMEM(w.shape, w.dtype),
+            pltpu.VMEM((2, q_gain.shape[0]), q_gain.dtype),
+            pltpu.VMEM((STEPS - 1, *fresh.shape[1:]), fresh.dtype),
             pltpu.VMEM(w_out.shape, w_out.dtype),
-            pltpu.VMEM((2, q_gain.shape[0]), q_gain.dtype),
         ),
-        in_specs=[pl.BlockSpec(memory_space=pl.ANY)] * 2 + [vmem] * 2,
-        out_specs=(vmem, vmem, vmem),
-        scratch_shapes=[pltpu.SemaphoreType.DMA((2,))],
+        in_specs=[pl.BlockSpec(memory_space=pl.ANY)] * 5,
+        out_specs=(vmem, vmem, vmem, vmem),
+        scratch_shapes=[
+            pltpu.VMEM(q_gain.shape, q_gain.dtype),
+            pltpu.VMEM(k_gain.shape, k_gain.dtype),
+            pltpu.SemaphoreType.DMA((5,)),
+        ],
         compiler_params=pltpu.CompilerParams(vmem_limit_bytes=VMEM_LIMIT),
-    )(*held, q_gain, k_gain)
+    )(*held)
 
 
 def near_kernel(kind, rows_mine, rows_other, w, gains, *refs):
@@ -344,29 +356,26 @@
     def down(block):
         return routed(block, lambda q, h: (q - 1, h))
 
-    w_out_hbm = w_out
     other = swap(frames)
     rows_mine = rows_call(level_index, (mod_shift, mod_scale, mod_gate))
     rows_other = swap(rows_mine)
-    w, w_out, gains = stage_call(w, w_out, q_gain, k_gain)
+    w_out_hbm = w_out
+    w, gains, fresh, w_out = stage_call(w, q_gain, k_gain, fresh_groups, w_out)
     near_mine = up(frames)
-    near_other = up(after(other, rows_other, gains))
-    piece = routed(fetched_piece(w_out_hbm), lambda q, h: (q ^ 2, 1 - h))
+    piece = routed(after(fetched_piece(w_out_hbm), other, rows_other, gains, near_mine), lambda q, h: (q ^ 2, 1 - h))
+    near_other = up(after(other, rows_other, gains, near_mine))
+    piece = routed(after(fetched_piece(w_out_hbm), other, rows_other, gains, near_mine), lambda q, h: (q ^ 2, 1 - h))
     table = (rows_mine, rows_other)
     kind, state = "pair", (frames, other)
     near_kind, near = "pair", (near_mine, near_other)
     *queries, keys, values = kernel_call(
         functools.partial(qkv_kernel, kind),
-        ((count, width),) * CHUNKS + ((rows, width), (rows, width)),
+        ((count, width),) * CHUNKS + ((rows, width),) * 2,
         (),
         (*table, w, gains, *state),
         3 * group_products,
     )
-    fresh_other = routed(
-        after(fresh_groups[: STEPS - 1], other),
-        lambda q, h: (last, 1 - h) if q == last - 2 else None,
-    )
-    near = (near_mine, after(near_other, keys, fresh_other))
+    near = (near_mine, after(near_other, keys))
     for step in range(STEPS):
         near_keys, near_values = kernel_call(
             functools.partial(near_kernel, near_kind),
@@ -375,9 +384,8 @@
             (*table, w, gains, *near),
             2 * group_products,
         )
-        if step == 0:
-            parts = []
-        else:
+        parts = []
+        if step > 0:
             first, *queries, keys, values = kernel_call(
                 functools.partial(own_kernel, kind, step - 1, count),
                 ((count, width), (rows - count, width), (rows, width), (rows, width)),
@@ -388,7 +396,7 @@
             )
             parts = [first]
         for query in queries:
-            part = kernel_call(
+            rest = kernel_call(
                 rest_kernel,
                 (count, width),
                 (window_start,),
@@ -396,10 +404,11 @@
                 attention_products,
                 attention_products // HD,
             )
-            parts.append(part)
+            parts.append(rest)
         received = [swap(part) for part in parts]
+        received[0] = after(received[0], parts[1])
         if step == 0:
-            w_other = other_projection(after(piece, other, rows_other, near_mine), near_keys, w_out.shape)
+            w_other = other_projection(piece, received[0], w_out.shape)
         if step < STEPS - 1:
             new = []
             for n in range(CHUNKS):
@@ -411,8 +420,13 @@
                     2 * out_products,
                 )
                 new.append(block)
-            state = (fresh_groups, fresh_other, *[down(block) for block in new])
-            near_kind, near = "chunks", (fresh_groups, fresh_other, *(after(block, state[2]) for block in new))
+            if step == 0:
+                fresh_other = routed(
+                    after(fresh, keys),
+                    lambda q, h: (last, 1 - h) if q == last - 2 else None,
+                )
+            state = (fresh, fresh_other, *[down(block) for block in new])
+            near_kind, near = "chunks", (fresh, fresh_other, *(after(block, state[2]) for block in new))
             kind = "fresh"
         else:
             done = []

time: 133 us -> 130 us (0.977)
  waiting for transfers between devices: 41.7 us -> 33.5 us
  starting transfers between devices: 47.5 us -> 53.6 us
  local copies, waits for them, and re-layouts: 2.6 us -> 1 us
    ppermute x22, waiting for transfers between devices: 41.7 us -> 33.5 us  [routed(): return lax.ppermute(block, AXES, pairs)]
    ppermute x22, starting transfers between devices: 47.5 us -> 53.6 us  [routed(): return lax.ppermute(block, AXES, pairs)]
  transfers between devices with their start and end apart: 22 -> 22, of which waited for: 13 -> 13; matrix products, arithmetic and copies ran while one was open for 2% -> 1% of each run, Pallas kernels for 21% -> 22%
where the time goes in v3:
time: 130 us
  starting transfers between devices  53.6 us (41%)
  Pallas kernels  37.9 us (29%)
  waiting for transfers between devices  33.5 us (26%)
  other arithmetic  2.77 us (2%)
    ppermute x22, starting transfers between devices, routed(): return lax.ppermute(block, AXES, pairs)  53.6 us
    ppermute x22, waiting for transfers between devices, routed(): return lax.ppermute(block, AXES, pairs)  33.5 us
    pallas_call x17, Pallas kernels, kernel_call(): pl.pallas_call(kernel, cost_estimate=pl.CostEstimate(flops=2 * products,...  32.7 us
    pallas_call x1, Pallas kernels, stage_call(): pl.pallas_call(stage_kernel, out_shape=(pltpu.VMEM(w.shape, w.dtype), plt...  4.03 us
  transfers between devices with their start and end apart: 22, of which 13 were waited for; matrix products, arithmetic and copies ran while one was open for 1% of the time, Pallas kernels for 22%

profile of v3, /device:TPU:12, one launch (start us, length us, event | category | flops | bytes accessed | tf_op | source)
XLA Modules:
  0.0 129.8 jit_solution(3163936320959976211)
XLA Ops:
  1.2 1.9 %collective-permute-start.2 = (bf16[256,768]{1,0:T(8,128)(2,1)}, bf16[256,768]{1,0:T(8,128)(2,1)S(1)}, u32[]{:S(2)}, u32[]{:S(2)}) collective-permute-start(bf16[256,768]{1,0:T(8,128)(2,1)} %refs_0_.5), channel_id=1, source_target_pairs={{0,2},{1,3},{2,4},{3,5},{4,6},{5,7},{6,8},{7,9},{8,10},{9,11},{10,... | collective-permute-start | bytes 1179656 | tf_op jit(solution)/shard_map/ppermute | solution.py:29
  4.4 3.1 %collective-permute-start.1 = (bf16[16,768]{1,0:T(8,128)(2,1)S(1)}, bf16[16,768]{1,0:T(8,128)(2,1)S(1)}, u32[]{:S(2)}, u32[]{:S(2)}) collective-permute-start(bf16[16,768]{1,0:T(8,128)(2,1)S(1)} %shard_map.122.rows_mine), channel_id=1, source_target_pairs={{0,1},{1,0},{2,3},{3,2},{4,5},{5,4},{6,7},{7,6},{8,9},{9,8},{10,11... | collective-permute-start | bytes 73736 | tf_op jit(solution)/shard_map/ppermute | solution.py:29
  7.5 4.0 %shard_map.123 = (bf16[3,1536,768]{2,1,0:T(8,128)(2,1)S(1)}, f32[2,768]{1,0:T(2,128)S(1)}, bf16[2,256,768]{2,1,0:T(8,128)(2,1)S(1)}, bf16[768,1536]{1,0:T(8,128)(2,1)S(1)}) custom-call(bf16[3,1536,768]{2,1,0:T(8,128)(2,1)} %bitcast.11, f32[768]{0:T(1024)} %q_hbm.1, f32[768]{0:T(1024)} %k_hbm.1, bf16[3,256,768]{2,1,0:T(8,128)(2,1)} %fresh_hbm.1, ...), custom_call_target="tpu_custom_call" | custom-call | tf_op jit(solution)/shard_map/pallas_call | solution.py:137
  11.5 3.5 %collective-permute-done.1.rows_other = bf16[16,768]{1,0:T(8,128)(2,1)S(1)} collective-permute-done((bf16[16,768]{1,0:T(8,128)(2,1)S(1)}, bf16[16,768]{1,0:T(8,128)(2,1)S(1)}, u32[]{:S(2)}, u32[]{:S(2)}) %collective-permute-start.1) | collective-permute-done | bytes 24608 | tf_op jit(solution)/shard_map/ppermute | solution.py:29
  15.3 4.4 %collective-permute-start.7 = (bf16[256,768]{1,0:T(8,128)(2,1)S(1)}, bf16[256,768]{1,0:T(8,128)(2,1)S(1)}, u32[]{:S(2)}, u32[]{:S(2)}) collective-permute-start(bf16[256,768]{1,0:T(8,128)(2,1)S(1)} %collective-permute-done.refs_1_), channel_id=1, source_target_pairs={{0,2},{1,3},{2,4},{3,5},{4,6},{5,7},{6,8},{7,9},{8,10},{9,11},{10,... | collective-permute-start | bytes 1179656 | tf_op jit(solution)/shard_map/ppermute | solution.py:29
  21.6 2.3 %shard_map.124 = (bf16[128,768]{1,0:T(8,128)(2,1)S(1)}, bf16[128,768]{1,0:T(8,128)(2,1)S(1)}, bf16[256,768]{1,0:T(8,128)(2,1)S(1)}, bf16[256,768]{1,0:T(8,128)(2,1)S(1)}) custom-call(bf16[16,768]{1,0:T(8,128)(2,1)S(1)} %shard_map.122.rows_mine, bf16[16,768]{1,0:T(8,128)(2,1)S(1)} %collective-permute-done.1.rows_other, ...), custom_call_target="tpu_custom_call" | custom-call | flops 1811939328 | bytes 7919616 | tf_op jit(solution)/shard_map/pallas_call | solution.py:292
  23.9 6.4 %collective-permute-done.3.own = bf16[96,1536]{1,0:T(8,128)(2,1)S(1)} collective-permute-done((bf16[96,1536]{1,0:T(8,128)(2,1)S(1)}, bf16[96,1536]{1,0:T(8,128)(2,1)S(1)}, u32[]{:S(2)}, u32[]{:S(2)}) %collective-permute-start.3) | collective-permute-done | bytes 294944 | tf_op jit(solution)/shard_map/ppermute | solution.py:29
  32.3 1.9 %collective-permute-start.6 = (bf16[96,1536]{1,0:T(8,128)(2,1)S(1)}, bf16[96,1536]{1,0:T(8,128)(2,1)S(1)}, u32[]{:S(2)}, u32[]{:S(2)}) collective-permute-start(bf16[96,1536]{1,0:T(8,128)(2,1)S(1)} %collective-permute-done.3.own), channel_id=1, source_target_pairs={{0,8},{1,9},{2,10},{3,11},{4,12},{5,13},{6,14},{7,15},{8,16},{9,17... | collective-permute-start | bytes 884744 | tf_op jit(solution)/shard_map/ppermute | solution.py:29
  34.2 1.6 %shard_map.125 = (bf16[256,768]{1,0:T(8,128)(2,1)S(1)}, bf16[256,768]{1,0:T(8,128)(2,1)S(1)}) custom-call(bf16[16,768]{1,0:T(8,128)(2,1)S(1)} %shard_map.122.rows_mine, bf16[16,768]{1,0:T(8,128)(2,1)S(1)} %collective-permute-done.1.rows_other, bf16[3,1536,768]{2,1,0:T(8,128)(2,1)S(1)} %get-tuple-element.52.w, f32[2,768]{1,0:T(2,128)S(1)} %get-tuple-element.50.gains, ...), custom_call_target="tpu_custom_call" | custom-call | flops 1207959552 | bytes 7919616 | tf_op jit(solution)/shard_map/pallas_call | solution.py:292
  35.9 2.3 %shard_map.126.a_mine = bf16[128,768]{1,0:T(8,128)(2,1)S(1)} custom-call(s32[128]{0:T(128)S(1)} %copy-done.2, bf16[128,768]{1,0:T(8,128)(2,1)S(1)} %get-tuple-element.53.queries, bf16[256,768]{1,0:T(8,128)(2,1)S(1)} %get-tuple-element.54.keys, bf16[256,768]{1,0:T(8,128)(2,1)S(1)} %get-tuple-element.55.values, ...), custom_call_target="tpu_custom_call" | custom-call | flops 201326592 | bytes 1769472 | tf_op jit(solution)/shard_map/pallas_call | solution.py:292
  39.6 2.3 %shard_map.127.a_mine = bf16[128,768]{1,0:T(8,128)(2,1)S(1)} custom-call(s32[128]{0:T(128)S(1)} %copy-done.2, bf16[128,768]{1,0:T(8,128)(2,1)S(1)} %get-tuple-element.61.queries, bf16[256,768]{1,0:T(8,128)(2,1)S(1)} %get-tuple-element.54.keys, bf16[256,768]{1,0:T(8,128)(2,1)S(1)} %get-tuple-element.55.values, ...), custom_call_target="tpu_custom_call" | custom-call | flops 201326592 | bytes 1769472 | tf_op jit(solution)/shard_map/pallas_call | solution.py:292
  41.9 4.1 %collective-permute-done.8.a_other = bf16[128,768]{1,0:T(8,128)(2,1)S(1)} collective-permute-done((bf16[128,768]{1,0:T(8,128)(2,1)S(1)}, bf16[128,768]{1,0:T(8,128)(2,1)S(1)}, u32[]{:S(2)}, u32[]{:S(2)}) %collective-permute-start.8) | collective-permute-done | bytes 196640 | tf_op jit(solution)/shard_map/ppermute | solution.py:29
  47.0 2.0 %collective-permute-start.12 = (bf16[128,768]{1,0:T(8,128)(2,1)S(1)}, bf16[128,768]{1,0:T(8,128)(2,1)S(1)}, u32[]{:S(2)}, u32[]{:S(2)}) collective-permute-start(bf16[128,768]{1,0:T(8,128)(2,1)S(1)} %shard_map.127.a_mine), channel_id=1, source_target_pairs={{0,1},{1,0},{2,3},{3,2},{4,5},{5,4},{6,7},{7,6},{8,9},{9,8},{10,11... | collective-permute-start | bytes 589832 | tf_op jit(solution)/shard_map/ppermute | solution.py:29
  50.6 7.8 %collective-permute-start.11 = (bf16[128,1536]{1,0:T(8,128)(2,1)S(1)}, bf16[128,1536]{1,0:T(8,128)(2,1)S(1)}, u32[]{:S(2)}, u32[]{:S(2)}) collective-permute-start(bf16[128,1536]{1,0:T(8,128)(2,1)S(1)} %shard_map.129.refs_2_), channel_id=1, source_target_pairs={{2,0},{3,1},{4,2},{5,3},{6,4},{7,5},{8,6},{9,7},{10,8},{11,9},{12,... | collective-permute-start | bytes 1179656 | tf_op jit(solution)/shard_map/ppermute | solution.py:29
  59.9 4.1 %collective-permute-start.13 = (bf16[128,1536]{1,0:T(8,128)(2,1)S(1)}, bf16[128,1536]{1,0:T(8,128)(2,1)S(1)}, u32[]{:S(2)}, u32[]{:S(2)}) collective-permute-start(bf16[128,1536]{1,0:T(8,128)(2,1)S(1)} %shard_map.130.refs_3_), channel_id=1, source_target_pairs={{2,0},{3,1},{4,2},{5,3},{6,4},{7,5},{8,6},{9,7},{10,8},{11,9},{12,... | collective-permute-start | bytes 1179656 | tf_op jit(solution)/shard_map/ppermute | solution.py:29
  65.6 3.7 %collective-permute-done.13.refs_3_ = bf16[128,1536]{1,0:T(8,128)(2,1)S(1)} collective-permute-done((bf16[128,1536]{1,0:T(8,128)(2,1)S(1)}, bf16[128,1536]{1,0:T(8,128)(2,1)S(1)}, u32[]{:S(2)}, u32[]{:S(2)}) %collective-permute-start.13) | collective-permute-done | bytes 393248 | tf_op jit(solution)/shard_map/ppermute | solution.py:29
  69.3 4.4 %shard_map.132 = (bf16[128,768]{1,0:T(8,128)(2,1)S(1)}, bf16[128,768]{1,0:T(8,128)(2,1)S(1)}, bf16[256,768]{1,0:T(8,128)(2,1)S(1)}, bf16[256,768]{1,0:T(8,128)(2,1)S(1)}) custom-call(s32[128]{0:T(128)S(1)} %copy-done.2, bf16[16,768]{1,0:T(8,128)(2,1)S(1)} %shard_map.122.rows_mine, bf16[16,768]{1,0:T(8,128)(2,1)S(1)} %collective-permute-done.1.rows_other, ...), custom_call_target="tpu_custom_call" | custom-call | flops 2013265920 | bytes 10278912 | tf_op jit(solution)/shard_map/pallas_call | solution.py:292
  73.7 2.2 %collective-permute-start.14 = (bf16[128,768]{1,0:T(8,128)(2,1)S(1)}, bf16[128,768]{1,0:T(8,128)(2,1)S(1)}, u32[]{:S(2)}, u32[]{:S(2)}) collective-permute-start(bf16[128,768]{1,0:T(8,128)(2,1)S(1)} %get-tuple-element.74.a_mine), channel_id=1, source_target_pairs={{0,1},{1,0},{2,3},{3,2},{4,5},{5,4},{6,7},{7,6},{8,9},{9,8},{10,11... | collective-permute-start | bytes 589832 | tf_op jit(solution)/shard_map/ppermute | solution.py:29
  75.9 2.3 %shard_map.133.a_mine = bf16[128,768]{1,0:T(8,128)(2,1)S(1)} custom-call(s32[128]{0:T(128)S(1)} %copy-done.2, bf16[128,768]{1,0:T(8,128)(2,1)S(1)} %get-tuple-element.76.queries, bf16[256,768]{1,0:T(8,128)(2,1)S(1)} %get-tuple-element.77.keys, bf16[256,768]{1,0:T(8,128)(2,1)S(1)} %get-tuple-element.78.values, ...), custom_call_target="tpu_custom_call" | custom-call | flops 201326592 | bytes 1769472 | tf_op jit(solution)/shard_map/pallas_call | solution.py:292
  79.7 3.4 %collective-permute-done.14.a_other = bf16[128,768]{1,0:T(8,128)(2,1)S(1)} collective-permute-done((bf16[128,768]{1,0:T(8,128)(2,1)S(1)}, bf16[128,768]{1,0:T(8,128)(2,1)S(1)}, u32[]{:S(2)}, u32[]{:S(2)}) %collective-permute-start.14) | collective-permute-done | bytes 196640 | tf_op jit(solution)/shard_map/ppermute | solution.py:29
  84.4 4.3 %collective-permute-start.15 = (bf16[128,1536]{1,0:T(8,128)(2,1)S(1)}, bf16[128,1536]{1,0:T(8,128)(2,1)S(1)}, u32[]{:S(2)}, u32[]{:S(2)}) collective-permute-start(bf16[128,1536]{1,0:T(8,128)(2,1)S(1)} %shard_map.134.refs_2_), channel_id=1, source_target_pairs={{2,0},{3,1},{4,2},{5,3},{6,4},{7,5},{8,6},{9,7},{10,8},{11,9},{12,... | collective-permute-start | bytes 1179656 | tf_op jit(solution)/shard_map/ppermute | solution.py:29
  90.1 3.0 %collective-permute-start.17 = (bf16[128,1536]{1,0:T(8,128)(2,1)S(1)}, bf16[128,1536]{1,0:T(8,128)(2,1)S(1)}, u32[]{:S(2)}, u32[]{:S(2)}) collective-permute-start(bf16[128,1536]{1,0:T(8,128)(2,1)S(1)} %shard_map.135.refs_3_), channel_id=1, source_target_pairs={{2,0},{3,1},{4,2},{5,3},{6,4},{7,5},{8,6},{9,7},{10,8},{11,9},{12,... | collective-permute-start | bytes 1179656 | tf_op jit(solution)/shard_map/ppermute | solution.py:29
  95.6 2.6 %collective-permute-done.17.refs_3_ = bf16[128,1536]{1,0:T(8,128)(2,1)S(1)} collective-permute-done((bf16[128,1536]{1,0:T(8,128)(2,1)S(1)}, bf16[128,1536]{1,0:T(8,128)(2,1)S(1)}, u32[]{:S(2)}, u32[]{:S(2)}) %collective-permute-start.17) | collective-permute-done | bytes 393248 | tf_op jit(solution)/shard_map/ppermute | solution.py:29
  98.2 4.4 %shard_map.137 = (bf16[128,768]{1,0:T(8,128)(2,1)S(1)}, bf16[128,768]{1,0:T(8,128)(2,1)S(1)}, bf16[256,768]{1,0:T(8,128)(2,1)S(1)}, bf16[256,768]{1,0:T(8,128)(2,1)S(1)}) custom-call(s32[128]{0:T(128)S(1)} %copy-done.2, bf16[16,768]{1,0:T(8,128)(2,1)S(1)} %shard_map.122.rows_mine, bf16[16,768]{1,0:T(8,128)(2,1)S(1)} %collective-permute-done.1.rows_other, ...), custom_call_target="tpu_custom_call" | custom-call | flops 2013265920 | bytes 10278912 | tf_op jit(solution)/shard_map/pallas_call | solution.py:292
  102.6 3.5 %collective-permute-start.18 = (bf16[128,768]{1,0:T(8,128)(2,1)S(1)}, bf16[128,768]{1,0:T(8,128)(2,1)S(1)}, u32[]{:S(2)}, u32[]{:S(2)}) collective-permute-start(bf16[128,768]{1,0:T(8,128)(2,1)S(1)} %get-tuple-element.85.a_mine), channel_id=1, source_target_pairs={{0,1},{1,0},{2,3},{3,2},{4,5},{5,4},{6,7},{7,6},{8,9},{9,8},{10,11... | collective-permute-start | bytes 589832 | tf_op jit(solution)/shard_map/ppermute | solution.py:29
  106.1 2.3 %shard_map.138.a_mine = bf16[128,768]{1,0:T(8,128)(2,1)S(1)} custom-call(s32[128]{0:T(128)S(1)} %copy-done.2, bf16[128,768]{1,0:T(8,128)(2,1)S(1)} %get-tuple-element.87.queries, bf16[256,768]{1,0:T(8,128)(2,1)S(1)} %get-tuple-element.88.keys, bf16[256,768]{1,0:T(8,128)(2,1)S(1)} %get-tuple-element.89.values, ...), custom_call_target="tpu_custom_call" | custom-call | flops 201326592 | bytes 1769472 | tf_op jit(solution)/shard_map/pallas_call | solution.py:292
  108.6 2.5 %collective-permute-done.18.a_other = bf16[128,768]{1,0:T(8,128)(2,1)S(1)} collective-permute-done((bf16[128,768]{1,0:T(8,128)(2,1)S(1)}, bf16[128,768]{1,0:T(8,128)(2,1)S(1)}, u32[]{:S(2)}, u32[]{:S(2)}) %collective-permute-start.18) | collective-permute-done | bytes 196640 | tf_op jit(solution)/shard_map/ppermute | solution.py:29
  112.1 3.5 %collective-permute-done.20.a_other = bf16[128,768]{1,0:T(8,128)(2,1)S(1)} collective-permute-done((bf16[128,768]{1,0:T(8,128)(2,1)S(1)}, bf16[128,768]{1,0:T(8,128)(2,1)S(1)}, u32[]{:S(2)}, u32[]{:S(2)}) %collective-permute-start.20) | collective-permute-done | bytes 196640 | tf_op jit(solution)/shard_map/ppermute | solution.py:29
  116.7 6.0 %collective-permute-start.21 = (bf16[128,768]{1,0:T(8,128)(2,1)S(1)}, bf16[128,768]{1,0:T(8,128)(2,1)S(1)}, u32[]{:S(2)}, u32[]{:S(2)}) collective-permute-start(bf16[128,768]{1,0:T(8,128)(2,1)S(1)} %get-tuple-element.93), channel_id=1, source_target_pairs={{2,0},{3,1},{4,2},{5,3},{6,4},{7,5},{8,6},{9,7},{10,8},{11,9},{12,... | collective-permute-start | bytes 589832 | tf_op jit(solution)/shard_map/ppermute | solution.py:29
  122.7 1.9 %collective-permute-start.19 = (bf16[128,768]{1,0:T(8,128)(2,1)S(1)}, bf16[128,768]{1,0:T(8,128)(2,1)S(1)}, u32[]{:S(2)}, u32[]{:S(2)}) collective-permute-start(bf16[128,768]{1,0:T(8,128)(2,1)S(1)} %get-tuple-element.91), channel_id=1, source_target_pairs={{2,0},{3,1},{4,2},{5,3},{6,4},{7,5},{8,6},{9,7},{10,8},{11,9},{12,... | collective-permute-start | bytes 589832 | tf_op jit(solution)/shard_map/ppermute | solution.py:29
  125.9 2.1 %collective-permute-done.19 = bf16[128,768]{1,0:T(8,128)(2,1)S(1)} collective-permute-done((bf16[128,768]{1,0:T(8,128)(2,1)S(1)}, bf16[128,768]{1,0:T(8,128)(2,1)S(1)}, u32[]{:S(2)}, u32[]{:S(2)}) %collective-permute-start.19) | collective-permute-done | bytes 196640 | tf_op jit(solution)/shard_map/ppermute | solution.py:29
  128.0 1.8 %maximum_select_fusion = bf16[256,768]{1,0:T(8,128)(2,1)} fusion(bf16[128,768]{1,0:T(8,128)(2,1)S(1)} %collective-permute-done.21, bf16[128,768]{1,0:T(8,128)(2,1)S(1)} %collective-permute-done.19, bf16[3,256,768]{2,1,0:T(8,128)(2,1)} %fresh_hbm.1, pred[]{:T(512)S(6)} %eq.7), kind=kLoop, calls=%fused_computation.1 | loop fusion | flops 983040 | bytes 1179649 | tf_op jit(solution)/shard_map/jit(_where)/select_n | solution.py:444
  (41 shorter events, 23.3 us)
Async XLA Ops:
  0.6 14.3 %collective-permute-start = (bf16[256,768]{1,0:T(8,128)(2,1)}, bf16[256,768]{1,0:T(8,128)(2,1)S(1)}, u32[]{:S(2)}, u32[]{:S(2)}) collective-permute-start(bf16[256,768]{1,0:T(8,128)(2,1)} %refs_0_.5), channel_id=1, source_target_pairs={{0,1},{1,0},{2,3},{3,2},{4,5},{5,4},{6,7},{7,6},{8,9},{9,8},{10,11... | collective-permute-start | bytes 1179656 | tf_op jit(solution)/shard_map/ppermute | solution.py:29
  1.2 14.1 %collective-permute-start.2 = (bf16[256,768]{1,0:T(8,128)(2,1)}, bf16[256,768]{1,0:T(8,128)(2,1)S(1)}, u32[]{:S(2)}, u32[]{:S(2)}) collective-permute-start(bf16[256,768]{1,0:T(8,128)(2,1)} %refs_0_.5), channel_id=1, source_target_pairs={{0,2},{1,3},{2,4},{3,5},{4,6},{5,7},{6,8},{7,9},{8,10},{9,11},{10,... | collective-permute-start | bytes 1179656 | tf_op jit(solution)/shard_map/ppermute | solution.py:29
  4.4 10.6 %collective-permute-start.1 = (bf16[16,768]{1,0:T(8,128)(2,1)S(1)}, bf16[16,768]{1,0:T(8,128)(2,1)S(1)}, u32[]{:S(2)}, u32[]{:S(2)}) collective-permute-start(bf16[16,768]{1,0:T(8,128)(2,1)S(1)} %shard_map.122.rows_mine), channel_id=1, source_target_pairs={{0,1},{1,0},{2,3},{3,2},{4,5},{5,4},{6,7},{7,6},{8,9},{9,8},{10,11... | collective-permute-start | bytes 73736 | tf_op jit(solution)/shard_map/ppermute | solution.py:29
  7.5 14.1 %copy-start = (bf16[256,768]{1,0:T(8,128)(2,1)S(1)}, bf16[256,768]{1,0:T(8,128)(2,1)}, u32[]{:S(2)}) copy-start(bf16[256,768]{1,0:T(8,128)(2,1)} %refs_0_.5) | copy-start | bytes 1179652
  15.3 18.9 %collective-permute-start.7 = (bf16[256,768]{1,0:T(8,128)(2,1)S(1)}, bf16[256,768]{1,0:T(8,128)(2,1)S(1)}, u32[]{:S(2)}, u32[]{:S(2)}) collective-permute-start(bf16[256,768]{1,0:T(8,128)(2,1)S(1)} %collective-permute-done.refs_1_), channel_id=1, source_target_pairs={{0,2},{1,3},{2,4},{3,5},{4,6},{5,7},{6,8},{7,9},{8,10},{9,11},{10,... | collective-permute-start | bytes 1179656 | tf_op jit(solution)/shard_map/ppermute | solution.py:29
  20.8 9.5 %collective-permute-start.3 = (bf16[96,1536]{1,0:T(8,128)(2,1)S(1)}, bf16[96,1536]{1,0:T(8,128)(2,1)S(1)}, u32[]{:S(2)}, u32[]{:S(2)}) collective-permute-start(bf16[96,1536]{1,0:T(8,128)(2,1)S(1)} %constant_dynamic-slice_fusion), channel_id=1, source_target_pairs={{0,5},{1,4},{2,7},{3,6},{4,1},{5,0},{6,3},{7,2},{8,13},{9,12},{10,... | collective-permute-start | bytes 884744 | tf_op jit(solution)/shard_map/ppermute | solution.py:29
  30.3 15.7 %collective-permute-start.4 = (bf16[96,1536]{1,0:T(8,128)(2,1)S(1)}, bf16[96,1536]{1,0:T(8,128)(2,1)S(1)}, u32[]{:S(2)}, u32[]{:S(2)}) collective-permute-start(bf16[96,1536]{1,0:T(8,128)(2,1)S(1)} %collective-permute-done.3.own), channel_id=1, source_target_pairs={{0,64},{1,65},{2,66},{3,67},{4,68},{5,69},{6,70},{7,71},{8,72},{9,... | collective-permute-start | bytes 884744 | tf_op jit(solution)/shard_map/ppermute | solution.py:29
  31.8 14.1 %collective-permute-start.5 = (bf16[96,1536]{1,0:T(8,128)(2,1)S(1)}, bf16[96,1536]{1,0:T(8,128)(2,1)S(1)}, u32[]{:S(2)}, u32[]{:S(2)}) collective-permute-start(bf16[96,1536]{1,0:T(8,128)(2,1)S(1)} %collective-permute-done.3.own), channel_id=1, source_target_pairs={{0,192},{1,193},{2,194},{3,195},{4,196},{5,197},{6,198},{7,199},{8... | collective-permute-start | bytes 884744 | tf_op jit(solution)/shard_map/ppermute | solution.py:29
  32.3 13.7 %collective-permute-start.6 = (bf16[96,1536]{1,0:T(8,128)(2,1)S(1)}, bf16[96,1536]{1,0:T(8,128)(2,1)S(1)}, u32[]{:S(2)}, u32[]{:S(2)}) collective-permute-start(bf16[96,1536]{1,0:T(8,128)(2,1)S(1)} %collective-permute-done.3.own), channel_id=1, source_target_pairs={{0,8},{1,9},{2,10},{3,11},{4,12},{5,13},{6,14},{7,15},{8,16},{9,17... | collective-permute-start | bytes 884744 | tf_op jit(solution)/shard_map/ppermute | solution.py:29
  34.2 1.7 %copy-start.2 = (s32[128]{0:T(128)S(1)}, s32[128]{0:T(128)}, u32[]{:S(2)}) copy-start(s32[128]{0:T(128)} %starts.11) | copy-start | bytes 1540
  38.2 7.8 %collective-permute-start.8 = (bf16[128,768]{1,0:T(8,128)(2,1)S(1)}, bf16[128,768]{1,0:T(8,128)(2,1)S(1)}, u32[]{:S(2)}, u32[]{:S(2)}) collective-permute-start(bf16[128,768]{1,0:T(8,128)(2,1)S(1)} %shard_map.126.a_mine), channel_id=1, source_target_pairs={{0,1},{1,0},{2,3},{3,2},{4,5},{5,4},{6,7},{7,6},{8,9},{9,8},{10,11... | collective-permute-start | bytes 589832 | tf_op jit(solution)/shard_map/ppermute | solution.py:29
  46.2 2.9 %collective-permute-start.9 = (bf16[4,96,1536]{2,1,0:T(8,128)(2,1)S(1)}, bf16[4,96,1536]{2,1,0:T(8,128)(2,1)S(1)}, u32[]{:S(2)}, u32[]{:S(2)}) collective-permute-start(bf16[4,96,1536]{2,1,0:T(8,128)(2,1)S(1)} %pad_maximum_fusion), channel_id=1, source_target_pairs={{0,2},{1,3},{2,0},{3,1},{4,6},{5,7},{6,4},{7,5},{8,10},{9,11},{10,... | collective-permute-start | bytes 3538952 | tf_op jit(solution)/shard_map/ppermute | solution.py:29
  46.3 3.0 %copy-start.1 = (s32[128]{0:T(128)S(1)}, s32[128]{0:T(128)}, u32[]{:S(2)}) copy-start(s32[128]{0:T(128)} %levels.11) | copy-start | bytes 1540
  46.3 17.7 %collective-permute-start.10 = (bf16[2,256,768]{2,1,0:T(8,128)(2,1)S(1)}, bf16[2,256,768]{2,1,0:T(8,128)(2,1)S(1)}, u32[]{:S(2)}, u32[]{:S(2)}) collective-permute-start(bf16[2,256,768]{2,1,0:T(8,128)(2,1)S(1)} %get-tuple-element.68.refs_0_), channel_id=1, source_target_pairs={{250,255},{251,254}} | collective-permute-start | bytes 2359304 | tf_op jit(solution)/shard_map/ppermute | solution.py:29
  47.0 11.5 %collective-permute-start.12 = (bf16[128,768]{1,0:T(8,128)(2,1)S(1)}, bf16[128,768]{1,0:T(8,128)(2,1)S(1)}, u32[]{:S(2)}, u32[]{:S(2)}) collective-permute-start(bf16[128,768]{1,0:T(8,128)(2,1)S(1)} %shard_map.127.a_mine), channel_id=1, source_target_pairs={{0,1},{1,0},{2,3},{3,2},{4,5},{5,4},{6,7},{7,6},{8,9},{9,8},{10,11... | collective-permute-start | bytes 589832 | tf_op jit(solution)/shard_map/ppermute | solution.py:29
  50.6 13.3 %collective-permute-start.11 = (bf16[128,1536]{1,0:T(8,128)(2,1)S(1)}, bf16[128,1536]{1,0:T(8,128)(2,1)S(1)}, u32[]{:S(2)}, u32[]{:S(2)}) collective-permute-start(bf16[128,1536]{1,0:T(8,128)(2,1)S(1)} %shard_map.129.refs_2_), channel_id=1, source_target_pairs={{2,0},{3,1},{4,2},{5,3},{6,4},{7,5},{8,6},{9,7},{10,8},{11,9},{12,... | collective-permute-start | bytes 1179656 | tf_op jit(solution)/shard_map/ppermute | solution.py:29
  59.9 9.4 %collective-permute-start.13 = (bf16[128,1536]{1,0:T(8,128)(2,1)S(1)}, bf16[128,1536]{1,0:T(8,128)(2,1)S(1)}, u32[]{:S(2)}, u32[]{:S(2)}) collective-permute-start(bf16[128,1536]{1,0:T(8,128)(2,1)S(1)} %shard_map.130.refs_3_), channel_id=1, source_target_pairs={{2,0},{3,1},{4,2},{5,3},{6,4},{7,5},{8,6},{9,7},{10,8},{11,9},{12,... | collective-permute-start | bytes 1179656 | tf_op jit(solution)/shard_map/ppermute | solution.py:29
  73.7 9.3 %collective-permute-start.14 = (bf16[128,768]{1,0:T(8,128)(2,1)S(1)}, bf16[128,768]{1,0:T(8,128)(2,1)S(1)}, u32[]{:S(2)}, u32[]{:S(2)}) collective-permute-start(bf16[128,768]{1,0:T(8,128)(2,1)S(1)} %get-tuple-element.74.a_mine), channel_id=1, source_target_pairs={{0,1},{1,0},{2,3},{3,2},{4,5},{5,4},{6,7},{7,6},{8,9},{9,8},{10,11... | collective-permute-start | bytes 589832 | tf_op jit(solution)/shard_map/ppermute | solution.py:29
  78.2 10.5 %collective-permute-start.16 = (bf16[128,768]{1,0:T(8,128)(2,1)S(1)}, bf16[128,768]{1,0:T(8,128)(2,1)S(1)}, u32[]{:S(2)}, u32[]{:S(2)}) collective-permute-start(bf16[128,768]{1,0:T(8,128)(2,1)S(1)} %shard_map.133.a_mine), channel_id=1, source_target_pairs={{0,1},{1,0},{2,3},{3,2},{4,5},{5,4},{6,7},{7,6},{8,9},{9,8},{10,11... | collective-permute-start | bytes 589832 | tf_op jit(solution)/shard_map/ppermute | solution.py:29
  84.4 9.6 %collective-permute-start.15 = (bf16[128,1536]{1,0:T(8,128)(2,1)S(1)}, bf16[128,1536]{1,0:T(8,128)(2,1)S(1)}, u32[]{:S(2)}, u32[]{:S(2)}) collective-permute-start(bf16[128,1536]{1,0:T(8,128)(2,1)S(1)} %shard_map.134.refs_2_), channel_id=1, source_target_pairs={{2,0},{3,1},{4,2},{5,3},{6,4},{7,5},{8,6},{9,7},{10,8},{11,9},{12,... | collective-permute-start | bytes 1179656 | tf_op jit(solution)/shard_map/ppermute | solution.py:29
  90.1 8.1 %collective-permute-start.17 = (bf16[128,1536]{1,0:T(8,128)(2,1)S(1)}, bf16[128,1536]{1,0:T(8,128)(2,1)S(1)}, u32[]{:S(2)}, u32[]{:S(2)}) collective-permute-start(bf16[128,1536]{1,0:T(8,128)(2,1)S(1)} %shard_map.135.refs_3_), channel_id=1, source_target_pairs={{2,0},{3,1},{4,2},{5,3},{6,4},{7,5},{8,6},{9,7},{10,8},{11,9},{12,... | collective-permute-start | bytes 1179656 | tf_op jit(solution)/shard_map/ppermute | solution.py:29
  102.6 8.5 %collective-permute-start.18 = (bf16[128,768]{1,0:T(8,128)(2,1)S(1)}, bf16[128,768]{1,0:T(8,128)(2,1)S(1)}, u32[]{:S(2)}, u32[]{:S(2)}) collective-permute-start(bf16[128,768]{1,0:T(8,128)(2,1)S(1)} %get-tuple-element.85.a_mine), channel_id=1, source_target_pairs={{0,1},{1,0},{2,3},{3,2},{4,5},{5,4},{6,7},{7,6},{8,9},{9,8},{10,11... | collective-permute-start | bytes 589832 | tf_op jit(solution)/shard_map/ppermute | solution.py:29
  108.4 7.3 %collective-permute-start.20 = (bf16[128,768]{1,0:T(8,128)(2,1)S(1)}, bf16[128,768]{1,0:T(8,128)(2,1)S(1)}, u32[]{:S(2)}, u32[]{:S(2)}) collective-permute-start(bf16[128,768]{1,0:T(8,128)(2,1)S(1)} %shard_map.138.a_mine), channel_id=1, source_target_pairs={{0,1},{1,0},{2,3},{3,2},{4,5},{5,4},{6,7},{7,6},{8,9},{9,8},{10,11... | collective-permute-start | bytes 589832 | tf_op jit(solution)/shard_map/ppermute | solution.py:29
  116.7 9.2 %collective-permute-start.21 = (bf16[128,768]{1,0:T(8,128)(2,1)S(1)}, bf16[128,768]{1,0:T(8,128)(2,1)S(1)}, u32[]{:S(2)}, u32[]{:S(2)}) collective-permute-start(bf16[128,768]{1,0:T(8,128)(2,1)S(1)} %get-tuple-element.93), channel_id=1, source_target_pairs={{2,0},{3,1},{4,2},{5,3},{6,4},{7,5},{8,6},{9,7},{10,8},{11,9},{12,... | collective-permute-start | bytes 589832 | tf_op jit(solution)/shard_map/ppermute | solution.py:29
  122.7 5.3 %collective-permute-start.19 = (bf16[128,768]{1,0:T(8,128)(2,1)S(1)}, bf16[128,768]{1,0:T(8,128)(2,1)S(1)}, u32[]{:S(2)}, u32[]{:S(2)}) collective-permute-start(bf16[128,768]{1,0:T(8,128)(2,1)S(1)} %get-tuple-element.91), channel_id=1, source_target_pairs={{2,0},{3,1},{4,2},{5,3},{6,4},{7,5},{8,6},{9,7},{10,8},{11,9},{12,... | collective-permute-start | bytes 589832 | tf_op jit(solution)/shard_map/ppermute | solution.py:29

commit v4 on v3

--- a/solution.py
+++ b/solution.py
@@ -65,7 +65,7 @@
 def halves_of(kind, refs, step, row, count):
     if kind == "pair":
         return ordered(refs[0][row : row + count, :], refs[1][row : row + count, :])
-    fresh, fresh_other, *chunks = refs
+    chunks = refs if kind == "chunks" else refs[2:]
     size = chunks[0].shape[0]
     wide = [c[...] for c in chunks[row // size : (row + count) // size]]
     wide = wide[0] if len(wide) == 1 else jnp.concatenate(wide, axis=0)
@@ -73,7 +73,7 @@
     low, high = wide[:, :width], wide[:, width:]
     if kind == "chunks":
         return low, high
-    passed = ordered(fresh[step, row : row + count, :], fresh_other[step, row : row + count, :])
+    passed = ordered(*(group[row : row + count, :] for group in refs[:2]))
     last = lax.axis_index("queue") == lax.axis_size("queue") - 1
     return jnp.where(last, passed[0], low), jnp.where(last, passed[1], high)
 
@@ -114,14 +114,10 @@
     )(*(pltpu.with_memory_space_constraint(a, pltpu.HBM) for a in (levels, *tables)))
 
 
-def stage_kernel(w_hbm, q_hbm, k_hbm, fresh_hbm, w_out_hbm, w, gains, fresh, w_out, q_gain, k_gain, arrived):
-    moves = (
-        (w_hbm, w),
-        (q_hbm, q_gain),
-        (k_hbm, k_gain),
-        (fresh_hbm.at[0 : STEPS - 1], fresh),
-        (w_out_hbm, w_out),
-    )
+def stage_kernel(w_hbm, q_hbm, k_hbm, fresh_hbm, w_out_hbm, w, gains, *refs):
+    *fresh, w_out, q_gain, k_gain, arrived = refs
+    moves = [(w_hbm, w), (q_hbm, q_gain), (k_hbm, k_gain), (w_out_hbm, w_out)]
+    moves += [(fresh_hbm.at[n], group) for n, group in enumerate(fresh)]
     copies = [pltpu.make_async_copy(a, b, arrived.at[n]) for n, (a, b) in enumerate(moves)]
     for copy in copies:
         copy.start()
@@ -134,20 +130,21 @@
 def stage_call(w, q_gain, k_gain, fresh, w_out):
     vmem = pl.BlockSpec(memory_space=pltpu.VMEM)
     held = [pltpu.with_memory_space_constraint(a, pltpu.HBM) for a in (w, q_gain, k_gain, fresh, w_out)]
+    groups = [pltpu.VMEM(fresh.shape[1:], fresh.dtype)] * STEPS
     return pl.pallas_call(
         stage_kernel,
         out_shape=(
             pltpu.VMEM(w.shape, w.dtype),
             pltpu.VMEM((2, q_gain.shape[0]), q_gain.dtype),
-            pltpu.VMEM((STEPS - 1, *fresh.shape[1:]), fresh.dtype),
+            *groups,
             pltpu.VMEM(w_out.shape, w_out.dtype),
         ),
         in_specs=[pl.BlockSpec(memory_space=pl.ANY)] * 5,
-        out_specs=(vmem, vmem, vmem, vmem),
+        out_specs=(vmem,) * (3 + len(groups)),
         scratch_shapes=[
             pltpu.VMEM(q_gain.shape, q_gain.dtype),
             pltpu.VMEM(k_gain.shape, k_gain.dtype),
-            pltpu.SemaphoreType.DMA((5,)),
+            pltpu.SemaphoreType.DMA((4 + len(groups),)),
         ],
         compiler_params=pltpu.CompilerParams(vmem_limit_bytes=VMEM_LIMIT),
     )(*held)
@@ -166,19 +163,27 @@
     values[...] = dot(moved, w[2]).astype(jnp.bfloat16)
 
 
-def attend(starts, query, key, value, near_key, near_value):
+def attend(starts, attended, queries, keys, values, near_keys, near_values):
     position = lax.axis_index("queue")
-    start = jnp.where(position > 0, starts[position], near_key.shape[0])
-    visible = lax.broadcasted_iota(jnp.int32, (1, near_key.shape[0]), 1) >= start
+    rows = values.shape[0]
+    start = jnp.where(position > 0, starts[position], rows)
+    visible = lax.broadcasted_iota(jnp.int32, (1, rows), 1) >= start
     factor = 1.4426950408889634 / (HD**0.5)
-    own = dot_t(query, key)
-    near = jnp.where(visible, dot_t(query, near_key), jnp.float32(-1e30))
-    top = jnp.maximum(jnp.max(own, axis=-1, keepdims=True), jnp.max(near, axis=-1, keepdims=True))
-    own = jnp.exp2((own - top) * factor)
-    near = jnp.exp2((near - top) * factor)
-    total = jnp.sum(own, axis=-1, keepdims=True) + jnp.sum(near, axis=-1, keepdims=True)
-    out = dot(own.astype(jnp.bfloat16), value) + dot(near.astype(jnp.bfloat16), near_value)
-    return (out / total).astype(jnp.bfloat16)
+    parts = [slice(a, a + HD) for a in range(0, values.shape[1], HD)]
+    scores = []
+    for n, part in enumerate(parts):
+        near = jnp.where(visible, dot_t(queries[n], near_keys[:, part]), jnp.float32(-1e30))
+        scores.append((dot_t(queries[n], keys[n]), near))
+    tops = [jnp.max(jnp.maximum(own, near), axis=-1, keepdims=True) for own, near in scores]
+    weights = [
+        (jnp.exp2((own - top) * factor), jnp.exp2((near - top) * factor))
+        for (own, near), top in zip(scores, tops)
+    ]
+    totals = [jnp.sum(own + near, axis=-1, keepdims=True) for own, near in weights]
+    for part, (own, near), total in zip(parts, weights, totals):
+        out = dot(own.astype(jnp.bfloat16), values[:, part])
+        out = out + dot(near.astype(jnp.bfloat16), near_values[:, part])
+        attended[:, part] = (out / total).astype(jnp.bfloat16)
 
 
 def own_kernel(kind, step, count, starts, rows_mine, rows_other, w, gains, near_keys, near_values, *refs):
@@ -194,15 +199,16 @@
     value = dot(moved, w[2]).astype(jnp.bfloat16)
     values[...] = value
     q_row, k_row = gains[0:1, :], gains[1:2, :]
+    query_heads, key_heads = [], []
     for a in range(0, width, HD):
         part = slice(a, a + HD)
         query = normed(query_raw[:, part], q_row[:, part])
         key = normed(key_raw[:, part], k_row[:, part])
         queries[:, part] = query[first:]
         keys[:, part] = key
-        attended[:, part] = attend(
-            starts, query[:first], key, value[:, part], near_keys[:, part], near_values[:, part]
-        )
+        query_heads.append(query[:first])
+        key_heads.append(key)
+    attend(starts, attended, query_heads, key_heads, value, near_keys, near_values)
 
 
 def qkv_kernel(kind, rows_mine, rows_other, w, gains, *refs):
@@ -225,11 +231,10 @@
 
 
 def rest_kernel(starts, queries, keys, values, near_keys, near_values, attended):
-    for a in range(0, attended.shape[1], HD):
-        part = slice(a, a + HD)
-        attended[:, part] = attend(
-            starts, queries[:, part], keys[:, part], values[:, part], near_keys[:, part], near_values[:, part]
-        )
+    parts = [slice(a, a + HD) for a in range(0, attended.shape[1], HD)]
+    query_heads = [queries[:, part] for part in parts]
+    key_heads = [keys[:, part] for part in parts]
+    attend(starts, attended, query_heads, key_heads, values, near_keys, near_values)
 
 
 def step_size_of(levels):
@@ -266,6 +271,23 @@
     velocity = rows_mine[GATE : GATE + 1, :].astype(jnp.float32) * product
     velocity_out[...] = velocity.astype(jnp.bfloat16)
     new[...] = (held + step_size_of(levels) * velocity).astype(jnp.bfloat16)
+
+
+def entering(advanced, fresh):
+    last = lax.axis_index("queue") == lax.axis_size("queue") - 1
+    return jnp.where(last, fresh, advanced)
+
+
+def enter_kernel(advanced, fresh, out):
+    out[...] = entering(advanced[...], fresh[: out.shape[0], :])
+
+
+def finish_kernel(first, advanced, fresh, velocity_first, velocity_rest, final, velocity):
+    count = first.shape[0]
+    final[:count, :] = first[...]
+    final[count:, :] = entering(advanced[...], fresh[count:, :])
+    velocity[:count, :] = velocity_first[...]
+    velocity[count:, :] = velocity_rest[...]
 
 
 def piece_of(position):
@@ -319,7 +341,7 @@
 
     back = routed(own, turned(1, 0))
     ahead = routed(own, turned(-1, 0))
-    across = routed(own, turned(0, 1))
+    across = routed(own, turned(0, -1))
     own, back, ahead, across, _ = lax.optimization_barrier((own, back, ahead, across, ready))
     others = routed(jnp.stack([own, back, ahead, across]), lambda q, h: (q ^ 1, h))
     return kernel_call(gather_kernel, shape, (), (own, back, ahead, across, others))
@@ -338,7 +360,6 @@
     k_gain,
     w_out,
 ):
-    position = lax.axis_index("queue")
     last = lax.axis_size("queue") - 1
     rows, width = frames.shape
     count = rows // CHUNKS
@@ -360,11 +381,10 @@
     rows_mine = rows_call(level_index, (mod_shift, mod_scale, mod_gate))
     rows_other = swap(rows_mine)
     w_out_hbm = w_out
-    w, gains, fresh, w_out = stage_call(w, q_gain, k_gain, fresh_groups, w_out)
-    near_mine = up(frames)
-    piece = routed(after(fetched_piece(w_out_hbm), other, rows_other, gains, near_mine), lambda q, h: (q ^ 2, 1 - h))
-    near_other = up(after(other, rows_other, gains, near_mine))
-    piece = routed(after(fetched_piece(w_out_hbm), other, rows_other, gains, near_mine), lambda q, h: (q ^ 2, 1 - h))
+    w, gains, *fresh, w_out = stage_call(w, q_gain, k_gain, fresh_groups, w_out)
+    near_mine = up(after(frames, other))
+    near_other = up(after(other, rows_other, gains))
+    piece = routed(after(fetched_piece(w_out_hbm), rows_mine), lambda q, h: (q ^ 2, 1 - h))
     table = (rows_mine, rows_other)
     kind, state = "pair", (frames, other)
     near_kind, near = "pair", (near_mine, near_other)
@@ -384,6 +404,10 @@
             (*table, w, gains, *near),
             2 * group_products,
         )
+        if step < STEPS - 1:
+            fresh_other = routed(
+                after(fresh[step], near_keys), lambda q, h: (last, 1 - h) if q == last - 2 else None
+            )
         parts = []
         if step > 0:
             first, *queries, keys, values = kernel_call(
@@ -420,13 +444,8 @@
                     2 * out_products,
                 )
                 new.append(block)
-            if step == 0:
-                fresh_other = routed(
-                    after(fresh, keys),
-                    lambda q, h: (last, 1 - h) if q == last - 2 else None,
-                )
-            state = (fresh, fresh_other, *[down(block) for block in new])
-            near_kind, near = "chunks", (fresh, fresh_other, *(after(block, state[2]) for block in new))
+            state = (fresh[step], fresh_other, *[down(block) for block in new])
+            near_kind, near = "chunks", [after(block, state[2]) for block in new]
             kind = "fresh"
         else:
             done = []
@@ -439,9 +458,14 @@
                     out_products,
                 )
                 done.append(pair)
-            advanced = jnp.concatenate([down(block) for block, _ in done], axis=0)
-            velocity = jnp.concatenate([block for _, block in done], axis=0)
-            final = jnp.where(position == last, fresh_groups[step], advanced)
+            advanced = [down(block) for block, _ in done]
+            first = kernel_call(enter_kernel, (count, width), (), (advanced[0], fresh[step]))
+            final, velocity = kernel_call(
+                finish_kernel,
+                ((rows, width), (rows, width)),
+                (),
+                (first, after(advanced[1], first), fresh[step], done[0][1], done[1][1]),
+            )
     return (final, velocity)
 
 

time: 130 us -> 117 us (0.900)
  the two profiles are of different devices: /device:TPU:12 before, /device:TPU:111 now
where the time goes in v4:
time: 117 us
  waiting for transfers between devices  45.6 us (39%)
  starting transfers between devices  36.2 us (31%)
  Pallas kernels  32.8 us (28%)
    ppermute x23, waiting for transfers between devices, routed(): return lax.ppermute(block, AXES, pairs)  45.6 us
    ppermute x23, starting transfers between devices, routed(): return lax.ppermute(block, AXES, pairs)  36.2 us
    pallas_call x19, Pallas kernels, kernel_call(): pl.pallas_call(kernel, cost_estimate=pl.CostEstimate(flops=2 * products,...  27.6 us
    pallas_call x1, Pallas kernels, stage_call(): pl.pallas_call(stage_kernel, out_shape=(pltpu.VMEM(w.shape, w.dtype), plt...  4.05 us
  transfers between devices with their start and end apart: 23, of which 13 were waited for; matrix products, arithmetic and copies ran while one was open for 1% of the time, Pallas kernels for 21%

profile of v4, /device:TPU:111, one launch (start us, length us, event | category | flops | bytes accessed | tf_op | source)
XLA Modules:
  0.0 116.7 jit_solution(13172304049717589461)
XLA Ops:
  4.0 1.9 %collective-permute-start = (bf16[96,1536]{1,0:T(8,128)(2,1)S(1)}, bf16[96,1536]{1,0:T(8,128)(2,1)S(1)}, u32[]{:S(2)}, u32[]{:S(2)}) collective-permute-start(bf16[96,1536]{1,0:T(8,128)(2,1)S(1)} %constant_dynamic-slice_fusion), channel_id=1, source_target_pairs={{0,5},{1,4},{2,7},{3,6},{4,1},{5,0},{6,3},{7,2},{8,13},{9,12},{10,... | collective-permute-start | bytes 884744 | tf_op jit(solution)/shard_map/ppermute | solution.py:29
  6.1 4.0 %shard_map.123 = (bf16[3,1536,768]{2,1,0:T(8,128)(2,1)S(1)}, f32[2,768]{1,0:T(2,128)S(1)}, bf16[256,768]{1,0:T(8,128)(2,1)S(1)}, bf16[256,768]{1,0:T(8,128)(2,1)...) custom-call(bf16[3,1536,768]{2,1,0:T(8,128)(2,1)} %bitcast.9, f32[768]{0:T(1024)} %q_hbm.1, f32[768]{0:T(1024)} %k_hbm.1, ...), custom_call_target="tpu_custom_call" | custom-call | tf_op jit(solution)/shard_map/pallas_call | solution.py:134
  10.1 2.9 %collective-permute-done.4.rows_other = bf16[16,768]{1,0:T(8,128)(2,1)S(1)} collective-permute-done((bf16[16,768]{1,0:T(8,128)(2,1)S(1)}, bf16[16,768]{1,0:T(8,128)(2,1)S(1)}, u32[]{:S(2)}, u32[]{:S(2)}) %collective-permute-start.4) | collective-permute-done | bytes 24608 | tf_op jit(solution)/shard_map/ppermute | solution.py:29
  13.0 6.5 %collective-permute-start.7 = (bf16[256,768]{1,0:T(8,128)(2,1)S(1)}, bf16[256,768]{1,0:T(8,128)(2,1)S(1)}, u32[]{:S(2)}, u32[]{:S(2)}) collective-permute-start(bf16[256,768]{1,0:T(8,128)(2,1)S(1)} %collective-permute-done.5.refs_1_), channel_id=1, source_target_pairs={{0,2},{1,3},{2,4},{3,5},{4,6},{5,7},{6,8},{7,9},{8,10},{9,11},{10,... | collective-permute-start | bytes 1179656 | tf_op jit(solution)/shard_map/ppermute | solution.py:29
  19.5 1.9 %collective-permute-start.6 = (bf16[256,768]{1,0:T(8,128)(2,1)S(1)}, bf16[256,768]{1,0:T(8,128)(2,1)S(1)}, u32[]{:S(2)}, u32[]{:S(2)}) collective-permute-start(bf16[256,768]{1,0:T(8,128)(2,1)S(1)} %copy-done), channel_id=1, source_target_pairs={{0,2},{1,3},{2,4},{3,5},{4,6},{5,7},{6,8},{7,9},{8,10},{9,11},{10,... | collective-permute-start | bytes 1179656 | tf_op jit(solution)/shard_map/ppermute | solution.py:29
  21.4 1.4 %collective-permute-start.1 = (bf16[96,1536]{1,0:T(8,128)(2,1)S(1)}, bf16[96,1536]{1,0:T(8,128)(2,1)S(1)}, u32[]{:S(2)}, u32[]{:S(2)}) collective-permute-start(bf16[96,1536]{1,0:T(8,128)(2,1)S(1)} %collective-permute-done.own), channel_id=1, source_target_pairs={{0,64},{1,65},{2,66},{3,67},{4,68},{5,69},{6,70},{7,71},{8,72},{9,... | collective-permute-start | bytes 884744 | tf_op jit(solution)/shard_map/ppermute | solution.py:29
  23.0 2.3 %shard_map.124 = (bf16[128,768]{1,0:T(8,128)(2,1)S(1)}, bf16[128,768]{1,0:T(8,128)(2,1)S(1)}, bf16[256,768]{1,0:T(8,128)(2,1)S(1)}, bf16[256,768]{1,0:T(8,128)(2,1)S(1)}) custom-call(bf16[16,768]{1,0:T(8,128)(2,1)S(1)} %shard_map.122.rows_mine, bf16[16,768]{1,0:T(8,128)(2,1)S(1)} %collective-permute-done.4.rows_other, ...), custom_call_target="tpu_custom_call" | custom-call | flops 1811939328 | bytes 7919616 | tf_op jit(solution)/shard_map/pallas_call | solution.py:314
  25.3 3.1 %collective-permute-done.6.refs_0_ = bf16[256,768]{1,0:T(8,128)(2,1)S(1)} collective-permute-done((bf16[256,768]{1,0:T(8,128)(2,1)S(1)}, bf16[256,768]{1,0:T(8,128)(2,1)S(1)}, u32[]{:S(2)}, u32[]{:S(2)}) %collective-permute-start.6) | collective-permute-done | bytes 393248 | tf_op jit(solution)/shard_map/ppermute | solution.py:29
  28.4 1.6 %shard_map.125 = (bf16[256,768]{1,0:T(8,128)(2,1)S(1)}, bf16[256,768]{1,0:T(8,128)(2,1)S(1)}) custom-call(bf16[16,768]{1,0:T(8,128)(2,1)S(1)} %shard_map.122.rows_mine, bf16[16,768]{1,0:T(8,128)(2,1)S(1)} %collective-permute-done.4.rows_other, bf16[3,1536,768]{2,1,0:T(8,128)(2,1)S(1)} %get-tuple-element.56.w, f32[2,768]{1,0:T(2,128)S(1)} %get-tuple-element.57.gains, ...), custom_call_target="tpu_custom_call" | custom-call | flops 1207959552 | bytes 7919616 | tf_op jit(solution)/shard_map/pallas_call | solution.py:314
  33.4 6.2 %collective-permute-done.8.a_other = bf16[128,768]{1,0:T(8,128)(2,1)S(1)} collective-permute-done((bf16[128,768]{1,0:T(8,128)(2,1)S(1)}, bf16[128,768]{1,0:T(8,128)(2,1)S(1)}, u32[]{:S(2)}, u32[]{:S(2)}) %collective-permute-start.8) | collective-permute-done | bytes 196640 | tf_op jit(solution)/shard_map/ppermute | solution.py:29
  41.3 1.5 %collective-permute-done.9.others = bf16[4,96,1536]{2,1,0:T(8,128)(2,1)S(1)} collective-permute-done((bf16[4,96,1536]{2,1,0:T(8,128)(2,1)S(1)}, bf16[4,96,1536]{2,1,0:T(8,128)(2,1)S(1)}, u32[]{:S(2)}, u32[]{:S(2)}) %collective-permute-start.9) | collective-permute-done | bytes 1179680 | tf_op jit(solution)/shard_map/ppermute | solution.py:29
  44.4 2.3 %collective-permute-start.10 = (bf16[128,1536]{1,0:T(8,128)(2,1)S(1)}, bf16[128,1536]{1,0:T(8,128)(2,1)S(1)}, u32[]{:S(2)}, u32[]{:S(2)}) collective-permute-start(bf16[128,1536]{1,0:T(8,128)(2,1)S(1)} %shard_map.129.refs_0_), channel_id=1, source_target_pairs={{2,0},{3,1},{4,2},{5,3},{6,4},{7,5},{8,6},{9,7},{10,8},{11,9},{12,... | collective-permute-start | bytes 1179656 | tf_op jit(solution)/shard_map/ppermute | solution.py:29
  49.6 2.9 %collective-permute-start.13 = (bf16[128,1536]{1,0:T(8,128)(2,1)S(1)}, bf16[128,1536]{1,0:T(8,128)(2,1)S(1)}, u32[]{:S(2)}, u32[]{:S(2)}) collective-permute-start(bf16[128,1536]{1,0:T(8,128)(2,1)S(1)} %shard_map.130.refs_1_), channel_id=1, source_target_pairs={{2,0},{3,1},{4,2},{5,3},{6,4},{7,5},{8,6},{9,7},{10,8},{11,9},{12,... | collective-permute-start | bytes 1179656 | tf_op jit(solution)/shard_map/ppermute | solution.py:29
  52.4 3.2 %collective-permute-done.10.refs_2_ = bf16[128,1536]{1,0:T(8,128)(2,1)S(1)} collective-permute-done((bf16[128,1536]{1,0:T(8,128)(2,1)S(1)}, bf16[128,1536]{1,0:T(8,128)(2,1)S(1)}, u32[]{:S(2)}, u32[]{:S(2)}) %collective-permute-start.10) | collective-permute-done | bytes 393248 | tf_op jit(solution)/shard_map/ppermute | solution.py:29
  55.6 1.6 %shard_map.131 = (bf16[256,768]{1,0:T(8,128)(2,1)S(1)}, bf16[256,768]{1,0:T(8,128)(2,1)S(1)}) custom-call(bf16[16,768]{1,0:T(8,128)(2,1)S(1)} %shard_map.122.rows_mine, bf16[16,768]{1,0:T(8,128)(2,1)S(1)} %collective-permute-done.4.rows_other, bf16[3,1536,768]{2,1,0:T(8,128)(2,1)S(1)} %get-tuple-element.56.w, f32[2,768]{1,0:T(2,128)S(1)} %get-tuple-element.57.gains, ...), custom_call_target="tpu_custom_call" | custom-call | flops 1207959552 | bytes 7919616 | tf_op jit(solution)/shard_map/pallas_call | solution.py:314
  57.2 8.1 %collective-permute-done.13.refs_3_ = bf16[128,1536]{1,0:T(8,128)(2,1)S(1)} collective-permute-done((bf16[128,1536]{1,0:T(8,128)(2,1)S(1)}, bf16[128,1536]{1,0:T(8,128)(2,1)S(1)}, u32[]{:S(2)}, u32[]{:S(2)}) %collective-permute-start.13) | collective-permute-done | bytes 393248 | tf_op jit(solution)/shard_map/ppermute | solution.py:29
  65.3 3.5 %shard_map.132 = (bf16[128,768]{1,0:T(8,128)(2,1)S(1)}, bf16[128,768]{1,0:T(8,128)(2,1)S(1)}, bf16[256,768]{1,0:T(8,128)(2,1)S(1)}, bf16[256,768]{1,0:T(8,128)(2,1)S(1)}) custom-call(s32[128]{0:T(128)S(1)} %copy-done.2, bf16[16,768]{1,0:T(8,128)(2,1)S(1)} %shard_map.122.rows_mine, bf16[16,768]{1,0:T(8,128)(2,1)S(1)} %collective-permute-done.4.rows_other, ...), custom_call_target="tpu_custom_call" | custom-call | flops 2013265920 | bytes 9492480 | tf_op jit(solution)/shard_map/pallas_call | solution.py:314
  70.1 3.0 %collective-permute-start.16 = (bf16[128,768]{1,0:T(8,128)(2,1)S(1)}, bf16[128,768]{1,0:T(8,128)(2,1)S(1)}, u32[]{:S(2)}, u32[]{:S(2)}) collective-permute-start(bf16[128,768]{1,0:T(8,128)(2,1)S(1)} %shard_map.133.a_mine), channel_id=1, source_target_pairs={{0,1},{1,0},{2,3},{3,2},{4,5},{5,4},{6,7},{7,6},{8,9},{9,8},{10,11... | collective-permute-start | bytes 589832 | tf_op jit(solution)/shard_map/ppermute | solution.py:29
  73.2 1.7 %collective-permute-done.14.a_other = bf16[128,768]{1,0:T(8,128)(2,1)S(1)} collective-permute-done((bf16[128,768]{1,0:T(8,128)(2,1)S(1)}, bf16[128,768]{1,0:T(8,128)(2,1)S(1)}, u32[]{:S(2)}, u32[]{:S(2)}) %collective-permute-start.14) | collective-permute-done | bytes 196640 | tf_op jit(solution)/shard_map/ppermute | solution.py:29
  76.3 1.9 %collective-permute-start.15 = (bf16[128,1536]{1,0:T(8,128)(2,1)S(1)}, bf16[128,1536]{1,0:T(8,128)(2,1)S(1)}, u32[]{:S(2)}, u32[]{:S(2)}) collective-permute-start(bf16[128,1536]{1,0:T(8,128)(2,1)S(1)} %shard_map.134.refs_0_), channel_id=1, source_target_pairs={{2,0},{3,1},{4,2},{5,3},{6,4},{7,5},{8,6},{9,7},{10,8},{11,9},{12,... | collective-permute-start | bytes 1179656 | tf_op jit(solution)/shard_map/ppermute | solution.py:29
  78.9 1.4 %shard_map.135.refs_1_ = bf16[128,1536]{1,0:T(8,128)(2,1)S(1)} custom-call(s32[128]{0:T(128)S(1)} %copy-done.1, bf16[16,768]{1,0:T(8,128)(2,1)S(1)} %shard_map.122.rows_mine, bf16[16,768]{1,0:T(8,128)(2,1)S(1)} %collective-permute-done.4.rows_other, bf16[768,1536]{1,0:T(8,128)(2,1)S(1)} %get-tuple-element.54.w_mine, ...), custom_call_target="tpu_custom_call" | custom-call | flops 603979776 | bytes 6733824 | tf_op jit(solution)/shard_map/pallas_call | solution.py:314
  80.2 1.9 %collective-permute-start.18 = (bf16[128,1536]{1,0:T(8,128)(2,1)S(1)}, bf16[128,1536]{1,0:T(8,128)(2,1)S(1)}, u32[]{:S(2)}, u32[]{:S(2)}) collective-permute-start(bf16[128,1536]{1,0:T(8,128)(2,1)S(1)} %shard_map.135.refs_1_), channel_id=1, source_target_pairs={{2,0},{3,1},{4,2},{5,3},{6,4},{7,5},{8,6},{9,7},{10,8},{11,9},{12,... | collective-permute-start | bytes 1179656 | tf_op jit(solution)/shard_map/ppermute | solution.py:29
  82.2 5.3 %collective-permute-done.15.refs_2_ = bf16[128,1536]{1,0:T(8,128)(2,1)S(1)} collective-permute-done((bf16[128,1536]{1,0:T(8,128)(2,1)S(1)}, bf16[128,1536]{1,0:T(8,128)(2,1)S(1)}, u32[]{:S(2)}, u32[]{:S(2)}) %collective-permute-start.15) | collective-permute-done | bytes 393248 | tf_op jit(solution)/shard_map/ppermute | solution.py:29
  87.5 1.6 %shard_map.136 = (bf16[256,768]{1,0:T(8,128)(2,1)S(1)}, bf16[256,768]{1,0:T(8,128)(2,1)S(1)}) custom-call(bf16[16,768]{1,0:T(8,128)(2,1)S(1)} %shard_map.122.rows_mine, bf16[16,768]{1,0:T(8,128)(2,1)S(1)} %collective-permute-done.4.rows_other, bf16[3,1536,768]{2,1,0:T(8,128)(2,1)S(1)} %get-tuple-element.56.w, f32[2,768]{1,0:T(2,128)S(1)} %get-tuple-element.57.gains, ...), custom_call_target="tpu_custom_call" | custom-call | flops 1207959552 | bytes 7919616 | tf_op jit(solution)/shard_map/pallas_call | solution.py:314
  89.0 2.7 %collective-permute-done.18.refs_3_ = bf16[128,1536]{1,0:T(8,128)(2,1)S(1)} collective-permute-done((bf16[128,1536]{1,0:T(8,128)(2,1)S(1)}, bf16[128,1536]{1,0:T(8,128)(2,1)S(1)}, u32[]{:S(2)}, u32[]{:S(2)}) %collective-permute-start.18) | collective-permute-done | bytes 393248 | tf_op jit(solution)/shard_map/ppermute | solution.py:29
  91.8 3.5 %shard_map.137 = (bf16[128,768]{1,0:T(8,128)(2,1)S(1)}, bf16[128,768]{1,0:T(8,128)(2,1)S(1)}, bf16[256,768]{1,0:T(8,128)(2,1)S(1)}, bf16[256,768]{1,0:T(8,128)(2,1)S(1)}) custom-call(s32[128]{0:T(128)S(1)} %copy-done.2, bf16[16,768]{1,0:T(8,128)(2,1)S(1)} %shard_map.122.rows_mine, bf16[16,768]{1,0:T(8,128)(2,1)S(1)} %collective-permute-done.4.rows_other, ...), custom_call_target="tpu_custom_call" | custom-call | flops 2013265920 | bytes 9492480 | tf_op jit(solution)/shard_map/pallas_call | solution.py:314
  96.6 3.0 %collective-permute-start.21 = (bf16[128,768]{1,0:T(8,128)(2,1)S(1)}, bf16[128,768]{1,0:T(8,128)(2,1)S(1)}, u32[]{:S(2)}, u32[]{:S(2)}) collective-permute-start(bf16[128,768]{1,0:T(8,128)(2,1)S(1)} %shard_map.138.a_mine), channel_id=1, source_target_pairs={{0,1},{1,0},{2,3},{3,2},{4,5},{5,4},{6,7},{7,6},{8,9},{9,8},{10,11... | collective-permute-start | bytes 589832 | tf_op jit(solution)/shard_map/ppermute | solution.py:29
  99.6 1.7 %collective-permute-done.19.a_other = bf16[128,768]{1,0:T(8,128)(2,1)S(1)} collective-permute-done((bf16[128,768]{1,0:T(8,128)(2,1)S(1)}, bf16[128,768]{1,0:T(8,128)(2,1)S(1)}, u32[]{:S(2)}, u32[]{:S(2)}) %collective-permute-start.19) | collective-permute-done | bytes 196640 | tf_op jit(solution)/shard_map/ppermute | solution.py:29
  102.4 1.9 %collective-permute-start.20 = (bf16[128,768]{1,0:T(8,128)(2,1)S(1)}, bf16[128,768]{1,0:T(8,128)(2,1)S(1)}, u32[]{:S(2)}, u32[]{:S(2)}) collective-permute-start(bf16[128,768]{1,0:T(8,128)(2,1)S(1)} %get-tuple-element.99), channel_id=1, source_target_pairs={{2,0},{3,1},{4,2},{5,3},{6,4},{7,5},{8,6},{9,7},{10,8},{11,9},{12,... | collective-permute-start | bytes 589832 | tf_op jit(solution)/shard_map/ppermute | solution.py:29
  105.4 1.9 %collective-permute-start.22 = (bf16[128,768]{1,0:T(8,128)(2,1)S(1)}, bf16[128,768]{1,0:T(8,128)(2,1)S(1)}, u32[]{:S(2)}, u32[]{:S(2)}) collective-permute-start(bf16[128,768]{1,0:T(8,128)(2,1)S(1)} %get-tuple-element.102), channel_id=1, source_target_pairs={{2,0},{3,1},{4,2},{5,3},{6,4},{7,5},{8,6},{9,7},{10,8},{11,9},{12,... | collective-permute-start | bytes 589832 | tf_op jit(solution)/shard_map/ppermute | solution.py:29
  107.3 4.2 %collective-permute-done.20.advanced = bf16[128,768]{1,0:T(8,128)(2,1)S(1)} collective-permute-done((bf16[128,768]{1,0:T(8,128)(2,1)S(1)}, bf16[128,768]{1,0:T(8,128)(2,1)S(1)}, u32[]{:S(2)}, u32[]{:S(2)}) %collective-permute-start.20) | collective-permute-done | bytes 196640 | tf_op jit(solution)/shard_map/ppermute | solution.py:29
  111.5 4.3 %collective-permute-done.22.advanced = bf16[128,768]{1,0:T(8,128)(2,1)S(1)} collective-permute-done((bf16[128,768]{1,0:T(8,128)(2,1)S(1)}, bf16[128,768]{1,0:T(8,128)(2,1)S(1)}, u32[]{:S(2)}, u32[]{:S(2)}) %collective-permute-start.22) | collective-permute-done | bytes 196640 | tf_op jit(solution)/shard_map/ppermute | solution.py:29
  (43 shorter events, 20.9 us)
Async XLA Ops:
  0.6 12.4 %collective-permute-start.5 = (bf16[256,768]{1,0:T(8,128)(2,1)}, bf16[256,768]{1,0:T(8,128)(2,1)S(1)}, u32[]{:S(2)}, u32[]{:S(2)}) collective-permute-start(bf16[256,768]{1,0:T(8,128)(2,1)} %refs_0_.5), channel_id=1, source_target_pairs={{0,1},{1,0},{2,3},{3,2},{4,5},{5,4},{6,7},{7,6},{8,9},{9,8},{10,11... | collective-permute-start | bytes 1179656 | tf_op jit(solution)/shard_map/ppermute | solution.py:29
  4.0 17.4 %collective-permute-start = (bf16[96,1536]{1,0:T(8,128)(2,1)S(1)}, bf16[96,1536]{1,0:T(8,128)(2,1)S(1)}, u32[]{:S(2)}, u32[]{:S(2)}) collective-permute-start(bf16[96,1536]{1,0:T(8,128)(2,1)S(1)} %constant_dynamic-slice_fusion), channel_id=1, source_target_pairs={{0,5},{1,4},{2,7},{3,6},{4,1},{5,0},{6,3},{7,2},{8,13},{9,12},{10,... | collective-permute-start | bytes 884744 | tf_op jit(solution)/shard_map/ppermute | solution.py:29
  5.9 7.0 %collective-permute-start.4 = (bf16[16,768]{1,0:T(8,128)(2,1)S(1)}, bf16[16,768]{1,0:T(8,128)(2,1)S(1)}, u32[]{:S(2)}, u32[]{:S(2)}) collective-permute-start(bf16[16,768]{1,0:T(8,128)(2,1)S(1)} %shard_map.122.rows_mine), channel_id=1, source_target_pairs={{0,1},{1,0},{2,3},{3,2},{4,5},{5,4},{6,7},{7,6},{8,9},{9,8},{10,11... | collective-permute-start | bytes 73736 | tf_op jit(solution)/shard_map/ppermute | solution.py:29
  6.1 13.4 %copy-start = (bf16[256,768]{1,0:T(8,128)(2,1)S(1)}, bf16[256,768]{1,0:T(8,128)(2,1)}, u32[]{:S(2)}) copy-start(bf16[256,768]{1,0:T(8,128)(2,1)} %refs_0_.5) | copy-start | bytes 1179652
  13.0 12.3 %collective-permute-start.7 = (bf16[256,768]{1,0:T(8,128)(2,1)S(1)}, bf16[256,768]{1,0:T(8,128)(2,1)S(1)}, u32[]{:S(2)}, u32[]{:S(2)}) collective-permute-start(bf16[256,768]{1,0:T(8,128)(2,1)S(1)} %collective-permute-done.5.refs_1_), channel_id=1, source_target_pairs={{0,2},{1,3},{2,4},{3,5},{4,6},{5,7},{6,8},{7,9},{8,10},{9,11},{10,... | collective-permute-start | bytes 1179656 | tf_op jit(solution)/shard_map/ppermute | solution.py:29
  19.5 8.9 %collective-permute-start.6 = (bf16[256,768]{1,0:T(8,128)(2,1)S(1)}, bf16[256,768]{1,0:T(8,128)(2,1)S(1)}, u32[]{:S(2)}, u32[]{:S(2)}) collective-permute-start(bf16[256,768]{1,0:T(8,128)(2,1)S(1)} %copy-done), channel_id=1, source_target_pairs={{0,2},{1,3},{2,4},{3,5},{4,6},{5,7},{6,8},{7,9},{8,10},{9,11},{10,... | collective-permute-start | bytes 1179656 | tf_op jit(solution)/shard_map/ppermute | solution.py:29
  21.4 18.2 %collective-permute-start.1 = (bf16[96,1536]{1,0:T(8,128)(2,1)S(1)}, bf16[96,1536]{1,0:T(8,128)(2,1)S(1)}, u32[]{:S(2)}, u32[]{:S(2)}) collective-permute-start(bf16[96,1536]{1,0:T(8,128)(2,1)S(1)} %collective-permute-done.own), channel_id=1, source_target_pairs={{0,64},{1,65},{2,66},{3,67},{4,68},{5,69},{6,70},{7,71},{8,72},{9,... | collective-permute-start | bytes 884744 | tf_op jit(solution)/shard_map/ppermute | solution.py:29
  22.8 16.9 %collective-permute-start.2 = (bf16[96,1536]{1,0:T(8,128)(2,1)S(1)}, bf16[96,1536]{1,0:T(8,128)(2,1)S(1)}, u32[]{:S(2)}, u32[]{:S(2)}) collective-permute-start(bf16[96,1536]{1,0:T(8,128)(2,1)S(1)} %collective-permute-done.own), channel_id=1, source_target_pairs={{0,192},{1,193},{2,194},{3,195},{4,196},{5,197},{6,198},{7,199},{8... | collective-permute-start | bytes 884744 | tf_op jit(solution)/shard_map/ppermute | solution.py:29
  23.0 16.7 %collective-permute-start.3 = (bf16[96,1536]{1,0:T(8,128)(2,1)S(1)}, bf16[96,1536]{1,0:T(8,128)(2,1)S(1)}, u32[]{:S(2)}, u32[]{:S(2)}) collective-permute-start(bf16[96,1536]{1,0:T(8,128)(2,1)S(1)} %collective-permute-done.own), channel_id=1, source_target_pairs={{0,56},{1,57},{2,58},{3,59},{4,60},{5,61},{6,62},{7,63},{8,0},{9,1... | collective-permute-start | bytes 884744 | tf_op jit(solution)/shard_map/ppermute | solution.py:29
  25.3 4.8 %copy-start.2 = (s32[128]{0:T(128)S(1)}, s32[128]{0:T(128)}, u32[]{:S(2)}) copy-start(s32[128]{0:T(128)} %starts.11) | copy-start | bytes 1540
  31.3 8.4 %collective-permute-start.8 = (bf16[128,768]{1,0:T(8,128)(2,1)S(1)}, bf16[128,768]{1,0:T(8,128)(2,1)S(1)}, u32[]{:S(2)}, u32[]{:S(2)}) collective-permute-start(bf16[128,768]{1,0:T(8,128)(2,1)S(1)} %shard_map.126.a_mine), channel_id=1, source_target_pairs={{0,1},{1,0},{2,3},{3,2},{4,5},{5,4},{6,7},{7,6},{8,9},{9,8},{10,11... | collective-permute-start | bytes 589832 | tf_op jit(solution)/shard_map/ppermute | solution.py:29
  39.9 3.2 %copy-start.1 = (s32[128]{0:T(128)S(1)}, s32[128]{0:T(128)}, u32[]{:S(2)}) copy-start(s32[128]{0:T(128)} %levels.11) | copy-start | bytes 1540
  39.9 3.0 %collective-permute-start.9 = (bf16[4,96,1536]{2,1,0:T(8,128)(2,1)S(1)}, bf16[4,96,1536]{2,1,0:T(8,128)(2,1)S(1)}, u32[]{:S(2)}, u32[]{:S(2)}) collective-permute-start(bf16[4,96,1536]{2,1,0:T(8,128)(2,1)S(1)} %pad_maximum_fusion), channel_id=1, source_target_pairs={{0,2},{1,3},{2,0},{3,1},{4,6},{5,7},{6,4},{7,5},{8,10},{9,11},{10,... | collective-permute-start | bytes 3538952 | tf_op jit(solution)/shard_map/ppermute | solution.py:29
  40.4 7.9 %collective-permute-start.11 = (bf16[128,768]{1,0:T(8,128)(2,1)S(1)}, bf16[128,768]{1,0:T(8,128)(2,1)S(1)}, u32[]{:S(2)}, u32[]{:S(2)}) collective-permute-start(bf16[128,768]{1,0:T(8,128)(2,1)S(1)} %shard_map.127.a_mine), channel_id=1, source_target_pairs={{0,1},{1,0},{2,3},{3,2},{4,5},{5,4},{6,7},{7,6},{8,9},{9,8},{10,11... | collective-permute-start | bytes 589832 | tf_op jit(solution)/shard_map/ppermute | solution.py:29
  44.4 11.2 %collective-permute-start.10 = (bf16[128,1536]{1,0:T(8,128)(2,1)S(1)}, bf16[128,1536]{1,0:T(8,128)(2,1)S(1)}, u32[]{:S(2)}, u32[]{:S(2)}) collective-permute-start(bf16[128,1536]{1,0:T(8,128)(2,1)S(1)} %shard_map.129.refs_0_), channel_id=1, source_target_pairs={{2,0},{3,1},{4,2},{5,3},{6,4},{7,5},{8,6},{9,7},{10,8},{11,9},{12,... | collective-permute-start | bytes 1179656 | tf_op jit(solution)/shard_map/ppermute | solution.py:29
  46.7 10.5 %collective-permute-start.12 = (bf16[256,768]{1,0:T(8,128)(2,1)S(1)}, bf16[256,768]{1,0:T(8,128)(2,1)S(1)}, u32[]{:S(2)}, u32[]{:S(2)}) collective-permute-start(bf16[256,768]{1,0:T(8,128)(2,1)S(1)} %get-tuple-element.79.refs_0_), channel_id=1, source_target_pairs={{250,255},{251,254}} | collective-permute-start | bytes 1179656 | tf_op jit(solution)/shard_map/ppermute | solution.py:29
  49.6 15.7 %collective-permute-start.13 = (bf16[128,1536]{1,0:T(8,128)(2,1)S(1)}, bf16[128,1536]{1,0:T(8,128)(2,1)S(1)}, u32[]{:S(2)}, u32[]{:S(2)}) collective-permute-start(bf16[128,1536]{1,0:T(8,128)(2,1)S(1)} %shard_map.130.refs_1_), channel_id=1, source_target_pairs={{2,0},{3,1},{4,2},{5,3},{6,4},{7,5},{8,6},{9,7},{10,8},{11,9},{12,... | collective-permute-start | bytes 1179656 | tf_op jit(solution)/shard_map/ppermute | solution.py:29
  68.8 6.1 %collective-permute-start.14 = (bf16[128,768]{1,0:T(8,128)(2,1)S(1)}, bf16[128,768]{1,0:T(8,128)(2,1)S(1)}, u32[]{:S(2)}, u32[]{:S(2)}) collective-permute-start(bf16[128,768]{1,0:T(8,128)(2,1)S(1)} %get-tuple-element.80.a_mine), channel_id=1, source_target_pairs={{0,1},{1,0},{2,3},{3,2},{4,5},{5,4},{6,7},{7,6},{8,9},{9,8},{10,11... | collective-permute-start | bytes 589832 | tf_op jit(solution)/shard_map/ppermute | solution.py:29
  70.1 8.8 %collective-permute-start.16 = (bf16[128,768]{1,0:T(8,128)(2,1)S(1)}, bf16[128,768]{1,0:T(8,128)(2,1)S(1)}, u32[]{:S(2)}, u32[]{:S(2)}) collective-permute-start(bf16[128,768]{1,0:T(8,128)(2,1)S(1)} %shard_map.133.a_mine), channel_id=1, source_target_pairs={{0,1},{1,0},{2,3},{3,2},{4,5},{5,4},{6,7},{7,6},{8,9},{9,8},{10,11... | collective-permute-start | bytes 589832 | tf_op jit(solution)/shard_map/ppermute | solution.py:29
  76.3 11.2 %collective-permute-start.15 = (bf16[128,1536]{1,0:T(8,128)(2,1)S(1)}, bf16[128,1536]{1,0:T(8,128)(2,1)S(1)}, u32[]{:S(2)}, u32[]{:S(2)}) collective-permute-start(bf16[128,1536]{1,0:T(8,128)(2,1)S(1)} %shard_map.134.refs_0_), channel_id=1, source_target_pairs={{2,0},{3,1},{4,2},{5,3},{6,4},{7,5},{8,6},{9,7},{10,8},{11,9},{12,... | collective-permute-start | bytes 1179656 | tf_op jit(solution)/shard_map/ppermute | solution.py:29
  78.2 10.9 %collective-permute-start.17 = (bf16[256,768]{1,0:T(8,128)(2,1)S(1)}, bf16[256,768]{1,0:T(8,128)(2,1)S(1)}, u32[]{:S(2)}, u32[]{:S(2)}) collective-permute-start(bf16[256,768]{1,0:T(8,128)(2,1)S(1)} %get-tuple-element.92.refs_0_), channel_id=1, source_target_pairs={{250,255},{251,254}} | collective-permute-start | bytes 1179656 | tf_op jit(solution)/shard_map/ppermute | solution.py:29
  80.2 11.5 %collective-permute-start.18 = (bf16[128,1536]{1,0:T(8,128)(2,1)S(1)}, bf16[128,1536]{1,0:T(8,128)(2,1)S(1)}, u32[]{:S(2)}, u32[]{:S(2)}) collective-permute-start(bf16[128,1536]{1,0:T(8,128)(2,1)S(1)} %shard_map.135.refs_1_), channel_id=1, source_target_pairs={{2,0},{3,1},{4,2},{5,3},{6,4},{7,5},{8,6},{9,7},{10,8},{11,9},{12,... | collective-permute-start | bytes 1179656 | tf_op jit(solution)/shard_map/ppermute | solution.py:29
  95.3 6.1 %collective-permute-start.19 = (bf16[128,768]{1,0:T(8,128)(2,1)S(1)}, bf16[128,768]{1,0:T(8,128)(2,1)S(1)}, u32[]{:S(2)}, u32[]{:S(2)}) collective-permute-start(bf16[128,768]{1,0:T(8,128)(2,1)S(1)} %get-tuple-element.93.a_mine), channel_id=1, source_target_pairs={{0,1},{1,0},{2,3},{3,2},{4,5},{5,4},{6,7},{7,6},{8,9},{9,8},{10,11... | collective-permute-start | bytes 589832 | tf_op jit(solution)/shard_map/ppermute | solution.py:29
  96.6 7.7 %collective-permute-start.21 = (bf16[128,768]{1,0:T(8,128)(2,1)S(1)}, bf16[128,768]{1,0:T(8,128)(2,1)S(1)}, u32[]{:S(2)}, u32[]{:S(2)}) collective-permute-start(bf16[128,768]{1,0:T(8,128)(2,1)S(1)} %shard_map.138.a_mine), channel_id=1, source_target_pairs={{0,1},{1,0},{2,3},{3,2},{4,5},{5,4},{6,7},{7,6},{8,9},{9,8},{10,11... | collective-permute-start | bytes 589832 | tf_op jit(solution)/shard_map/ppermute | solution.py:29
  102.4 9.1 %collective-permute-start.20 = (bf16[128,768]{1,0:T(8,128)(2,1)S(1)}, bf16[128,768]{1,0:T(8,128)(2,1)S(1)}, u32[]{:S(2)}, u32[]{:S(2)}) collective-permute-start(bf16[128,768]{1,0:T(8,128)(2,1)S(1)} %get-tuple-element.99), channel_id=1, source_target_pairs={{2,0},{3,1},{4,2},{5,3},{6,4},{7,5},{8,6},{9,7},{10,8},{11,9},{12,... | collective-permute-start | bytes 589832 | tf_op jit(solution)/shard_map/ppermute | solution.py:29
  105.4 10.4 %collective-permute-start.22 = (bf16[128,768]{1,0:T(8,128)(2,1)S(1)}, bf16[128,768]{1,0:T(8,128)(2,1)S(1)}, u32[]{:S(2)}, u32[]{:S(2)}) collective-permute-start(bf16[128,768]{1,0:T(8,128)(2,1)S(1)} %get-tuple-element.102), channel_id=1, source_target_pairs={{2,0},{3,1},{4,2},{5,3},{6,4},{7,5},{8,6},{9,7},{10,8},{11,9},{12,... | collective-permute-start | bytes 589832 | tf_op jit(solution)/shard_map/ppermute | solution.py:29

commit v5 on v4

--- a/solution.py
+++ b/solution.py
@@ -62,7 +62,7 @@
     return ordered(mine, other)
 
 
-def halves_of(kind, refs, step, row, count):
+def halves_of(kind, refs, row, count):
     if kind == "pair":
         return ordered(refs[0][row : row + count, :], refs[1][row : row + count, :])
     chunks = refs if kind == "chunks" else refs[2:]
@@ -154,7 +154,7 @@
     x, (keys, values) = refs[:-2], refs[-2:]
     width = w.shape[2]
     table = (rows_mine, rows_other)
-    low, high = halves_of(kind, x, None, 0, keys.shape[0])
+    low, high = halves_of(kind, x, 0, keys.shape[0])
     moved = modulated(low, high, table_row(table, NEAR_SHIFT), table_row(table, NEAR_SCALE))
     raw = dot(moved, w[1])
     gain = gains[1:2, :]
@@ -186,48 +186,57 @@
         attended[:, part] = (out / total).astype(jnp.bfloat16)
 
 
-def own_kernel(kind, step, count, starts, rows_mine, rows_other, w, gains, near_keys, near_values, *refs):
-    x, (attended, queries, keys, values) = refs[:-4], refs[-4:]
-    rows = keys.shape[0]
+def projected(low, high, table, w, gains):
     width = w.shape[2]
-    first = attended.shape[0]
-    table = (rows_mine, rows_other)
-    low, high = halves_of(kind, x, step, 0, rows)
     moved = modulated(low, high, table_row(table, SHIFT), table_row(table, SCALE))
     query_raw = dot(moved, w[0])
     key_raw = dot(moved, w[1])
-    value = dot(moved, w[2]).astype(jnp.bfloat16)
+    values = dot(moved, w[2]).astype(jnp.bfloat16)
+    parts = [slice(a, a + HD) for a in range(0, width, HD)]
+    queries = [normed(query_raw[:, part], gains[0:1, part]) for part in parts]
+    keys = [normed(key_raw[:, part], gains[1:2, part]) for part in parts]
+    return queries, keys, values
+
+
+def head_kernel(rows_mine, rows_other, w, gains, fresh, fresh_other, chunk, queries, keys, values):
+    low, high = halves_of("fresh", (fresh, fresh_other, chunk), 0, chunk.shape[0])
+    heads, key_heads, value = projected(low, high, (rows_mine, rows_other), w, gains)
     values[...] = value
-    q_row, k_row = gains[0:1, :], gains[1:2, :]
-    query_heads, key_heads = [], []
-    for a in range(0, width, HD):
-        part = slice(a, a + HD)
-        query = normed(query_raw[:, part], q_row[:, part])
-        key = normed(key_raw[:, part], k_row[:, part])
-        queries[:, part] = query[first:]
-        keys[:, part] = key
-        query_heads.append(query[:first])
-        key_heads.append(key)
-    attend(starts, attended, query_heads, key_heads, value, near_keys, near_values)
-
-
-def qkv_kernel(kind, rows_mine, rows_other, w, gains, *refs):
-    x, (*queries, keys, values) = refs[:2], refs[2:]
-    rows = keys.shape[0]
-    width = w.shape[2]
-    table = (rows_mine, rows_other)
-    low, high = halves_of(kind, x, None, 0, rows)
-    moved = modulated(low, high, table_row(table, SHIFT), table_row(table, SCALE))
-    query_raw = dot(moved, w[0])
-    key_raw = dot(moved, w[1])
-    values[...] = dot(moved, w[2]).astype(jnp.bfloat16)
-    q_row, k_row = gains[0:1, :], gains[1:2, :]
-    for a in range(0, width, HD):
-        part = slice(a, a + HD)
-        query = normed(query_raw[:, part], q_row[:, part])
-        keys[:, part] = normed(key_raw[:, part], k_row[:, part])
-        for n, chunk in enumerate(queries):
-            chunk[:, part] = query[n * chunk.shape[0] : (n + 1) * chunk.shape[0]]
+    for n in range(len(heads)):
+        queries[:, n * HD : (n + 1) * HD] = heads[n]
+        keys[:, n * HD : (n + 1) * HD] = key_heads[n]
+
+
+def own_kernel(
+    starts, rows_mine, rows_other, w, gains, near_keys, near_values, first_queries, first_keys, first_values,
+    fresh, fresh_other, first, rest, attended, queries, keys, values,
+):
+    count = rest.shape[0]
+    low, high = halves_of("fresh", (fresh, fresh_other, first, rest), count, count)
+    heads, key_heads, value = projected(low, high, (rows_mine, rows_other), w, gains)
+    values[:count, :] = first_values[...]
+    values[count:, :] = value
+    keys[:count, :] = first_keys[...]
+    first_heads, all_keys = [], []
+    for n in range(len(heads)):
+        part = slice(n * HD, (n + 1) * HD)
+        queries[:, part] = heads[n]
+        keys[count:, part] = key_heads[n]
+        first_heads.append(first_queries[:, part])
+        all_keys.append(keys[:, part])
+    attend(starts, attended, first_heads, all_keys, values, near_keys, near_values)
+
+
+def qkv_kernel(rows_mine, rows_other, w, gains, mine, other, *refs):
+    *queries, keys, values = refs
+    low, high = halves_of("pair", (mine, other), 0, keys.shape[0])
+    heads, key_heads, value = projected(low, high, (rows_mine, rows_other), w, gains)
+    values[...] = value
+    for n in range(len(heads)):
+        part = slice(n * HD, (n + 1) * HD)
+        keys[:, part] = key_heads[n]
+        for c, chunk in enumerate(queries):
+            chunk[:, part] = heads[n][c * chunk.shape[0] : (c + 1) * chunk.shape[0]]
 
 
 def rest_kernel(starts, queries, keys, values, near_keys, near_values, attended):
@@ -246,12 +255,12 @@
     return t_next - t_cur
 
 
-def project_kernel(kind, step, row, levels, rows_mine, rows_other, w_mine, w_other, a_mine, a_other, *refs):
+def project_kernel(kind, row, levels, rows_mine, rows_other, w_mine, w_other, a_mine, a_other, *refs):
     x, new = refs[:-1], refs[-1]
     count = new.shape[0]
     width = new.shape[1] // 2
     gate = table_row((rows_mine, rows_other), GATE)
-    halves = halves_of(kind, x, step - 1, row, count)
+    halves = halves_of(kind, x, row, count)
     product = dot(a_mine[...], w_mine[...]) + dot(a_other[...], w_other[...])
     for n in range(2):
         part = slice(n * width, (n + 1) * width)
@@ -260,12 +269,12 @@
         new[:, part] = value
 
 
-def final_kernel(kind, step, row, levels, rows_mine, w_mine, w_other, a_mine, a_other, *refs):
+def final_kernel(kind, row, levels, rows_mine, w_mine, w_other, a_mine, a_other, *refs):
     x, (new, velocity_out) = refs[:-2], refs[-2:]
     count, width = new.shape
     half = lax.axis_index("heads")
     part = pl.ds(pl.multiple_of(half * width, HD), width)
-    low, high = halves_of(kind, x, step - 1, row, count)
+    low, high = halves_of(kind, x, row, count)
     held = jnp.where(half == 0, low, high).astype(jnp.float32)
     product = dot(a_mine[...], w_mine[:, part]) + dot(a_other[...], w_other[:, part])
     velocity = rows_mine[GATE : GATE + 1, :].astype(jnp.float32) * product
@@ -389,7 +398,7 @@
     kind, state = "pair", (frames, other)
     near_kind, near = "pair", (near_mine, near_other)
     *queries, keys, values = kernel_call(
-        functools.partial(qkv_kernel, kind),
+        qkv_kernel,
         ((count, width),) * CHUNKS + ((rows, width),) * 2,
         (),
         (*table, w, gains, *state),
@@ -404,17 +413,19 @@
             (*table, w, gains, *near),
             2 * group_products,
         )
-        if step < STEPS - 1:
-            fresh_other = routed(
-                after(fresh[step], near_keys), lambda q, h: (last, 1 - h) if q == last - 2 else None
-            )
         parts = []
         if step > 0:
+            head = kernel_call(
+                head_kernel,
+                ((count, width),) * 3,
+                (),
+                (*table, w, gains, *state[:3]),
+            )
             first, *queries, keys, values = kernel_call(
-                functools.partial(own_kernel, kind, step - 1, count),
+                own_kernel,
                 ((count, width), (rows - count, width), (rows, width), (rows, width)),
                 (window_start,),
-                (*table, w, gains, near_keys, near_values, *state),
+                (*table, w, gains, near_keys, near_values, *head, *state),
                 3 * group_products + attention_products,
                 attention_products // HD,
             )
@@ -430,14 +441,20 @@
             )
             parts.append(rest)
         received = [swap(part) for part in parts]
-        received[0] = after(received[0], parts[1])
+        waits = []
+        if step < STEPS - 1:
+            fresh_other = routed(
+                after(fresh[step], near_keys), lambda q, h: (last, 1 - h) if q == last - 2 else None
+            )
+            waits = [fresh_other]
+        received[0] = after(received[0], parts[1], *waits)
         if step == 0:
-            w_other = other_projection(piece, received[0], w_out.shape)
+            w_other = other_projection(piece, parts[1], w_out.shape)
         if step < STEPS - 1:
             new = []
             for n in range(CHUNKS):
                 block = kernel_call(
-                    functools.partial(project_kernel, kind, step, n * count),
+                    functools.partial(project_kernel, kind, n * count),
                     (count, 2 * width),
                     (level_index,),
                     (*table, w_out, w_other, parts[n], after(received[n], *new), *state),
@@ -451,7 +468,7 @@
             done = []
             for n in range(CHUNKS):
                 pair = kernel_call(
-                    functools.partial(final_kernel, kind, step, n * count),
+                    functools.partial(final_kernel, kind, n * count),
                     ((count, width), (count, width)),
                     (level_index,),
                     (rows_mine, w_out, w_other, parts[n], after(received[n], *(p[0] for p in done)), *state),

time: 117 us -> 115 us (0.983)
  the two profiles are of different devices: /device:TPU:111 before, /device:TPU:12 now
where the time goes in v5:
time: 115 us; the launch traced here: 114 us
  starting transfers between devices  50.5 us (44%)
  Pallas kernels  33.4 us (29%)
  waiting for transfers between devices  27.8 us (24%)
    ppermute x23, starting transfers between devices, routed(): return lax.ppermute(block, AXES, pairs)  50.5 us
    pallas_call x21, Pallas kernels, kernel_call(): pl.pallas_call(kernel, cost_estimate=pl.CostEstimate(flops=2 * products,...  28.1 us
    ppermute x23, waiting for transfers between devices, routed(): return lax.ppermute(block, AXES, pairs)  27.8 us
    pallas_call x1, Pallas kernels, stage_call(): pl.pallas_call(stage_kernel, out_shape=(pltpu.VMEM(w.shape, w.dtype), plt...  4.05 us
  transfers between devices with their start and end apart: 23, of which 12 were waited for; matrix products, arithmetic and copies ran while one was open for 1% of the time, Pallas kernels for 26%

profile of v5, /device:TPU:12, one launch (start us, length us, event | category | flops | bytes accessed | tf_op | source)
XLA Modules:
  0.0 113.9 jit_solution(6681868981261596618)
XLA Ops:
  3.4 2.2 %collective-permute-start = (bf16[96,1536]{1,0:T(8,128)(2,1)S(1)}, bf16[96,1536]{1,0:T(8,128)(2,1)S(1)}, u32[]{:S(2)}, u32[]{:S(2)}) collective-permute-start(bf16[96,1536]{1,0:T(8,128)(2,1)S(1)} %constant_dynamic-slice_fusion), channel_id=1, source_target_pairs={{0,5},{1,4},{2,7},{3,6},{4,1},{5,0},{6,3},{7,2},{8,13},{9,12},{10,... | collective-permute-start | bytes 884744 | tf_op jit(solution)/shard_map/ppermute | solution.py:29
  5.7 2.0 %collective-permute-start.4 = (bf16[16,768]{1,0:T(8,128)(2,1)S(1)}, bf16[16,768]{1,0:T(8,128)(2,1)S(1)}, u32[]{:S(2)}, u32[]{:S(2)}) collective-permute-start(bf16[16,768]{1,0:T(8,128)(2,1)S(1)} %shard_map.122.rows_mine), channel_id=1, source_target_pairs={{0,1},{1,0},{2,3},{3,2},{4,5},{5,4},{6,7},{7,6},{8,9},{9,8},{10,11... | collective-permute-start | bytes 73736 | tf_op jit(solution)/shard_map/ppermute | solution.py:29
  7.7 4.0 %shard_map.123 = (bf16[3,1536,768]{2,1,0:T(8,128)(2,1)S(1)}, f32[2,768]{1,0:T(2,128)S(1)}, bf16[256,768]{1,0:T(8,128)(2,1)S(1)}, bf16[256,768]{1,0:T(8,128)(2,1)...) custom-call(bf16[3,1536,768]{2,1,0:T(8,128)(2,1)} %bitcast.9, f32[768]{0:T(1024)} %q_hbm.1, f32[768]{0:T(1024)} %k_hbm.1, ...), custom_call_target="tpu_custom_call" | custom-call | tf_op jit(solution)/shard_map/pallas_call | solution.py:134
  11.7 2.2 %collective-permute-done.4.rows_other = bf16[16,768]{1,0:T(8,128)(2,1)S(1)} collective-permute-done((bf16[16,768]{1,0:T(8,128)(2,1)S(1)}, bf16[16,768]{1,0:T(8,128)(2,1)S(1)}, u32[]{:S(2)}, u32[]{:S(2)}) %collective-permute-start.4) | collective-permute-done | bytes 24608 | tf_op jit(solution)/shard_map/ppermute | solution.py:29
  13.9 1.9 %collective-permute-start.7 = (bf16[256,768]{1,0:T(8,128)(2,1)S(1)}, bf16[256,768]{1,0:T(8,128)(2,1)S(1)}, u32[]{:S(2)}, u32[]{:S(2)}) collective-permute-start(bf16[256,768]{1,0:T(8,128)(2,1)S(1)} %collective-permute-done.5.other.refs_1_), channel_id=1, source_target_pairs={{0,2},{1,3},{2,4},{3,5},{4,6},{5,7},{6,8},{7,9},{8,10},{9,11},{10,... | collective-permute-start | bytes 1179656 | tf_op jit(solution)/shard_map/ppermute | solution.py:29
  15.8 3.2 %collective-permute-start.6 = (bf16[256,768]{1,0:T(8,128)(2,1)S(1)}, bf16[256,768]{1,0:T(8,128)(2,1)S(1)}, u32[]{:S(2)}, u32[]{:S(2)}) collective-permute-start(bf16[256,768]{1,0:T(8,128)(2,1)S(1)} %copy-done), channel_id=1, source_target_pairs={{0,2},{1,3},{2,4},{3,5},{4,6},{5,7},{6,8},{7,9},{8,10},{9,11},{10,... | collective-permute-start | bytes 1179656 | tf_op jit(solution)/shard_map/ppermute | solution.py:29
  20.1 1.6 %collective-permute-start.1 = (bf16[96,1536]{1,0:T(8,128)(2,1)S(1)}, bf16[96,1536]{1,0:T(8,128)(2,1)S(1)}, u32[]{:S(2)}, u32[]{:S(2)}) collective-permute-start(bf16[96,1536]{1,0:T(8,128)(2,1)S(1)} %collective-permute-done.own), channel_id=1, source_target_pairs={{0,64},{1,65},{2,66},{3,67},{4,68},{5,69},{6,70},{7,71},{8,72},{9,... | collective-permute-start | bytes 884744 | tf_op jit(solution)/shard_map/ppermute | solution.py:29
  22.2 5.9 %collective-permute-start.3 = (bf16[96,1536]{1,0:T(8,128)(2,1)S(1)}, bf16[96,1536]{1,0:T(8,128)(2,1)S(1)}, u32[]{:S(2)}, u32[]{:S(2)}) collective-permute-start(bf16[96,1536]{1,0:T(8,128)(2,1)S(1)} %collective-permute-done.own), channel_id=1, source_target_pairs={{0,56},{1,57},{2,58},{3,59},{4,60},{5,61},{6,62},{7,63},{8,0},{9,1... | collective-permute-start | bytes 884744 | tf_op jit(solution)/shard_map/ppermute | solution.py:29
  28.0 2.3 %shard_map.124 = (bf16[128,768]{1,0:T(8,128)(2,1)S(1)}, bf16[128,768]{1,0:T(8,128)(2,1)S(1)}, bf16[256,768]{1,0:T(8,128)(2,1)S(1)}, bf16[256,768]{1,0:T(8,128)(2,1)S(1)}) custom-call(bf16[16,768]{1,0:T(8,128)(2,1)S(1)} %shard_map.122.rows_mine, bf16[16,768]{1,0:T(8,128)(2,1)S(1)} %collective-permute-done.4.rows_other, ...), custom_call_target="tpu_custom_call" | custom-call | flops 1811939328 | bytes 7919616 | tf_op jit(solution)/shard_map/pallas_call | solution.py:323
  30.5 1.6 %shard_map.125 = (bf16[256,768]{1,0:T(8,128)(2,1)S(1)}, bf16[256,768]{1,0:T(8,128)(2,1)S(1)}) custom-call(bf16[16,768]{1,0:T(8,128)(2,1)S(1)} %shard_map.122.rows_mine, bf16[16,768]{1,0:T(8,128)(2,1)S(1)} %collective-permute-done.4.rows_other, bf16[3,1536,768]{2,1,0:T(8,128)(2,1)S(1)} %get-tuple-element.62.w, f32[2,768]{1,0:T(2,128)S(1)} %get-tuple-element.63.gains, ...), custom_call_target="tpu_custom_call" | custom-call | flops 1207959552 | bytes 7919616 | tf_op jit(solution)/shard_map/pallas_call | solution.py:323
  34.6 2.1 %collective-permute-done.1.back = bf16[96,1536]{1,0:T(8,128)(2,1)S(1)} collective-permute-done((bf16[96,1536]{1,0:T(8,128)(2,1)S(1)}, bf16[96,1536]{1,0:T(8,128)(2,1)S(1)}, u32[]{:S(2)}, u32[]{:S(2)}) %collective-permute-start.1) | collective-permute-done | bytes 294944 | tf_op jit(solution)/shard_map/ppermute | solution.py:29
  38.7 2.7 %collective-permute-start.12 = (bf16[128,768]{1,0:T(8,128)(2,1)S(1)}, bf16[128,768]{1,0:T(8,128)(2,1)S(1)}, u32[]{:S(2)}, u32[]{:S(2)}) collective-permute-start(bf16[128,768]{1,0:T(8,128)(2,1)S(1)} %shard_map.127.a_mine), channel_id=1, source_target_pairs={{0,1},{1,0},{2,3},{3,2},{4,5},{5,4},{6,7},{7,6},{8,9},{9,8},{10,11... | collective-permute-start | bytes 589832 | tf_op jit(solution)/shard_map/ppermute | solution.py:29
  41.4 5.7 %collective-permute-done.9.a_other = bf16[128,768]{1,0:T(8,128)(2,1)S(1)} collective-permute-done((bf16[128,768]{1,0:T(8,128)(2,1)S(1)}, bf16[128,768]{1,0:T(8,128)(2,1)S(1)}, u32[]{:S(2)}, u32[]{:S(2)}) %collective-permute-start.9) | collective-permute-done | bytes 196640 | tf_op jit(solution)/shard_map/ppermute | solution.py:29
  48.6 3.8 %collective-permute-start.11 = (bf16[128,1536]{1,0:T(8,128)(2,1)S(1)}, bf16[128,1536]{1,0:T(8,128)(2,1)S(1)}, u32[]{:S(2)}, u32[]{:S(2)}) collective-permute-start(bf16[128,1536]{1,0:T(8,128)(2,1)S(1)} %shard_map.129.refs_0_), channel_id=1, source_target_pairs={{2,0},{3,1},{4,2},{5,3},{6,4},{7,5},{8,6},{9,7},{10,8},{11,9},{12,... | collective-permute-start | bytes 1179656 | tf_op jit(solution)/shard_map/ppermute | solution.py:29
  53.8 2.9 %collective-permute-start.13 = (bf16[128,1536]{1,0:T(8,128)(2,1)S(1)}, bf16[128,1536]{1,0:T(8,128)(2,1)S(1)}, u32[]{:S(2)}, u32[]{:S(2)}) collective-permute-start(bf16[128,1536]{1,0:T(8,128)(2,1)S(1)} %shard_map.130.refs_1_), channel_id=1, source_target_pairs={{2,0},{3,1},{4,2},{5,3},{6,4},{7,5},{8,6},{9,7},{10,8},{11,9},{12,... | collective-permute-start | bytes 1179656 | tf_op jit(solution)/shard_map/ppermute | solution.py:29
  57.6 1.6 %shard_map.131 = (bf16[256,768]{1,0:T(8,128)(2,1)S(1)}, bf16[256,768]{1,0:T(8,128)(2,1)S(1)}) custom-call(bf16[16,768]{1,0:T(8,128)(2,1)S(1)} %shard_map.122.rows_mine, bf16[16,768]{1,0:T(8,128)(2,1)S(1)} %collective-permute-done.4.rows_other, bf16[3,1536,768]{2,1,0:T(8,128)(2,1)S(1)} %get-tuple-element.62.w, f32[2,768]{1,0:T(2,128)S(1)} %get-tuple-element.63.gains, ...), custom_call_target="tpu_custom_call" | custom-call | flops 1207959552 | bytes 7919616 | tf_op jit(solution)/shard_map/pallas_call | solution.py:323
  62.0 2.5 %shard_map.133 = (bf16[128,768]{1,0:T(8,128)(2,1)S(1)}, bf16[128,768]{1,0:T(8,128)(2,1)S(1)}, bf16[256,768]{1,0:T(8,128)(2,1)S(1)}, bf16[256,768]{1,0:T(8,128)(2,1)S(1)}) custom-call(s32[128]{0:T(128)S(1)} %copy-done.2, bf16[16,768]{1,0:T(8,128)(2,1)S(1)} %shard_map.122.rows_mine, bf16[16,768]{1,0:T(8,128)(2,1)S(1)} %collective-permute-done.4.rows_other, ...), custom_call_target="tpu_custom_call" | custom-call | flops 2013265920 | bytes 10082304 | tf_op jit(solution)/shard_map/pallas_call | solution.py:323
  66.6 2.8 %collective-permute-start.17 = (bf16[128,768]{1,0:T(8,128)(2,1)S(1)}, bf16[128,768]{1,0:T(8,128)(2,1)S(1)}, u32[]{:S(2)}, u32[]{:S(2)}) collective-permute-start(bf16[128,768]{1,0:T(8,128)(2,1)S(1)} %shard_map.134.a_mine), channel_id=1, source_target_pairs={{0,1},{1,0},{2,3},{3,2},{4,5},{5,4},{6,7},{7,6},{8,9},{9,8},{10,11... | collective-permute-start | bytes 589832 | tf_op jit(solution)/shard_map/ppermute | solution.py:29
  69.4 4.4 %collective-permute-done.14.a_other = bf16[128,768]{1,0:T(8,128)(2,1)S(1)} collective-permute-done((bf16[128,768]{1,0:T(8,128)(2,1)S(1)}, bf16[128,768]{1,0:T(8,128)(2,1)S(1)}, u32[]{:S(2)}, u32[]{:S(2)}) %collective-permute-start.14) | collective-permute-done | bytes 196640 | tf_op jit(solution)/shard_map/ppermute | solution.py:29
  73.8 1.3 %shard_map.135.refs_0_ = bf16[128,1536]{1,0:T(8,128)(2,1)S(1)} custom-call(s32[128]{0:T(128)S(1)} %copy-done.1, bf16[16,768]{1,0:T(8,128)(2,1)S(1)} %shard_map.122.rows_mine, bf16[16,768]{1,0:T(8,128)(2,1)S(1)} %collective-permute-done.4.rows_other, bf16[768,1536]{1,0:T(8,128)(2,1)S(1)} %get-tuple-element.60.w_mine, ...), custom_call_target="tpu_custom_call" | custom-call | flops 603979776 | bytes 6733824 | tf_op jit(solution)/shard_map/pallas_call | solution.py:323
  75.2 4.7 %collective-permute-start.16 = (bf16[128,1536]{1,0:T(8,128)(2,1)S(1)}, bf16[128,1536]{1,0:T(8,128)(2,1)S(1)}, u32[]{:S(2)}, u32[]{:S(2)}) collective-permute-start(bf16[128,1536]{1,0:T(8,128)(2,1)S(1)} %shard_map.135.refs_0_), channel_id=1, source_target_pairs={{2,0},{3,1},{4,2},{5,3},{6,4},{7,5},{8,6},{9,7},{10,8},{11,9},{12,... | collective-permute-start | bytes 1179656 | tf_op jit(solution)/shard_map/ppermute | solution.py:29
  79.9 1.3 %shard_map.136.refs_1_ = bf16[128,1536]{1,0:T(8,128)(2,1)S(1)} custom-call(s32[128]{0:T(128)S(1)} %copy-done.1, bf16[16,768]{1,0:T(8,128)(2,1)S(1)} %shard_map.122.rows_mine, bf16[16,768]{1,0:T(8,128)(2,1)S(1)} %collective-permute-done.4.rows_other, bf16[768,1536]{1,0:T(8,128)(2,1)S(1)} %get-tuple-element.60.w_mine, ...), custom_call_target="tpu_custom_call" | custom-call | flops 603979776 | bytes 6733824 | tf_op jit(solution)/shard_map/pallas_call | solution.py:323
  81.3 2.1 %collective-permute-start.18 = (bf16[128,1536]{1,0:T(8,128)(2,1)S(1)}, bf16[128,1536]{1,0:T(8,128)(2,1)S(1)}, u32[]{:S(2)}, u32[]{:S(2)}) collective-permute-start(bf16[128,1536]{1,0:T(8,128)(2,1)S(1)} %shard_map.136.refs_1_), channel_id=1, source_target_pairs={{2,0},{3,1},{4,2},{5,3},{6,4},{7,5},{8,6},{9,7},{10,8},{11,9},{12,... | collective-permute-start | bytes 1179656 | tf_op jit(solution)/shard_map/ppermute | solution.py:29
  83.4 1.8 %collective-permute-done.16.chunk.first.refs_2_ = bf16[128,1536]{1,0:T(8,128)(2,1)S(1)} collective-permute-done((bf16[128,1536]{1,0:T(8,128)(2,1)S(1)}, bf16[128,1536]{1,0:T(8,128)(2,1)S(1)}, u32[]{:S(2)}, u32[]{:S(2)}) %collective-permute-start.16) | collective-permute-done | bytes 393248 | tf_op jit(solution)/shard_map/ppermute | solution.py:29
  86.5 1.6 %shard_map.137 = (bf16[256,768]{1,0:T(8,128)(2,1)S(1)}, bf16[256,768]{1,0:T(8,128)(2,1)S(1)}) custom-call(bf16[16,768]{1,0:T(8,128)(2,1)S(1)} %shard_map.122.rows_mine, bf16[16,768]{1,0:T(8,128)(2,1)S(1)} %collective-permute-done.4.rows_other, bf16[3,1536,768]{2,1,0:T(8,128)(2,1)S(1)} %get-tuple-element.62.w, f32[2,768]{1,0:T(2,128)S(1)} %get-tuple-element.63.gains, ...), custom_call_target="tpu_custom_call" | custom-call | flops 1207959552 | bytes 7919616 | tf_op jit(solution)/shard_map/pallas_call | solution.py:323
  89.4 2.5 %shard_map.139 = (bf16[128,768]{1,0:T(8,128)(2,1)S(1)}, bf16[128,768]{1,0:T(8,128)(2,1)S(1)}, bf16[256,768]{1,0:T(8,128)(2,1)S(1)}, bf16[256,768]{1,0:T(8,128)(2,1)S(1)}) custom-call(s32[128]{0:T(128)S(1)} %copy-done.2, bf16[16,768]{1,0:T(8,128)(2,1)S(1)} %shard_map.122.rows_mine, bf16[16,768]{1,0:T(8,128)(2,1)S(1)} %collective-permute-done.4.rows_other, ...), custom_call_target="tpu_custom_call" | custom-call | flops 2013265920 | bytes 10082304 | tf_op jit(solution)/shard_map/pallas_call | solution.py:323
  91.9 2.0 %collective-permute-start.19 = (bf16[128,768]{1,0:T(8,128)(2,1)S(1)}, bf16[128,768]{1,0:T(8,128)(2,1)S(1)}, u32[]{:S(2)}, u32[]{:S(2)}) collective-permute-start(bf16[128,768]{1,0:T(8,128)(2,1)S(1)} %get-tuple-element.105.a_mine), channel_id=1, source_target_pairs={{0,1},{1,0},{2,3},{3,2},{4,5},{5,4},{6,7},{7,6},{8,9},{9,8},{10,11... | collective-permute-start | bytes 589832 | tf_op jit(solution)/shard_map/ppermute | solution.py:29
  95.1 1.7 %collective-permute-start.21 = (bf16[128,768]{1,0:T(8,128)(2,1)S(1)}, bf16[128,768]{1,0:T(8,128)(2,1)S(1)}, u32[]{:S(2)}, u32[]{:S(2)}) collective-permute-start(bf16[128,768]{1,0:T(8,128)(2,1)S(1)} %shard_map.140.a_mine), channel_id=1, source_target_pairs={{0,1},{1,0},{2,3},{3,2},{4,5},{5,4},{6,7},{7,6},{8,9},{9,8},{10,11... | collective-permute-start | bytes 589832 | tf_op jit(solution)/shard_map/ppermute | solution.py:29
  96.8 4.3 %collective-permute-done.19.a_other = bf16[128,768]{1,0:T(8,128)(2,1)S(1)} collective-permute-done((bf16[128,768]{1,0:T(8,128)(2,1)S(1)}, bf16[128,768]{1,0:T(8,128)(2,1)S(1)}, u32[]{:S(2)}, u32[]{:S(2)}) %collective-permute-start.19) | collective-permute-done | bytes 196640 | tf_op jit(solution)/shard_map/ppermute | solution.py:29
  102.1 3.8 %collective-permute-start.20 = (bf16[128,768]{1,0:T(8,128)(2,1)S(1)}, bf16[128,768]{1,0:T(8,128)(2,1)S(1)}, u32[]{:S(2)}, u32[]{:S(2)}) collective-permute-start(bf16[128,768]{1,0:T(8,128)(2,1)S(1)} %get-tuple-element.111), channel_id=1, source_target_pairs={{2,0},{3,1},{4,2},{5,3},{6,4},{7,5},{8,6},{9,7},{10,8},{11,9},{12,... | collective-permute-start | bytes 589832 | tf_op jit(solution)/shard_map/ppermute | solution.py:29
  107.0 2.8 %collective-permute-start.22 = (bf16[128,768]{1,0:T(8,128)(2,1)S(1)}, bf16[128,768]{1,0:T(8,128)(2,1)S(1)}, u32[]{:S(2)}, u32[]{:S(2)}) collective-permute-start(bf16[128,768]{1,0:T(8,128)(2,1)S(1)} %get-tuple-element.114), channel_id=1, source_target_pairs={{2,0},{3,1},{4,2},{5,3},{6,4},{7,5},{8,6},{9,7},{10,8},{11,9},{12,... | collective-permute-start | bytes 589832 | tf_op jit(solution)/shard_map/ppermute | solution.py:29
  109.8 3.1 %collective-permute-done.22.advanced = bf16[128,768]{1,0:T(8,128)(2,1)S(1)} collective-permute-done((bf16[128,768]{1,0:T(8,128)(2,1)S(1)}, bf16[128,768]{1,0:T(8,128)(2,1)S(1)}, u32[]{:S(2)}, u32[]{:S(2)}) %collective-permute-start.22) | collective-permute-done | bytes 196640 | tf_op jit(solution)/shard_map/ppermute | solution.py:29
  (45 shorter events, 24.5 us)
Async XLA Ops:
  0.6 13.3 %collective-permute-start.5 = (bf16[256,768]{1,0:T(8,128)(2,1)}, bf16[256,768]{1,0:T(8,128)(2,1)S(1)}, u32[]{:S(2)}, u32[]{:S(2)}) collective-permute-start(bf16[256,768]{1,0:T(8,128)(2,1)} %refs_0_.3), channel_id=1, source_target_pairs={{0,1},{1,0},{2,3},{3,2},{4,5},{5,4},{6,7},{7,6},{8,9},{9,8},{10,11... | collective-permute-start | bytes 1179656 | tf_op jit(solution)/shard_map/ppermute | solution.py:29
  3.4 16.7 %collective-permute-start = (bf16[96,1536]{1,0:T(8,128)(2,1)S(1)}, bf16[96,1536]{1,0:T(8,128)(2,1)S(1)}, u32[]{:S(2)}, u32[]{:S(2)}) collective-permute-start(bf16[96,1536]{1,0:T(8,128)(2,1)S(1)} %constant_dynamic-slice_fusion), channel_id=1, source_target_pairs={{0,5},{1,4},{2,7},{3,6},{4,1},{5,0},{6,3},{7,2},{8,13},{9,12},{10,... | collective-permute-start | bytes 884744 | tf_op jit(solution)/shard_map/ppermute | solution.py:29
  5.7 8.3 %collective-permute-start.4 = (bf16[16,768]{1,0:T(8,128)(2,1)S(1)}, bf16[16,768]{1,0:T(8,128)(2,1)S(1)}, u32[]{:S(2)}, u32[]{:S(2)}) collective-permute-start(bf16[16,768]{1,0:T(8,128)(2,1)S(1)} %shard_map.122.rows_mine), channel_id=1, source_target_pairs={{0,1},{1,0},{2,3},{3,2},{4,5},{5,4},{6,7},{7,6},{8,9},{9,8},{10,11... | collective-permute-start | bytes 73736 | tf_op jit(solution)/shard_map/ppermute | solution.py:29
  7.7 8.2 %copy-start = (bf16[256,768]{1,0:T(8,128)(2,1)S(1)}, bf16[256,768]{1,0:T(8,128)(2,1)}, u32[]{:S(2)}) copy-start(bf16[256,768]{1,0:T(8,128)(2,1)} %refs_0_.3) | copy-start | bytes 1179652
  13.9 16.4 %collective-permute-start.7 = (bf16[256,768]{1,0:T(8,128)(2,1)S(1)}, bf16[256,768]{1,0:T(8,128)(2,1)S(1)}, u32[]{:S(2)}, u32[]{:S(2)}) collective-permute-start(bf16[256,768]{1,0:T(8,128)(2,1)S(1)} %collective-permute-done.5.other.refs_1_), channel_id=1, source_target_pairs={{0,2},{1,3},{2,4},{3,5},{4,6},{5,7},{6,8},{7,9},{8,10},{9,11},{10,... | collective-permute-start | bytes 1179656 | tf_op jit(solution)/shard_map/ppermute | solution.py:29
  15.8 14.6 %collective-permute-start.6 = (bf16[256,768]{1,0:T(8,128)(2,1)S(1)}, bf16[256,768]{1,0:T(8,128)(2,1)S(1)}, u32[]{:S(2)}, u32[]{:S(2)}) collective-permute-start(bf16[256,768]{1,0:T(8,128)(2,1)S(1)} %copy-done), channel_id=1, source_target_pairs={{0,2},{1,3},{2,4},{3,5},{4,6},{5,7},{6,8},{7,9},{8,10},{9,11},{10,... | collective-permute-start | bytes 1179656 | tf_op jit(solution)/shard_map/ppermute | solution.py:29
  20.1 16.6 %collective-permute-start.1 = (bf16[96,1536]{1,0:T(8,128)(2,1)S(1)}, bf16[96,1536]{1,0:T(8,128)(2,1)S(1)}, u32[]{:S(2)}, u32[]{:S(2)}) collective-permute-start(bf16[96,1536]{1,0:T(8,128)(2,1)S(1)} %collective-permute-done.own), channel_id=1, source_target_pairs={{0,64},{1,65},{2,66},{3,67},{4,68},{5,69},{6,70},{7,71},{8,72},{9,... | collective-permute-start | bytes 884744 | tf_op jit(solution)/shard_map/ppermute | solution.py:29
  21.7 15.0 %collective-permute-start.2 = (bf16[96,1536]{1,0:T(8,128)(2,1)S(1)}, bf16[96,1536]{1,0:T(8,128)(2,1)S(1)}, u32[]{:S(2)}, u32[]{:S(2)}) collective-permute-start(bf16[96,1536]{1,0:T(8,128)(2,1)S(1)} %collective-permute-done.own), channel_id=1, source_target_pairs={{0,192},{1,193},{2,194},{3,195},{4,196},{5,197},{6,198},{7,199},{8... | collective-permute-start | bytes 884744 | tf_op jit(solution)/shard_map/ppermute | solution.py:29
  22.2 14.5 %collective-permute-start.3 = (bf16[96,1536]{1,0:T(8,128)(2,1)S(1)}, bf16[96,1536]{1,0:T(8,128)(2,1)S(1)}, u32[]{:S(2)}, u32[]{:S(2)}) collective-permute-start(bf16[96,1536]{1,0:T(8,128)(2,1)S(1)} %collective-permute-done.own), channel_id=1, source_target_pairs={{0,56},{1,57},{2,58},{3,59},{4,60},{5,61},{6,62},{7,63},{8,0},{9,1... | collective-permute-start | bytes 884744 | tf_op jit(solution)/shard_map/ppermute | solution.py:29
  30.3 1.8 %copy-start.2 = (s32[128]{0:T(128)S(1)}, s32[128]{0:T(128)}, u32[]{:S(2)}) copy-start(s32[128]{0:T(128)} %starts.11) | copy-start | bytes 1540
  36.8 10.2 %collective-permute-start.8 = (bf16[4,96,1536]{2,1,0:T(8,128)(2,1)S(1)}, bf16[4,96,1536]{2,1,0:T(8,128)(2,1)S(1)}, u32[]{:S(2)}, u32[]{:S(2)}) collective-permute-start(bf16[4,96,1536]{2,1,0:T(8,128)(2,1)S(1)} %pad_maximum_fusion), channel_id=1, source_target_pairs={{0,2},{1,3},{2,0},{3,1},{4,6},{5,7},{6,4},{7,5},{8,10},{9,11},{10,... | collective-permute-start | bytes 3538952 | tf_op jit(solution)/shard_map/ppermute | solution.py:29
  37.0 10.3 %copy-start.1 = (s32[128]{0:T(128)S(1)}, s32[128]{0:T(128)}, u32[]{:S(2)}) copy-start(s32[128]{0:T(128)} %levels.11) | copy-start | bytes 1540
  37.0 10.1 %collective-permute-start.10 = (bf16[256,768]{1,0:T(8,128)(2,1)S(1)}, bf16[256,768]{1,0:T(8,128)(2,1)S(1)}, u32[]{:S(2)}, u32[]{:S(2)}) collective-permute-start(bf16[256,768]{1,0:T(8,128)(2,1)S(1)} %get-tuple-element.79.fresh.refs_0_), channel_id=1, source_target_pairs={{250,255},{251,254}} | collective-permute-start | bytes 1179656 | tf_op jit(solution)/shard_map/ppermute | solution.py:29
  37.8 9.3 %collective-permute-start.9 = (bf16[128,768]{1,0:T(8,128)(2,1)S(1)}, bf16[128,768]{1,0:T(8,128)(2,1)S(1)}, u32[]{:S(2)}, u32[]{:S(2)}) collective-permute-start(bf16[128,768]{1,0:T(8,128)(2,1)S(1)} %shard_map.126.a_mine), channel_id=1, source_target_pairs={{0,1},{1,0},{2,3},{3,2},{4,5},{5,4},{6,7},{7,6},{8,9},{9,8},{10,11... | collective-permute-start | bytes 589832 | tf_op jit(solution)/shard_map/ppermute | solution.py:29
  38.7 13.8 %collective-permute-start.12 = (bf16[128,768]{1,0:T(8,128)(2,1)S(1)}, bf16[128,768]{1,0:T(8,128)(2,1)S(1)}, u32[]{:S(2)}, u32[]{:S(2)}) collective-permute-start(bf16[128,768]{1,0:T(8,128)(2,1)S(1)} %shard_map.127.a_mine), channel_id=1, source_target_pairs={{0,1},{1,0},{2,3},{3,2},{4,5},{5,4},{6,7},{7,6},{8,9},{9,8},{10,11... | collective-permute-start | bytes 589832 | tf_op jit(solution)/shard_map/ppermute | solution.py:29
  48.6 8.9 %collective-permute-start.11 = (bf16[128,1536]{1,0:T(8,128)(2,1)S(1)}, bf16[128,1536]{1,0:T(8,128)(2,1)S(1)}, u32[]{:S(2)}, u32[]{:S(2)}) collective-permute-start(bf16[128,1536]{1,0:T(8,128)(2,1)S(1)} %shard_map.129.refs_0_), channel_id=1, source_target_pairs={{2,0},{3,1},{4,2},{5,3},{6,4},{7,5},{8,6},{9,7},{10,8},{11,9},{12,... | collective-permute-start | bytes 1179656 | tf_op jit(solution)/shard_map/ppermute | solution.py:29
  53.8 8.1 %collective-permute-start.13 = (bf16[128,1536]{1,0:T(8,128)(2,1)S(1)}, bf16[128,1536]{1,0:T(8,128)(2,1)S(1)}, u32[]{:S(2)}, u32[]{:S(2)}) collective-permute-start(bf16[128,1536]{1,0:T(8,128)(2,1)S(1)} %shard_map.130.refs_1_), channel_id=1, source_target_pairs={{2,0},{3,1},{4,2},{5,3},{6,4},{7,5},{8,6},{9,7},{10,8},{11,9},{12,... | collective-permute-start | bytes 1179656 | tf_op jit(solution)/shard_map/ppermute | solution.py:29
  59.1 14.7 %collective-permute-start.15 = (bf16[256,768]{1,0:T(8,128)(2,1)S(1)}, bf16[256,768]{1,0:T(8,128)(2,1)S(1)}, u32[]{:S(2)}, u32[]{:S(2)}) collective-permute-start(bf16[256,768]{1,0:T(8,128)(2,1)S(1)} %get-tuple-element.95.fresh.refs_0_), channel_id=1, source_target_pairs={{250,255},{251,254}} | collective-permute-start | bytes 1179656 | tf_op jit(solution)/shard_map/ppermute | solution.py:29
  64.4 9.4 %collective-permute-start.14 = (bf16[128,768]{1,0:T(8,128)(2,1)S(1)}, bf16[128,768]{1,0:T(8,128)(2,1)S(1)}, u32[]{:S(2)}, u32[]{:S(2)}) collective-permute-start(bf16[128,768]{1,0:T(8,128)(2,1)S(1)} %get-tuple-element.89.a_mine), channel_id=1, source_target_pairs={{0,1},{1,0},{2,3},{3,2},{4,5},{5,4},{6,7},{7,6},{8,9},{9,8},{10,11... | collective-permute-start | bytes 589832 | tf_op jit(solution)/shard_map/ppermute | solution.py:29
  66.6 13.3 %collective-permute-start.17 = (bf16[128,768]{1,0:T(8,128)(2,1)S(1)}, bf16[128,768]{1,0:T(8,128)(2,1)S(1)}, u32[]{:S(2)}, u32[]{:S(2)}) collective-permute-start(bf16[128,768]{1,0:T(8,128)(2,1)S(1)} %shard_map.134.a_mine), channel_id=1, source_target_pairs={{0,1},{1,0},{2,3},{3,2},{4,5},{5,4},{6,7},{7,6},{8,9},{9,8},{10,11... | collective-permute-start | bytes 589832 | tf_op jit(solution)/shard_map/ppermute | solution.py:29
  75.2 10.0 %collective-permute-start.16 = (bf16[128,1536]{1,0:T(8,128)(2,1)S(1)}, bf16[128,1536]{1,0:T(8,128)(2,1)S(1)}, u32[]{:S(2)}, u32[]{:S(2)}) collective-permute-start(bf16[128,1536]{1,0:T(8,128)(2,1)S(1)} %shard_map.135.refs_0_), channel_id=1, source_target_pairs={{2,0},{3,1},{4,2},{5,3},{6,4},{7,5},{8,6},{9,7},{10,8},{11,9},{12,... | collective-permute-start | bytes 1179656 | tf_op jit(solution)/shard_map/ppermute | solution.py:29
  81.3 8.1 %collective-permute-start.18 = (bf16[128,1536]{1,0:T(8,128)(2,1)S(1)}, bf16[128,1536]{1,0:T(8,128)(2,1)S(1)}, u32[]{:S(2)}, u32[]{:S(2)}) collective-permute-start(bf16[128,1536]{1,0:T(8,128)(2,1)S(1)} %shard_map.136.refs_1_), channel_id=1, source_target_pairs={{2,0},{3,1},{4,2},{5,3},{6,4},{7,5},{8,6},{9,7},{10,8},{11,9},{12,... | collective-permute-start | bytes 1179656 | tf_op jit(solution)/shard_map/ppermute | solution.py:29
  91.9 9.2 %collective-permute-start.19 = (bf16[128,768]{1,0:T(8,128)(2,1)S(1)}, bf16[128,768]{1,0:T(8,128)(2,1)S(1)}, u32[]{:S(2)}, u32[]{:S(2)}) collective-permute-start(bf16[128,768]{1,0:T(8,128)(2,1)S(1)} %get-tuple-element.105.a_mine), channel_id=1, source_target_pairs={{0,1},{1,0},{2,3},{3,2},{4,5},{5,4},{6,7},{7,6},{8,9},{9,8},{10,11... | collective-permute-start | bytes 589832 | tf_op jit(solution)/shard_map/ppermute | solution.py:29
  95.1 10.8 %collective-permute-start.21 = (bf16[128,768]{1,0:T(8,128)(2,1)S(1)}, bf16[128,768]{1,0:T(8,128)(2,1)S(1)}, u32[]{:S(2)}, u32[]{:S(2)}) collective-permute-start(bf16[128,768]{1,0:T(8,128)(2,1)S(1)} %shard_map.140.a_mine), channel_id=1, source_target_pairs={{0,1},{1,0},{2,3},{3,2},{4,5},{5,4},{6,7},{7,6},{8,9},{9,8},{10,11... | collective-permute-start | bytes 589832 | tf_op jit(solution)/shard_map/ppermute | solution.py:29
  102.1 7.7 %collective-permute-start.20 = (bf16[128,768]{1,0:T(8,128)(2,1)S(1)}, bf16[128,768]{1,0:T(8,128)(2,1)S(1)}, u32[]{:S(2)}, u32[]{:S(2)}) collective-permute-start(bf16[128,768]{1,0:T(8,128)(2,1)S(1)} %get-tuple-element.111), channel_id=1, source_target_pairs={{2,0},{3,1},{4,2},{5,3},{6,4},{7,5},{8,6},{9,7},{10,8},{11,9},{12,... | collective-permute-start | bytes 589832 | tf_op jit(solution)/shard_map/ppermute | solution.py:29
  107.0 6.0 %collective-permute-start.22 = (bf16[128,768]{1,0:T(8,128)(2,1)S(1)}, bf16[128,768]{1,0:T(8,128)(2,1)S(1)}, u32[]{:S(2)}, u32[]{:S(2)}) collective-permute-start(bf16[128,768]{1,0:T(8,128)(2,1)S(1)} %get-tuple-element.114), channel_id=1, source_target_pairs={{2,0},{3,1},{4,2},{5,3},{6,4},{7,5},{8,6},{9,7},{10,8},{11,9},{12,... | collective-permute-start | bytes 589832 | tf_op jit(solution)/shard_map/ppermute | solution.py:29

commit v6 on v5

--- a/solution.py
+++ b/solution.py
@@ -255,29 +255,46 @@
     return t_next - t_cur
 
 
-def project_kernel(kind, row, levels, rows_mine, rows_other, w_mine, w_other, a_mine, a_other, *refs):
-    x, new = refs[:-1], refs[-1]
-    count = new.shape[0]
+def mine_kernel(kind, levels, rows_mine, rows_other, w_mine, *refs):
+    x, chunks, bases = refs[: -2 * CHUNKS], refs[-2 * CHUNKS : -CHUNKS], refs[-CHUNKS:]
+    gate = table_row((rows_mine, rows_other), GATE)
+    size = step_size_of(levels)
+    for c, (chunk, base) in enumerate(zip(chunks, bases)):
+        count, width = chunk.shape[0], base.shape[1] // 2
+        halves = halves_of(kind, x, c * count, count)
+        product = dot(chunk[...], w_mine[...])
+        for n in range(2):
+            part = slice(n * width, (n + 1) * width)
+            base[:, part] = halves[n].astype(jnp.float32) + size * gate[n] * product[:, part]
+
+
+def project_kernel(levels, rows_mine, rows_other, w_other, base, a_other, new):
     width = new.shape[1] // 2
     gate = table_row((rows_mine, rows_other), GATE)
-    halves = halves_of(kind, x, row, count)
-    product = dot(a_mine[...], w_mine[...]) + dot(a_other[...], w_other[...])
+    size = step_size_of(levels)
+    product = dot(a_other[...], w_other[...])
     for n in range(2):
         part = slice(n * width, (n + 1) * width)
-        velocity = gate[n] * product[:, part]
-        value = (halves[n].astype(jnp.float32) + step_size_of(levels) * velocity).astype(jnp.bfloat16)
-        new[:, part] = value
-
-
-def final_kernel(kind, row, levels, rows_mine, w_mine, w_other, a_mine, a_other, *refs):
+        new[:, part] = (base[:, part] + size * gate[n] * product[:, part]).astype(jnp.bfloat16)
+
+
+def own_features(width):
+    return pl.ds(pl.multiple_of(lax.axis_index("heads") * width, HD), width)
+
+
+def last_mine_kernel(rows_mine, w_mine, *refs):
+    gate = rows_mine[GATE : GATE + 1, :].astype(jnp.float32)
+    for chunk, base in zip(refs[:CHUNKS], refs[CHUNKS:]):
+        base[...] = gate * dot(chunk[...], w_mine[:, own_features(base.shape[1])])
+
+
+def final_kernel(kind, row, levels, rows_mine, w_other, base, a_other, *refs):
     x, (new, velocity_out) = refs[:-2], refs[-2:]
     count, width = new.shape
-    half = lax.axis_index("heads")
-    part = pl.ds(pl.multiple_of(half * width, HD), width)
     low, high = halves_of(kind, x, row, count)
-    held = jnp.where(half == 0, low, high).astype(jnp.float32)
-    product = dot(a_mine[...], w_mine[:, part]) + dot(a_other[...], w_other[:, part])
-    velocity = rows_mine[GATE : GATE + 1, :].astype(jnp.float32) * product
+    held = jnp.where(lax.axis_index("heads") == 0, low, high).astype(jnp.float32)
+    gate = rows_mine[GATE : GATE + 1, :].astype(jnp.float32)
+    velocity = base[...] + gate * dot(a_other[...], w_other[:, own_features(width)])
     velocity_out[...] = velocity.astype(jnp.bfloat16)
     new[...] = (held + step_size_of(levels) * velocity).astype(jnp.bfloat16)
 
@@ -444,21 +461,39 @@
         waits = []
         if step < STEPS - 1:
             fresh_other = routed(
-                after(fresh[step], near_keys), lambda q, h: (last, 1 - h) if q == last - 2 else None
-            )
-            waits = [fresh_other]
-        received[0] = after(received[0], parts[1], *waits)
+                after(fresh[step], near_keys if step else received[0]), lambda q, h: (last, 1 - h) if q == last - 2 else None
+            )
+            waits = [fresh_other] if step else []
+        if step < STEPS - 1:
+            bases = kernel_call(
+                functools.partial(mine_kernel, kind),
+                ((count, 2 * width),) * CHUNKS,
+                (level_index,),
+                (*table, w_out, *state, *parts),
+                2 * out_products,
+                dtype=jnp.float32,
+            )
+        else:
+            bases = kernel_call(
+                last_mine_kernel,
+                ((count, width),) * CHUNKS,
+                (),
+                (rows_mine, w_out, *parts),
+                out_products,
+                dtype=jnp.float32,
+            )
+        received[0] = after(received[0], *bases, *waits)
         if step == 0:
-            w_other = other_projection(piece, parts[1], w_out.shape)
+            w_other = other_projection(piece, parts[0], w_out.shape)
         if step < STEPS - 1:
             new = []
             for n in range(CHUNKS):
                 block = kernel_call(
-                    functools.partial(project_kernel, kind, n * count),
+                    project_kernel,
                     (count, 2 * width),
                     (level_index,),
-                    (*table, w_out, w_other, parts[n], after(received[n], *new), *state),
-                    2 * out_products,
+                    (*table, w_other, bases[n], after(received[n], *new)),
+                    out_products,
                 )
                 new.append(block)
             state = (fresh[step], fresh_other, *[down(block) for block in new])
@@ -471,8 +506,8 @@
                     functools.partial(final_kernel, kind, n * count),
                     ((count, width), (count, width)),
                     (level_index,),
-                    (rows_mine, w_out, w_other, parts[n], after(received[n], *(p[0] for p in done)), *state),
-                    out_products,
+                    (rows_mine, w_other, bases[n], after(received[n], *(p[0] for p in done)), *state),
+                    out_products // 2,
                 )
                 done.append(pair)
             advanced = [down(block) for block, _ in done]

time: 115 us -> 114 us (level)
  starting transfers between devices: 50.5 us -> 48.2 us
  Pallas kernels: 33.4 us -> 35 us
    ppermute x23, starting transfers between devices: 50.5 us -> 48.2 us  [routed(): return lax.ppermute(block, AXES, pairs)]
    pallas_call x21 -> x24, Pallas kernels: 28.1 us -> 29.8 us  [kernel_call(): pl.pallas_call(kernel, cost_estimate=pl.CostEstimate(flops=2 * products,...]
  transfers between devices with their start and end apart: 23 -> 23, of which waited for: 12 -> 13; matrix products, arithmetic and copies ran while one was open for 1% -> 1% of each run, Pallas kernels for 26% -> 28%
where the time goes in v6:
time: 114 us; the launch traced here: 113 us
  starting transfers between devices  48.2 us (42%)
  Pallas kernels  35 us (31%)
  waiting for transfers between devices  27.9 us (24%)
    ppermute x23, starting transfers between devices, routed(): return lax.ppermute(block, AXES, pairs)  48.2 us
    pallas_call x24, Pallas kernels, kernel_call(): pl.pallas_call(kernel, cost_estimate=pl.CostEstimate(flops=2 * products,...  29.8 us
    ppermute x23, waiting for transfers between devices, routed(): return lax.ppermute(block, AXES, pairs)  27.9 us
    pallas_call x1, Pallas kernels, stage_call(): pl.pallas_call(stage_kernel, out_shape=(pltpu.VMEM(w.shape, w.dtype), plt...  4.05 us
  transfers between devices with their start and end apart: 23, of which 13 were waited for; matrix products, arithmetic and copies ran while one was open for 1% of the time, Pallas kernels for 28%

profile of v6, /device:TPU:12, one launch (start us, length us, event | category | flops | bytes accessed | tf_op | source)
XLA Modules:
  0.0 113.2 jit_solution(6128891207931514190)
XLA Ops:
  3.4 2.2 %collective-permute-start = (bf16[96,1536]{1,0:T(8,128)(2,1)S(1)}, bf16[96,1536]{1,0:T(8,128)(2,1)S(1)}, u32[]{:S(2)}, u32[]{:S(2)}) collective-permute-start(bf16[96,1536]{1,0:T(8,128)(2,1)S(1)} %constant_dynamic-slice_fusion), channel_id=1, source_target_pairs={{0,5},{1,4},{2,7},{3,6},{4,1},{5,0},{6,3},{7,2},{8,13},{9,12},{10,... | collective-permute-start | bytes 884744 | tf_op jit(solution)/shard_map/ppermute | solution.py:29
  5.7 2.0 %collective-permute-start.4 = (bf16[16,768]{1,0:T(8,128)(2,1)S(1)}, bf16[16,768]{1,0:T(8,128)(2,1)S(1)}, u32[]{:S(2)}, u32[]{:S(2)}) collective-permute-start(bf16[16,768]{1,0:T(8,128)(2,1)S(1)} %shard_map.122.rows_mine), channel_id=1, source_target_pairs={{0,1},{1,0},{2,3},{3,2},{4,5},{5,4},{6,7},{7,6},{8,9},{9,8},{10,11... | collective-permute-start | bytes 73736 | tf_op jit(solution)/shard_map/ppermute | solution.py:29
  7.7 4.0 %shard_map.123 = (bf16[3,1536,768]{2,1,0:T(8,128)(2,1)S(1)}, f32[2,768]{1,0:T(2,128)S(1)}, bf16[256,768]{1,0:T(8,128)(2,1)S(1)}, bf16[256,768]{1,0:T(8,128)(2,1)...) custom-call(bf16[3,1536,768]{2,1,0:T(8,128)(2,1)} %bitcast.9, f32[768]{0:T(1024)} %q_hbm.1, f32[768]{0:T(1024)} %k_hbm.1, ...), custom_call_target="tpu_custom_call" | custom-call | tf_op jit(solution)/shard_map/pallas_call | solution.py:134
  11.7 2.2 %collective-permute-done.4.rows_other = bf16[16,768]{1,0:T(8,128)(2,1)S(1)} collective-permute-done((bf16[16,768]{1,0:T(8,128)(2,1)S(1)}, bf16[16,768]{1,0:T(8,128)(2,1)S(1)}, u32[]{:S(2)}, u32[]{:S(2)}) %collective-permute-start.4) | collective-permute-done | bytes 24608 | tf_op jit(solution)/shard_map/ppermute | solution.py:29
  13.9 1.9 %collective-permute-start.7 = (bf16[256,768]{1,0:T(8,128)(2,1)S(1)}, bf16[256,768]{1,0:T(8,128)(2,1)S(1)}, u32[]{:S(2)}, u32[]{:S(2)}) collective-permute-start(bf16[256,768]{1,0:T(8,128)(2,1)S(1)} %collective-permute-done.5.other.refs_1_), channel_id=1, source_target_pairs={{0,2},{1,3},{2,4},{3,5},{4,6},{5,7},{6,8},{7,9},{8,10},{9,11},{10,... | collective-permute-start | bytes 1179656 | tf_op jit(solution)/shard_map/ppermute | solution.py:29
  15.8 3.2 %collective-permute-start.6 = (bf16[256,768]{1,0:T(8,128)(2,1)S(1)}, bf16[256,768]{1,0:T(8,128)(2,1)S(1)}, u32[]{:S(2)}, u32[]{:S(2)}) collective-permute-start(bf16[256,768]{1,0:T(8,128)(2,1)S(1)} %copy-done), channel_id=1, source_target_pairs={{0,2},{1,3},{2,4},{3,5},{4,6},{5,7},{6,8},{7,9},{8,10},{9,11},{10,... | collective-permute-start | bytes 1179656 | tf_op jit(solution)/shard_map/ppermute | solution.py:29
  20.1 1.6 %collective-permute-start.1 = (bf16[96,1536]{1,0:T(8,128)(2,1)S(1)}, bf16[96,1536]{1,0:T(8,128)(2,1)S(1)}, u32[]{:S(2)}, u32[]{:S(2)}) collective-permute-start(bf16[96,1536]{1,0:T(8,128)(2,1)S(1)} %collective-permute-done.own), channel_id=1, source_target_pairs={{0,64},{1,65},{2,66},{3,67},{4,68},{5,69},{6,70},{7,71},{8,72},{9,... | collective-permute-start | bytes 884744 | tf_op jit(solution)/shard_map/ppermute | solution.py:29
  22.2 5.9 %collective-permute-start.3 = (bf16[96,1536]{1,0:T(8,128)(2,1)S(1)}, bf16[96,1536]{1,0:T(8,128)(2,1)S(1)}, u32[]{:S(2)}, u32[]{:S(2)}) collective-permute-start(bf16[96,1536]{1,0:T(8,128)(2,1)S(1)} %collective-permute-done.own), channel_id=1, source_target_pairs={{0,56},{1,57},{2,58},{3,59},{4,60},{5,61},{6,62},{7,63},{8,0},{9,1... | collective-permute-start | bytes 884744 | tf_op jit(solution)/shard_map/ppermute | solution.py:29
  28.0 2.3 %shard_map.124 = (bf16[128,768]{1,0:T(8,128)(2,1)S(1)}, bf16[128,768]{1,0:T(8,128)(2,1)S(1)}, bf16[256,768]{1,0:T(8,128)(2,1)S(1)}, bf16[256,768]{1,0:T(8,128)(2,1)S(1)}) custom-call(bf16[16,768]{1,0:T(8,128)(2,1)S(1)} %shard_map.122.rows_mine, bf16[16,768]{1,0:T(8,128)(2,1)S(1)} %collective-permute-done.4.rows_other, ...), custom_call_target="tpu_custom_call" | custom-call | flops 1811939328 | bytes 7919616 | tf_op jit(solution)/shard_map/pallas_call | solution.py:340
  30.5 1.6 %shard_map.125 = (bf16[256,768]{1,0:T(8,128)(2,1)S(1)}, bf16[256,768]{1,0:T(8,128)(2,1)S(1)}) custom-call(bf16[16,768]{1,0:T(8,128)(2,1)S(1)} %shard_map.122.rows_mine, bf16[16,768]{1,0:T(8,128)(2,1)S(1)} %collective-permute-done.4.rows_other, bf16[3,1536,768]{2,1,0:T(8,128)(2,1)S(1)} %get-tuple-element.67.w, f32[2,768]{1,0:T(2,128)S(1)} %get-tuple-element.68.gains, ...), custom_call_target="tpu_custom_call" | custom-call | flops 1207959552 | bytes 7919616 | tf_op jit(solution)/shard_map/pallas_call | solution.py:340
  33.4 3.3 %collective-permute-done.1.back = bf16[96,1536]{1,0:T(8,128)(2,1)S(1)} collective-permute-done((bf16[96,1536]{1,0:T(8,128)(2,1)S(1)}, bf16[96,1536]{1,0:T(8,128)(2,1)S(1)}, u32[]{:S(2)}, u32[]{:S(2)}) %collective-permute-start.1) | collective-permute-done | bytes 294944 | tf_op jit(solution)/shard_map/ppermute | solution.py:29
  39.1 2.8 %collective-permute-start.12 = (bf16[128,768]{1,0:T(8,128)(2,1)S(1)}, bf16[128,768]{1,0:T(8,128)(2,1)S(1)}, u32[]{:S(2)}, u32[]{:S(2)}) collective-permute-start(bf16[128,768]{1,0:T(8,128)(2,1)S(1)} %shard_map.128.refs_3_), channel_id=1, source_target_pairs={{0,1},{1,0},{2,3},{3,2},{4,5},{5,4},{6,7},{7,6},{8,9},{9,8},{10,11... | collective-permute-start | bytes 589832 | tf_op jit(solution)/shard_map/ppermute | solution.py:29
  43.2 3.0 %collective-permute-done.9.a_other = bf16[128,768]{1,0:T(8,128)(2,1)S(1)} collective-permute-done((bf16[128,768]{1,0:T(8,128)(2,1)S(1)}, bf16[128,768]{1,0:T(8,128)(2,1)S(1)}, u32[]{:S(2)}, u32[]{:S(2)}) %collective-permute-start.9) | collective-permute-done | bytes 196640 | tf_op jit(solution)/shard_map/ppermute | solution.py:29
  47.5 3.4 %collective-permute-start.11 = (bf16[128,1536]{1,0:T(8,128)(2,1)S(1)}, bf16[128,1536]{1,0:T(8,128)(2,1)S(1)}, u32[]{:S(2)}, u32[]{:S(2)}) collective-permute-start(bf16[128,1536]{1,0:T(8,128)(2,1)S(1)} %shard_map.130.refs_0_), channel_id=1, source_target_pairs={{2,0},{3,1},{4,2},{5,3},{6,4},{7,5},{8,6},{9,7},{10,8},{11,9},{12,... | collective-permute-start | bytes 1179656 | tf_op jit(solution)/shard_map/ppermute | solution.py:29
  51.7 2.5 %collective-permute-done.12.a_other = bf16[128,768]{1,0:T(8,128)(2,1)S(1)} collective-permute-done((bf16[128,768]{1,0:T(8,128)(2,1)S(1)}, bf16[128,768]{1,0:T(8,128)(2,1)S(1)}, u32[]{:S(2)}, u32[]{:S(2)}) %collective-permute-start.12) | collective-permute-done | bytes 196640 | tf_op jit(solution)/shard_map/ppermute | solution.py:29
  55.2 1.9 %collective-permute-start.13 = (bf16[128,1536]{1,0:T(8,128)(2,1)S(1)}, bf16[128,1536]{1,0:T(8,128)(2,1)S(1)}, u32[]{:S(2)}, u32[]{:S(2)}) collective-permute-start(bf16[128,1536]{1,0:T(8,128)(2,1)S(1)} %shard_map.131.refs_1_), channel_id=1, source_target_pairs={{2,0},{3,1},{4,2},{5,3},{6,4},{7,5},{8,6},{9,7},{10,8},{11,9},{12,... | collective-permute-start | bytes 1179656 | tf_op jit(solution)/shard_map/ppermute | solution.py:29
  57.2 1.6 %shard_map.132 = (bf16[256,768]{1,0:T(8,128)(2,1)S(1)}, bf16[256,768]{1,0:T(8,128)(2,1)S(1)}) custom-call(bf16[16,768]{1,0:T(8,128)(2,1)S(1)} %shard_map.122.rows_mine, bf16[16,768]{1,0:T(8,128)(2,1)S(1)} %collective-permute-done.4.rows_other, bf16[3,1536,768]{2,1,0:T(8,128)(2,1)S(1)} %get-tuple-element.67.w, f32[2,768]{1,0:T(2,128)S(1)} %get-tuple-element.68.gains, ...), custom_call_target="tpu_custom_call" | custom-call | flops 1207959552 | bytes 7919616 | tf_op jit(solution)/shard_map/pallas_call | solution.py:340
  60.8 1.7 %collective-permute-done.13.rest.refs_3_ = bf16[128,1536]{1,0:T(8,128)(2,1)S(1)} collective-permute-done((bf16[128,1536]{1,0:T(8,128)(2,1)S(1)}, bf16[128,1536]{1,0:T(8,128)(2,1)S(1)}, u32[]{:S(2)}, u32[]{:S(2)}) %collective-permute-start.13) | collective-permute-done | bytes 393248 | tf_op jit(solution)/shard_map/ppermute | solution.py:29
  62.4 2.5 %shard_map.134 = (bf16[128,768]{1,0:T(8,128)(2,1)S(1)}, bf16[128,768]{1,0:T(8,128)(2,1)S(1)}, bf16[256,768]{1,0:T(8,128)(2,1)S(1)}, bf16[256,768]{1,0:T(8,128)(2,1)S(1)}) custom-call(s32[128]{0:T(128)S(1)} %copy-done.2, bf16[16,768]{1,0:T(8,128)(2,1)S(1)} %shard_map.122.rows_mine, bf16[16,768]{1,0:T(8,128)(2,1)S(1)} %collective-permute-done.4.rows_other, ...), custom_call_target="tpu_custom_call" | custom-call | flops 2013265920 | bytes 10082304 | tf_op jit(solution)/shard_map/pallas_call | solution.py:340
  66.3 3.6 %collective-permute-start.17 = (bf16[128,768]{1,0:T(8,128)(2,1)S(1)}, bf16[128,768]{1,0:T(8,128)(2,1)S(1)}, u32[]{:S(2)}, u32[]{:S(2)}) collective-permute-start(bf16[128,768]{1,0:T(8,128)(2,1)S(1)} %shard_map.135.refs_5_), channel_id=1, source_target_pairs={{0,1},{1,0},{2,3},{3,2},{4,5},{5,4},{6,7},{7,6},{8,9},{9,8},{10,11... | collective-permute-start | bytes 589832 | tf_op jit(solution)/shard_map/ppermute | solution.py:29
  71.2 3.0 %collective-permute-done.14.a_other = bf16[128,768]{1,0:T(8,128)(2,1)S(1)} collective-permute-done((bf16[128,768]{1,0:T(8,128)(2,1)S(1)}, bf16[128,768]{1,0:T(8,128)(2,1)S(1)}, u32[]{:S(2)}, u32[]{:S(2)}) %collective-permute-start.14) | collective-permute-done | bytes 196640 | tf_op jit(solution)/shard_map/ppermute | solution.py:29
  75.3 3.7 %collective-permute-start.16 = (bf16[128,1536]{1,0:T(8,128)(2,1)S(1)}, bf16[128,1536]{1,0:T(8,128)(2,1)S(1)}, u32[]{:S(2)}, u32[]{:S(2)}) collective-permute-start(bf16[128,1536]{1,0:T(8,128)(2,1)S(1)} %shard_map.137.refs_0_), channel_id=1, source_target_pairs={{2,0},{3,1},{4,2},{5,3},{6,4},{7,5},{8,6},{9,7},{10,8},{11,9},{12,... | collective-permute-start | bytes 1179656 | tf_op jit(solution)/shard_map/ppermute | solution.py:29
  79.0 1.6 %collective-permute-done.17.a_other = bf16[128,768]{1,0:T(8,128)(2,1)S(1)} collective-permute-done((bf16[128,768]{1,0:T(8,128)(2,1)S(1)}, bf16[128,768]{1,0:T(8,128)(2,1)S(1)}, u32[]{:S(2)}, u32[]{:S(2)}) %collective-permute-start.17) | collective-permute-done | bytes 196640 | tf_op jit(solution)/shard_map/ppermute | solution.py:29
  81.6 2.1 %collective-permute-start.18 = (bf16[128,1536]{1,0:T(8,128)(2,1)S(1)}, bf16[128,1536]{1,0:T(8,128)(2,1)S(1)}, u32[]{:S(2)}, u32[]{:S(2)}) collective-permute-start(bf16[128,1536]{1,0:T(8,128)(2,1)S(1)} %shard_map.138.refs_1_), channel_id=1, source_target_pairs={{2,0},{3,1},{4,2},{5,3},{6,4},{7,5},{8,6},{9,7},{10,8},{11,9},{12,... | collective-permute-start | bytes 1179656 | tf_op jit(solution)/shard_map/ppermute | solution.py:29
  85.6 1.6 %shard_map.139 = (bf16[256,768]{1,0:T(8,128)(2,1)S(1)}, bf16[256,768]{1,0:T(8,128)(2,1)S(1)}) custom-call(bf16[16,768]{1,0:T(8,128)(2,1)S(1)} %shard_map.122.rows_mine, bf16[16,768]{1,0:T(8,128)(2,1)S(1)} %collective-permute-done.4.rows_other, bf16[3,1536,768]{2,1,0:T(8,128)(2,1)S(1)} %get-tuple-element.67.w, f32[2,768]{1,0:T(2,128)S(1)} %get-tuple-element.68.gains, ...), custom_call_target="tpu_custom_call" | custom-call | flops 1207959552 | bytes 7919616 | tf_op jit(solution)/shard_map/pallas_call | solution.py:340
  87.1 1.7 %collective-permute-done.18.rest.refs_3_ = bf16[128,1536]{1,0:T(8,128)(2,1)S(1)} collective-permute-done((bf16[128,1536]{1,0:T(8,128)(2,1)S(1)}, bf16[128,1536]{1,0:T(8,128)(2,1)S(1)}, u32[]{:S(2)}, u32[]{:S(2)}) %collective-permute-start.18) | collective-permute-done | bytes 393248 | tf_op jit(solution)/shard_map/ppermute | solution.py:29
  88.8 2.5 %shard_map.141 = (bf16[128,768]{1,0:T(8,128)(2,1)S(1)}, bf16[128,768]{1,0:T(8,128)(2,1)S(1)}, bf16[256,768]{1,0:T(8,128)(2,1)S(1)}, bf16[256,768]{1,0:T(8,128)(2,1)S(1)}) custom-call(s32[128]{0:T(128)S(1)} %copy-done.2, bf16[16,768]{1,0:T(8,128)(2,1)S(1)} %shard_map.122.rows_mine, bf16[16,768]{1,0:T(8,128)(2,1)S(1)} %collective-permute-done.4.rows_other, ...), custom_call_target="tpu_custom_call" | custom-call | flops 2013265920 | bytes 10082304 | tf_op jit(solution)/shard_map/pallas_call | solution.py:340
  94.1 2.2 %collective-permute-start.21 = (bf16[128,768]{1,0:T(8,128)(2,1)S(1)}, bf16[128,768]{1,0:T(8,128)(2,1)S(1)}, u32[]{:S(2)}, u32[]{:S(2)}) collective-permute-start(bf16[128,768]{1,0:T(8,128)(2,1)S(1)} %shard_map.142.refs_1_), channel_id=1, source_target_pairs={{0,1},{1,0},{2,3},{3,2},{4,5},{5,4},{6,7},{7,6},{8,9},{9,8},{10,11... | collective-permute-start | bytes 589832 | tf_op jit(solution)/shard_map/ppermute | solution.py:29
  96.8 4.0 %collective-permute-done.19.a_other = bf16[128,768]{1,0:T(8,128)(2,1)S(1)} collective-permute-done((bf16[128,768]{1,0:T(8,128)(2,1)S(1)}, bf16[128,768]{1,0:T(8,128)(2,1)S(1)}, u32[]{:S(2)}, u32[]{:S(2)}) %collective-permute-start.19) | collective-permute-done | bytes 196640 | tf_op jit(solution)/shard_map/ppermute | solution.py:29
  101.7 3.6 %collective-permute-start.20 = (bf16[128,768]{1,0:T(8,128)(2,1)S(1)}, bf16[128,768]{1,0:T(8,128)(2,1)S(1)}, u32[]{:S(2)}, u32[]{:S(2)}) collective-permute-start(bf16[128,768]{1,0:T(8,128)(2,1)S(1)} %get-tuple-element.123), channel_id=1, source_target_pairs={{2,0},{3,1},{4,2},{5,3},{6,4},{7,5},{8,6},{9,7},{10,8},{11,9},{12,... | collective-permute-start | bytes 589832 | tf_op jit(solution)/shard_map/ppermute | solution.py:29
  106.2 2.9 %collective-permute-start.22 = (bf16[128,768]{1,0:T(8,128)(2,1)S(1)}, bf16[128,768]{1,0:T(8,128)(2,1)S(1)}, u32[]{:S(2)}, u32[]{:S(2)}) collective-permute-start(bf16[128,768]{1,0:T(8,128)(2,1)S(1)} %get-tuple-element.126), channel_id=1, source_target_pairs={{2,0},{3,1},{4,2},{5,3},{6,4},{7,5},{8,6},{9,7},{10,8},{11,9},{12,... | collective-permute-start | bytes 589832 | tf_op jit(solution)/shard_map/ppermute | solution.py:29
  109.2 3.1 %collective-permute-done.22.advanced = bf16[128,768]{1,0:T(8,128)(2,1)S(1)} collective-permute-done((bf16[128,768]{1,0:T(8,128)(2,1)S(1)}, bf16[128,768]{1,0:T(8,128)(2,1)S(1)}, u32[]{:S(2)}, u32[]{:S(2)}) %collective-permute-start.22) | collective-permute-done | bytes 196640 | tf_op jit(solution)/shard_map/ppermute | solution.py:29
  (48 shorter events, 27.0 us)
Async XLA Ops:
  0.6 13.3 %collective-permute-start.5 = (bf16[256,768]{1,0:T(8,128)(2,1)}, bf16[256,768]{1,0:T(8,128)(2,1)S(1)}, u32[]{:S(2)}, u32[]{:S(2)}) collective-permute-start(bf16[256,768]{1,0:T(8,128)(2,1)} %refs_0_.1), channel_id=1, source_target_pairs={{0,1},{1,0},{2,3},{3,2},{4,5},{5,4},{6,7},{7,6},{8,9},{9,8},{10,11... | collective-permute-start | bytes 1179656 | tf_op jit(solution)/shard_map/ppermute | solution.py:29
  3.4 16.7 %collective-permute-start = (bf16[96,1536]{1,0:T(8,128)(2,1)S(1)}, bf16[96,1536]{1,0:T(8,128)(2,1)S(1)}, u32[]{:S(2)}, u32[]{:S(2)}) collective-permute-start(bf16[96,1536]{1,0:T(8,128)(2,1)S(1)} %constant_dynamic-slice_fusion), channel_id=1, source_target_pairs={{0,5},{1,4},{2,7},{3,6},{4,1},{5,0},{6,3},{7,2},{8,13},{9,12},{10,... | collective-permute-start | bytes 884744 | tf_op jit(solution)/shard_map/ppermute | solution.py:29
  5.7 8.3 %collective-permute-start.4 = (bf16[16,768]{1,0:T(8,128)(2,1)S(1)}, bf16[16,768]{1,0:T(8,128)(2,1)S(1)}, u32[]{:S(2)}, u32[]{:S(2)}) collective-permute-start(bf16[16,768]{1,0:T(8,128)(2,1)S(1)} %shard_map.122.rows_mine), channel_id=1, source_target_pairs={{0,1},{1,0},{2,3},{3,2},{4,5},{5,4},{6,7},{7,6},{8,9},{9,8},{10,11... | collective-permute-start | bytes 73736 | tf_op jit(solution)/shard_map/ppermute | solution.py:29
  7.7 8.2 %copy-start = (bf16[256,768]{1,0:T(8,128)(2,1)S(1)}, bf16[256,768]{1,0:T(8,128)(2,1)}, u32[]{:S(2)}) copy-start(bf16[256,768]{1,0:T(8,128)(2,1)} %refs_0_.1) | copy-start | bytes 1179652
  13.9 16.4 %collective-permute-start.7 = (bf16[256,768]{1,0:T(8,128)(2,1)S(1)}, bf16[256,768]{1,0:T(8,128)(2,1)S(1)}, u32[]{:S(2)}, u32[]{:S(2)}) collective-permute-start(bf16[256,768]{1,0:T(8,128)(2,1)S(1)} %collective-permute-done.5.other.refs_1_), channel_id=1, source_target_pairs={{0,2},{1,3},{2,4},{3,5},{4,6},{5,7},{6,8},{7,9},{8,10},{9,11},{10,... | collective-permute-start | bytes 1179656 | tf_op jit(solution)/shard_map/ppermute | solution.py:29
  15.8 14.6 %collective-permute-start.6 = (bf16[256,768]{1,0:T(8,128)(2,1)S(1)}, bf16[256,768]{1,0:T(8,128)(2,1)S(1)}, u32[]{:S(2)}, u32[]{:S(2)}) collective-permute-start(bf16[256,768]{1,0:T(8,128)(2,1)S(1)} %copy-done), channel_id=1, source_target_pairs={{0,2},{1,3},{2,4},{3,5},{4,6},{5,7},{6,8},{7,9},{8,10},{9,11},{10,... | collective-permute-start | bytes 1179656 | tf_op jit(solution)/shard_map/ppermute | solution.py:29
  20.1 16.6 %collective-permute-start.1 = (bf16[96,1536]{1,0:T(8,128)(2,1)S(1)}, bf16[96,1536]{1,0:T(8,128)(2,1)S(1)}, u32[]{:S(2)}, u32[]{:S(2)}) collective-permute-start(bf16[96,1536]{1,0:T(8,128)(2,1)S(1)} %collective-permute-done.own), channel_id=1, source_target_pairs={{0,64},{1,65},{2,66},{3,67},{4,68},{5,69},{6,70},{7,71},{8,72},{9,... | collective-permute-start | bytes 884744 | tf_op jit(solution)/shard_map/ppermute | solution.py:29
  21.7 15.0 %collective-permute-start.2 = (bf16[96,1536]{1,0:T(8,128)(2,1)S(1)}, bf16[96,1536]{1,0:T(8,128)(2,1)S(1)}, u32[]{:S(2)}, u32[]{:S(2)}) collective-permute-start(bf16[96,1536]{1,0:T(8,128)(2,1)S(1)} %collective-permute-done.own), channel_id=1, source_target_pairs={{0,192},{1,193},{2,194},{3,195},{4,196},{5,197},{6,198},{7,199},{8... | collective-permute-start | bytes 884744 | tf_op jit(solution)/shard_map/ppermute | solution.py:29
  22.2 14.5 %collective-permute-start.3 = (bf16[96,1536]{1,0:T(8,128)(2,1)S(1)}, bf16[96,1536]{1,0:T(8,128)(2,1)S(1)}, u32[]{:S(2)}, u32[]{:S(2)}) collective-permute-start(bf16[96,1536]{1,0:T(8,128)(2,1)S(1)} %collective-permute-done.own), channel_id=1, source_target_pairs={{0,56},{1,57},{2,58},{3,59},{4,60},{5,61},{6,62},{7,63},{8,0},{9,1... | collective-permute-start | bytes 884744 | tf_op jit(solution)/shard_map/ppermute | solution.py:29
  30.3 1.8 %copy-start.2 = (s32[128]{0:T(128)S(1)}, s32[128]{0:T(128)}, u32[]{:S(2)}) copy-start(s32[128]{0:T(128)} %starts.11) | copy-start | bytes 1540
  36.8 5.0 %copy-start.1 = (s32[128]{0:T(128)S(1)}, s32[128]{0:T(128)}, u32[]{:S(2)}) copy-start(s32[128]{0:T(128)} %levels.15) | copy-start | bytes 1540
  36.9 9.4 %collective-permute-start.8 = (bf16[4,96,1536]{2,1,0:T(8,128)(2,1)S(1)}, bf16[4,96,1536]{2,1,0:T(8,128)(2,1)S(1)}, u32[]{:S(2)}, u32[]{:S(2)}) collective-permute-start(bf16[4,96,1536]{2,1,0:T(8,128)(2,1)S(1)} %pad_maximum_fusion), channel_id=1, source_target_pairs={{0,2},{1,3},{2,0},{3,1},{4,6},{5,7},{6,4},{7,5},{8,10},{9,11},{10,... | collective-permute-start | bytes 3538952 | tf_op jit(solution)/shard_map/ppermute | solution.py:29
  37.0 9.3 %collective-permute-start.9 = (bf16[128,768]{1,0:T(8,128)(2,1)S(1)}, bf16[128,768]{1,0:T(8,128)(2,1)S(1)}, u32[]{:S(2)}, u32[]{:S(2)}) collective-permute-start(bf16[128,768]{1,0:T(8,128)(2,1)S(1)} %shard_map.126.refs_2_), channel_id=1, source_target_pairs={{0,1},{1,0},{2,3},{3,2},{4,5},{5,4},{6,7},{7,6},{8,9},{9,8},{10,11... | collective-permute-start | bytes 589832 | tf_op jit(solution)/shard_map/ppermute | solution.py:29
  39.1 15.1 %collective-permute-start.12 = (bf16[128,768]{1,0:T(8,128)(2,1)S(1)}, bf16[128,768]{1,0:T(8,128)(2,1)S(1)}, u32[]{:S(2)}, u32[]{:S(2)}) collective-permute-start(bf16[128,768]{1,0:T(8,128)(2,1)S(1)} %shard_map.128.refs_3_), channel_id=1, source_target_pairs={{0,1},{1,0},{2,3},{3,2},{4,5},{5,4},{6,7},{7,6},{8,9},{9,8},{10,11... | collective-permute-start | bytes 589832 | tf_op jit(solution)/shard_map/ppermute | solution.py:29
  47.5 9.7 %collective-permute-start.11 = (bf16[128,1536]{1,0:T(8,128)(2,1)S(1)}, bf16[128,1536]{1,0:T(8,128)(2,1)S(1)}, u32[]{:S(2)}, u32[]{:S(2)}) collective-permute-start(bf16[128,1536]{1,0:T(8,128)(2,1)S(1)} %shard_map.130.refs_0_), channel_id=1, source_target_pairs={{2,0},{3,1},{4,2},{5,3},{6,4},{7,5},{8,6},{9,7},{10,8},{11,9},{12,... | collective-permute-start | bytes 1179656 | tf_op jit(solution)/shard_map/ppermute | solution.py:29
  50.9 8.6 %collective-permute-start.10 = (bf16[256,768]{1,0:T(8,128)(2,1)S(1)}, bf16[256,768]{1,0:T(8,128)(2,1)S(1)}, u32[]{:S(2)}, u32[]{:S(2)}) collective-permute-start(bf16[256,768]{1,0:T(8,128)(2,1)S(1)} %get-tuple-element.83.fresh.refs_0_), channel_id=1, source_target_pairs={{250,255},{251,254}} | collective-permute-start | bytes 1179656 | tf_op jit(solution)/shard_map/ppermute | solution.py:29
  55.2 7.2 %collective-permute-start.13 = (bf16[128,1536]{1,0:T(8,128)(2,1)S(1)}, bf16[128,1536]{1,0:T(8,128)(2,1)S(1)}, u32[]{:S(2)}, u32[]{:S(2)}) collective-permute-start(bf16[128,1536]{1,0:T(8,128)(2,1)S(1)} %shard_map.131.refs_1_), channel_id=1, source_target_pairs={{2,0},{3,1},{4,2},{5,3},{6,4},{7,5},{8,6},{9,7},{10,8},{11,9},{12,... | collective-permute-start | bytes 1179656 | tf_op jit(solution)/shard_map/ppermute | solution.py:29
  58.8 15.5 %collective-permute-start.15 = (bf16[256,768]{1,0:T(8,128)(2,1)S(1)}, bf16[256,768]{1,0:T(8,128)(2,1)S(1)}, u32[]{:S(2)}, u32[]{:S(2)}) collective-permute-start(bf16[256,768]{1,0:T(8,128)(2,1)S(1)} %get-tuple-element.105.fresh.refs_0_), channel_id=1, source_target_pairs={{250,255},{251,254}} | collective-permute-start | bytes 1179656 | tf_op jit(solution)/shard_map/ppermute | solution.py:29
  64.9 9.4 %collective-permute-start.14 = (bf16[128,768]{1,0:T(8,128)(2,1)S(1)}, bf16[128,768]{1,0:T(8,128)(2,1)S(1)}, u32[]{:S(2)}, u32[]{:S(2)}) collective-permute-start(bf16[128,768]{1,0:T(8,128)(2,1)S(1)} %get-tuple-element.97.refs_4_), channel_id=1, source_target_pairs={{0,1},{1,0},{2,3},{3,2},{4,5},{5,4},{6,7},{7,6},{8,9},{9,8},{10,11... | collective-permute-start | bytes 589832 | tf_op jit(solution)/shard_map/ppermute | solution.py:29
  66.3 14.3 %collective-permute-start.17 = (bf16[128,768]{1,0:T(8,128)(2,1)S(1)}, bf16[128,768]{1,0:T(8,128)(2,1)S(1)}, u32[]{:S(2)}, u32[]{:S(2)}) collective-permute-start(bf16[128,768]{1,0:T(8,128)(2,1)S(1)} %shard_map.135.refs_5_), channel_id=1, source_target_pairs={{0,1},{1,0},{2,3},{3,2},{4,5},{5,4},{6,7},{7,6},{8,9},{9,8},{10,11... | collective-permute-start | bytes 589832 | tf_op jit(solution)/shard_map/ppermute | solution.py:29
  75.3 8.9 %collective-permute-start.16 = (bf16[128,1536]{1,0:T(8,128)(2,1)S(1)}, bf16[128,1536]{1,0:T(8,128)(2,1)S(1)}, u32[]{:S(2)}, u32[]{:S(2)}) collective-permute-start(bf16[128,1536]{1,0:T(8,128)(2,1)S(1)} %shard_map.137.refs_0_), channel_id=1, source_target_pairs={{2,0},{3,1},{4,2},{5,3},{6,4},{7,5},{8,6},{9,7},{10,8},{11,9},{12,... | collective-permute-start | bytes 1179656 | tf_op jit(solution)/shard_map/ppermute | solution.py:29
  81.6 7.2 %collective-permute-start.18 = (bf16[128,1536]{1,0:T(8,128)(2,1)S(1)}, bf16[128,1536]{1,0:T(8,128)(2,1)S(1)}, u32[]{:S(2)}, u32[]{:S(2)}) collective-permute-start(bf16[128,1536]{1,0:T(8,128)(2,1)S(1)} %shard_map.138.refs_1_), channel_id=1, source_target_pairs={{2,0},{3,1},{4,2},{5,3},{6,4},{7,5},{8,6},{9,7},{10,8},{11,9},{12,... | collective-permute-start | bytes 1179656 | tf_op jit(solution)/shard_map/ppermute | solution.py:29
  91.3 9.4 %collective-permute-start.19 = (bf16[128,768]{1,0:T(8,128)(2,1)S(1)}, bf16[128,768]{1,0:T(8,128)(2,1)S(1)}, u32[]{:S(2)}, u32[]{:S(2)}) collective-permute-start(bf16[128,768]{1,0:T(8,128)(2,1)S(1)} %get-tuple-element.115.refs_0_), channel_id=1, source_target_pairs={{0,1},{1,0},{2,3},{3,2},{4,5},{5,4},{6,7},{7,6},{8,9},{9,8},{10,11... | collective-permute-start | bytes 589832 | tf_op jit(solution)/shard_map/ppermute | solution.py:29
  94.1 11.1 %collective-permute-start.21 = (bf16[128,768]{1,0:T(8,128)(2,1)S(1)}, bf16[128,768]{1,0:T(8,128)(2,1)S(1)}, u32[]{:S(2)}, u32[]{:S(2)}) collective-permute-start(bf16[128,768]{1,0:T(8,128)(2,1)S(1)} %shard_map.142.refs_1_), channel_id=1, source_target_pairs={{0,1},{1,0},{2,3},{3,2},{4,5},{5,4},{6,7},{7,6},{8,9},{9,8},{10,11... | collective-permute-start | bytes 589832 | tf_op jit(solution)/shard_map/ppermute | solution.py:29
  101.7 7.5 %collective-permute-start.20 = (bf16[128,768]{1,0:T(8,128)(2,1)S(1)}, bf16[128,768]{1,0:T(8,128)(2,1)S(1)}, u32[]{:S(2)}, u32[]{:S(2)}) collective-permute-start(bf16[128,768]{1,0:T(8,128)(2,1)S(1)} %get-tuple-element.123), channel_id=1, source_target_pairs={{2,0},{3,1},{4,2},{5,3},{6,4},{7,5},{8,6},{9,7},{10,8},{11,9},{12,... | collective-permute-start | bytes 589832 | tf_op jit(solution)/shard_map/ppermute | solution.py:29
  106.2 6.1 %collective-permute-start.22 = (bf16[128,768]{1,0:T(8,128)(2,1)S(1)}, bf16[128,768]{1,0:T(8,128)(2,1)S(1)}, u32[]{:S(2)}, u32[]{:S(2)}) collective-permute-start(bf16[128,768]{1,0:T(8,128)(2,1)S(1)} %get-tuple-element.126), channel_id=1, source_target_pairs={{2,0},{3,1},{4,2},{5,3},{6,4},{7,5},{8,6},{9,7},{10,8},{11,9},{12,... | collective-permute-start | bytes 589832 | tf_op jit(solution)/shard_map/ppermute | solution.py:29

commit v7 on v6

--- a/solution.py
+++ b/solution.py
@@ -58,7 +58,7 @@
 
 
 def table_row(rows, n):
-    mine, other = (r[n : n + 1, :].astype(jnp.float32) for r in rows)
+    mine, other = (r[...].astype(jnp.float32)[n : n + 1, :] for r in rows)
     return ordered(mine, other)
 
 
@@ -283,7 +283,7 @@
 
 
 def last_mine_kernel(rows_mine, w_mine, *refs):
-    gate = rows_mine[GATE : GATE + 1, :].astype(jnp.float32)
+    gate = rows_mine[...].astype(jnp.float32)[GATE : GATE + 1, :]
     for chunk, base in zip(refs[:CHUNKS], refs[CHUNKS:]):
         base[...] = gate * dot(chunk[...], w_mine[:, own_features(base.shape[1])])
 
@@ -293,7 +293,7 @@
     count, width = new.shape
     low, high = halves_of(kind, x, row, count)
     held = jnp.where(lax.axis_index("heads") == 0, low, high).astype(jnp.float32)
-    gate = rows_mine[GATE : GATE + 1, :].astype(jnp.float32)
+    gate = rows_mine[...].astype(jnp.float32)[GATE : GATE + 1, :]
     velocity = base[...] + gate * dot(a_other[...], w_other[:, own_features(width)])
     velocity_out[...] = velocity.astype(jnp.bfloat16)
     new[...] = (held + step_size_of(levels) * velocity).astype(jnp.bfloat16)
@@ -484,7 +484,7 @@
             )
         received[0] = after(received[0], *bases, *waits)
         if step == 0:
-            w_other = other_projection(piece, parts[0], w_out.shape)
+            w_other = other_projection(piece, parts[1], w_out.shape)
         if step < STEPS - 1:
             new = []
             for n in range(CHUNKS):

time: 114 us -> 114 us (level)
  starting transfers between devices: 48.2 us -> 51.6 us
  waiting for transfers between devices: 27.9 us -> 24.7 us
    ppermute x23, starting transfers between devices: 48.2 us -> 51.6 us  [routed(): return lax.ppermute(block, AXES, pairs)]
    ppermute x23, waiting for transfers between devices: 27.9 us -> 24.7 us  [routed(): return lax.ppermute(block, AXES, pairs)]
  transfers between devices with their start and end apart: 23 -> 23, of which waited for: 13 -> 12; matrix products, arithmetic and copies ran while one was open for 1% -> 1% of each run, Pallas kernels for 28% -> 28%
where the time goes in v7:
time: 114 us
  starting transfers between devices  51.6 us (45%)
  Pallas kernels  35 us (31%)
  waiting for transfers between devices  24.7 us (22%)
    ppermute x23, starting transfers between devices, routed(): return lax.ppermute(block, AXES, pairs)  51.6 us
    pallas_call x24, Pallas kernels, kernel_call(): pl.pallas_call(kernel, cost_estimate=pl.CostEstimate(flops=2 * products,...  29.8 us
    ppermute x23, waiting for transfers between devices, routed(): return lax.ppermute(block, AXES, pairs)  24.7 us
    pallas_call x1, Pallas kernels, stage_call(): pl.pallas_call(stage_kernel, out_shape=(pltpu.VMEM(w.shape, w.dtype), plt...  4.05 us
  transfers between devices with their start and end apart: 23, of which 12 were waited for; matrix products, arithmetic and copies ran while one was open for 1% of the time, Pallas kernels for 28%

profile of v7, /device:TPU:12, one launch (start us, length us, event | category | flops | bytes accessed | tf_op | source)
XLA Modules:
  0.0 113.5 jit_solution(4613461223299023899)
XLA Ops:
  3.4 2.2 %collective-permute-start = (bf16[96,1536]{1,0:T(8,128)(2,1)S(1)}, bf16[96,1536]{1,0:T(8,128)(2,1)S(1)}, u32[]{:S(2)}, u32[]{:S(2)}) collective-permute-start(bf16[96,1536]{1,0:T(8,128)(2,1)S(1)} %constant_dynamic-slice_fusion), channel_id=1, source_target_pairs={{0,5},{1,4},{2,7},{3,6},{4,1},{5,0},{6,3},{7,2},{8,13},{9,12},{10,... | collective-permute-start | bytes 884744 | tf_op jit(solution)/shard_map/ppermute | solution.py:29
  5.7 2.0 %collective-permute-start.4 = (bf16[16,768]{1,0:T(8,128)(2,1)S(1)}, bf16[16,768]{1,0:T(8,128)(2,1)S(1)}, u32[]{:S(2)}, u32[]{:S(2)}) collective-permute-start(bf16[16,768]{1,0:T(8,128)(2,1)S(1)} %shard_map.122.rows_mine), channel_id=1, source_target_pairs={{0,1},{1,0},{2,3},{3,2},{4,5},{5,4},{6,7},{7,6},{8,9},{9,8},{10,11... | collective-permute-start | bytes 73736 | tf_op jit(solution)/shard_map/ppermute | solution.py:29
  7.7 4.0 %shard_map.123 = (bf16[3,1536,768]{2,1,0:T(8,128)(2,1)S(1)}, f32[2,768]{1,0:T(2,128)S(1)}, bf16[256,768]{1,0:T(8,128)(2,1)S(1)}, bf16[256,768]{1,0:T(8,128)(2,1)...) custom-call(bf16[3,1536,768]{2,1,0:T(8,128)(2,1)} %bitcast.9, f32[768]{0:T(1024)} %q_hbm.1, f32[768]{0:T(1024)} %k_hbm.1, ...), custom_call_target="tpu_custom_call" | custom-call | tf_op jit(solution)/shard_map/pallas_call | solution.py:134
  11.7 2.2 %collective-permute-done.4.rows_other = bf16[16,768]{1,0:T(8,128)(2,1)S(1)} collective-permute-done((bf16[16,768]{1,0:T(8,128)(2,1)S(1)}, bf16[16,768]{1,0:T(8,128)(2,1)S(1)}, u32[]{:S(2)}, u32[]{:S(2)}) %collective-permute-start.4) | collective-permute-done | bytes 24608 | tf_op jit(solution)/shard_map/ppermute | solution.py:29
  13.9 1.9 %collective-permute-start.7 = (bf16[256,768]{1,0:T(8,128)(2,1)S(1)}, bf16[256,768]{1,0:T(8,128)(2,1)S(1)}, u32[]{:S(2)}, u32[]{:S(2)}) collective-permute-start(bf16[256,768]{1,0:T(8,128)(2,1)S(1)} %collective-permute-done.5.other.refs_1_), channel_id=1, source_target_pairs={{0,2},{1,3},{2,4},{3,5},{4,6},{5,7},{6,8},{7,9},{8,10},{9,11},{10,... | collective-permute-start | bytes 1179656 | tf_op jit(solution)/shard_map/ppermute | solution.py:29
  15.8 3.2 %collective-permute-start.6 = (bf16[256,768]{1,0:T(8,128)(2,1)S(1)}, bf16[256,768]{1,0:T(8,128)(2,1)S(1)}, u32[]{:S(2)}, u32[]{:S(2)}) collective-permute-start(bf16[256,768]{1,0:T(8,128)(2,1)S(1)} %copy-done), channel_id=1, source_target_pairs={{0,2},{1,3},{2,4},{3,5},{4,6},{5,7},{6,8},{7,9},{8,10},{9,11},{10,... | collective-permute-start | bytes 1179656 | tf_op jit(solution)/shard_map/ppermute | solution.py:29
  20.1 1.6 %collective-permute-start.1 = (bf16[96,1536]{1,0:T(8,128)(2,1)S(1)}, bf16[96,1536]{1,0:T(8,128)(2,1)S(1)}, u32[]{:S(2)}, u32[]{:S(2)}) collective-permute-start(bf16[96,1536]{1,0:T(8,128)(2,1)S(1)} %collective-permute-done.own), channel_id=1, source_target_pairs={{0,64},{1,65},{2,66},{3,67},{4,68},{5,69},{6,70},{7,71},{8,72},{9,... | collective-permute-start | bytes 884744 | tf_op jit(solution)/shard_map/ppermute | solution.py:29
  22.2 5.9 %collective-permute-start.3 = (bf16[96,1536]{1,0:T(8,128)(2,1)S(1)}, bf16[96,1536]{1,0:T(8,128)(2,1)S(1)}, u32[]{:S(2)}, u32[]{:S(2)}) collective-permute-start(bf16[96,1536]{1,0:T(8,128)(2,1)S(1)} %collective-permute-done.own), channel_id=1, source_target_pairs={{0,56},{1,57},{2,58},{3,59},{4,60},{5,61},{6,62},{7,63},{8,0},{9,1... | collective-permute-start | bytes 884744 | tf_op jit(solution)/shard_map/ppermute | solution.py:29
  28.0 2.3 %shard_map.124 = (bf16[128,768]{1,0:T(8,128)(2,1)S(1)}, bf16[128,768]{1,0:T(8,128)(2,1)S(1)}, bf16[256,768]{1,0:T(8,128)(2,1)S(1)}, bf16[256,768]{1,0:T(8,128)(2,1)S(1)}) custom-call(bf16[16,768]{1,0:T(8,128)(2,1)S(1)} %shard_map.122.rows_mine, bf16[16,768]{1,0:T(8,128)(2,1)S(1)} %collective-permute-done.4.rows_other, ...), custom_call_target="tpu_custom_call" | custom-call | flops 1811939328 | bytes 7919616 | tf_op jit(solution)/shard_map/pallas_call | solution.py:340
  30.5 1.6 %shard_map.125 = (bf16[256,768]{1,0:T(8,128)(2,1)S(1)}, bf16[256,768]{1,0:T(8,128)(2,1)S(1)}) custom-call(bf16[16,768]{1,0:T(8,128)(2,1)S(1)} %shard_map.122.rows_mine, bf16[16,768]{1,0:T(8,128)(2,1)S(1)} %collective-permute-done.4.rows_other, bf16[3,1536,768]{2,1,0:T(8,128)(2,1)S(1)} %get-tuple-element.67.w, f32[2,768]{1,0:T(2,128)S(1)} %get-tuple-element.68.gains, ...), custom_call_target="tpu_custom_call" | custom-call | flops 1207959552 | bytes 7919616 | tf_op jit(solution)/shard_map/pallas_call | solution.py:340
  34.6 2.1 %collective-permute-done.1.back = bf16[96,1536]{1,0:T(8,128)(2,1)S(1)} collective-permute-done((bf16[96,1536]{1,0:T(8,128)(2,1)S(1)}, bf16[96,1536]{1,0:T(8,128)(2,1)S(1)}, u32[]{:S(2)}, u32[]{:S(2)}) %collective-permute-start.1) | collective-permute-done | bytes 294944 | tf_op jit(solution)/shard_map/ppermute | solution.py:29
  37.8 2.7 %collective-permute-start.12 = (bf16[128,768]{1,0:T(8,128)(2,1)S(1)}, bf16[128,768]{1,0:T(8,128)(2,1)S(1)}, u32[]{:S(2)}, u32[]{:S(2)}) collective-permute-start(bf16[128,768]{1,0:T(8,128)(2,1)S(1)} %shard_map.127.refs_3_), channel_id=1, source_target_pairs={{0,1},{1,0},{2,3},{3,2},{4,5},{5,4},{6,7},{7,6},{8,9},{9,8},{10,11... | collective-permute-start | bytes 589832 | tf_op jit(solution)/shard_map/ppermute | solution.py:29
  41.9 4.3 %collective-permute-done.9.a_other = bf16[128,768]{1,0:T(8,128)(2,1)S(1)} collective-permute-done((bf16[128,768]{1,0:T(8,128)(2,1)S(1)}, bf16[128,768]{1,0:T(8,128)(2,1)S(1)}, u32[]{:S(2)}, u32[]{:S(2)}) %collective-permute-start.9) | collective-permute-done | bytes 196640 | tf_op jit(solution)/shard_map/ppermute | solution.py:29
  47.5 3.4 %collective-permute-start.11 = (bf16[128,1536]{1,0:T(8,128)(2,1)S(1)}, bf16[128,1536]{1,0:T(8,128)(2,1)S(1)}, u32[]{:S(2)}, u32[]{:S(2)}) collective-permute-start(bf16[128,1536]{1,0:T(8,128)(2,1)S(1)} %shard_map.130.refs_0_), channel_id=1, source_target_pairs={{2,0},{3,1},{4,2},{5,3},{6,4},{7,5},{8,6},{9,7},{10,8},{11,9},{12,... | collective-permute-start | bytes 1179656 | tf_op jit(solution)/shard_map/ppermute | solution.py:29
  52.8 3.3 %collective-permute-start.13 = (bf16[128,1536]{1,0:T(8,128)(2,1)S(1)}, bf16[128,1536]{1,0:T(8,128)(2,1)S(1)}, u32[]{:S(2)}, u32[]{:S(2)}) collective-permute-start(bf16[128,1536]{1,0:T(8,128)(2,1)S(1)} %shard_map.131.refs_1_), channel_id=1, source_target_pairs={{2,0},{3,1},{4,2},{5,3},{6,4},{7,5},{8,6},{9,7},{10,8},{11,9},{12,... | collective-permute-start | bytes 1179656 | tf_op jit(solution)/shard_map/ppermute | solution.py:29
  56.1 1.6 %shard_map.132 = (bf16[256,768]{1,0:T(8,128)(2,1)S(1)}, bf16[256,768]{1,0:T(8,128)(2,1)S(1)}) custom-call(bf16[16,768]{1,0:T(8,128)(2,1)S(1)} %shard_map.122.rows_mine, bf16[16,768]{1,0:T(8,128)(2,1)S(1)} %collective-permute-done.4.rows_other, bf16[3,1536,768]{2,1,0:T(8,128)(2,1)S(1)} %get-tuple-element.67.w, f32[2,768]{1,0:T(2,128)S(1)} %get-tuple-element.68.gains, ...), custom_call_target="tpu_custom_call" | custom-call | flops 1207959552 | bytes 7919616 | tf_op jit(solution)/shard_map/pallas_call | solution.py:340
  59.7 1.6 %collective-permute-done.13.rest.refs_3_ = bf16[128,1536]{1,0:T(8,128)(2,1)S(1)} collective-permute-done((bf16[128,1536]{1,0:T(8,128)(2,1)S(1)}, bf16[128,1536]{1,0:T(8,128)(2,1)S(1)}, u32[]{:S(2)}, u32[]{:S(2)}) %collective-permute-start.13) | collective-permute-done | bytes 393248 | tf_op jit(solution)/shard_map/ppermute | solution.py:29
  61.3 2.5 %shard_map.134 = (bf16[128,768]{1,0:T(8,128)(2,1)S(1)}, bf16[128,768]{1,0:T(8,128)(2,1)S(1)}, bf16[256,768]{1,0:T(8,128)(2,1)S(1)}, bf16[256,768]{1,0:T(8,128)(2,1)S(1)}) custom-call(s32[128]{0:T(128)S(1)} %copy-done.2, bf16[16,768]{1,0:T(8,128)(2,1)S(1)} %shard_map.122.rows_mine, bf16[16,768]{1,0:T(8,128)(2,1)S(1)} %collective-permute-done.4.rows_other, ...), custom_call_target="tpu_custom_call" | custom-call | flops 2013265920 | bytes 10082304 | tf_op jit(solution)/shard_map/pallas_call | solution.py:340
  65.9 2.8 %collective-permute-start.17 = (bf16[128,768]{1,0:T(8,128)(2,1)S(1)}, bf16[128,768]{1,0:T(8,128)(2,1)S(1)}, u32[]{:S(2)}, u32[]{:S(2)}) collective-permute-start(bf16[128,768]{1,0:T(8,128)(2,1)S(1)} %shard_map.135.refs_5_), channel_id=1, source_target_pairs={{0,1},{1,0},{2,3},{3,2},{4,5},{5,4},{6,7},{7,6},{8,9},{9,8},{10,11... | collective-permute-start | bytes 589832 | tf_op jit(solution)/shard_map/ppermute | solution.py:29
  68.8 1.4 %shard_map.136 = (f32[128,1536]{1,0:T(8,128)S(1)}, f32[128,1536]{1,0:T(8,128)S(1)}) custom-call(s32[128]{0:T(128)S(1)} %copy-done.1, bf16[16,768]{1,0:T(8,128)(2,1)S(1)} %shard_map.122.rows_mine, bf16[16,768]{1,0:T(8,128)(2,1)S(1)} %collective-permute-done.4.rows_other, bf16[768,1536]{1,0:T(8,128)(2,1)S(1)} %get-tuple-element.83.w_mine, ...), custom_call_target="tpu_custom_call" | custom-call | flops 603979776 | bytes 4374528 | tf_op jit(solution)/shard_map/pallas_call | solution.py:340
  70.1 3.1 %collective-permute-done.14.a_other = bf16[128,768]{1,0:T(8,128)(2,1)S(1)} collective-permute-done((bf16[128,768]{1,0:T(8,128)(2,1)S(1)}, bf16[128,768]{1,0:T(8,128)(2,1)S(1)}, u32[]{:S(2)}, u32[]{:S(2)}) %collective-permute-start.14) | collective-permute-done | bytes 196640 | tf_op jit(solution)/shard_map/ppermute | solution.py:29
  74.2 4.6 %collective-permute-start.16 = (bf16[128,1536]{1,0:T(8,128)(2,1)S(1)}, bf16[128,1536]{1,0:T(8,128)(2,1)S(1)}, u32[]{:S(2)}, u32[]{:S(2)}) collective-permute-start(bf16[128,1536]{1,0:T(8,128)(2,1)S(1)} %shard_map.137.refs_0_), channel_id=1, source_target_pairs={{2,0},{3,1},{4,2},{5,3},{6,4},{7,5},{8,6},{9,7},{10,8},{11,9},{12,... | collective-permute-start | bytes 1179656 | tf_op jit(solution)/shard_map/ppermute | solution.py:29
  79.9 2.1 %collective-permute-start.18 = (bf16[128,1536]{1,0:T(8,128)(2,1)S(1)}, bf16[128,1536]{1,0:T(8,128)(2,1)S(1)}, u32[]{:S(2)}, u32[]{:S(2)}) collective-permute-start(bf16[128,1536]{1,0:T(8,128)(2,1)S(1)} %shard_map.138.refs_1_), channel_id=1, source_target_pairs={{2,0},{3,1},{4,2},{5,3},{6,4},{7,5},{8,6},{9,7},{10,8},{11,9},{12,... | collective-permute-start | bytes 1179656 | tf_op jit(solution)/shard_map/ppermute | solution.py:29
  82.0 2.1 %collective-permute-done.16.chunk.first.refs_2_ = bf16[128,1536]{1,0:T(8,128)(2,1)S(1)} collective-permute-done((bf16[128,1536]{1,0:T(8,128)(2,1)S(1)}, bf16[128,1536]{1,0:T(8,128)(2,1)S(1)}, u32[]{:S(2)}, u32[]{:S(2)}) %collective-permute-start.16) | collective-permute-done | bytes 393248 | tf_op jit(solution)/shard_map/ppermute | solution.py:29
  85.4 1.6 %shard_map.139 = (bf16[256,768]{1,0:T(8,128)(2,1)S(1)}, bf16[256,768]{1,0:T(8,128)(2,1)S(1)}) custom-call(bf16[16,768]{1,0:T(8,128)(2,1)S(1)} %shard_map.122.rows_mine, bf16[16,768]{1,0:T(8,128)(2,1)S(1)} %collective-permute-done.4.rows_other, bf16[3,1536,768]{2,1,0:T(8,128)(2,1)S(1)} %get-tuple-element.67.w, f32[2,768]{1,0:T(2,128)S(1)} %get-tuple-element.68.gains, ...), custom_call_target="tpu_custom_call" | custom-call | flops 1207959552 | bytes 7919616 | tf_op jit(solution)/shard_map/pallas_call | solution.py:340
  88.3 2.5 %shard_map.141 = (bf16[128,768]{1,0:T(8,128)(2,1)S(1)}, bf16[128,768]{1,0:T(8,128)(2,1)S(1)}, bf16[256,768]{1,0:T(8,128)(2,1)S(1)}, bf16[256,768]{1,0:T(8,128)(2,1)S(1)}) custom-call(s32[128]{0:T(128)S(1)} %copy-done.2, bf16[16,768]{1,0:T(8,128)(2,1)S(1)} %shard_map.122.rows_mine, bf16[16,768]{1,0:T(8,128)(2,1)S(1)} %collective-permute-done.4.rows_other, ...), custom_call_target="tpu_custom_call" | custom-call | flops 2013265920 | bytes 10082304 | tf_op jit(solution)/shard_map/pallas_call | solution.py:340
  90.8 2.1 %collective-permute-start.19 = (bf16[128,768]{1,0:T(8,128)(2,1)S(1)}, bf16[128,768]{1,0:T(8,128)(2,1)S(1)}, u32[]{:S(2)}, u32[]{:S(2)}) collective-permute-start(bf16[128,768]{1,0:T(8,128)(2,1)S(1)} %get-tuple-element.115.refs_0_), channel_id=1, source_target_pairs={{0,1},{1,0},{2,3},{3,2},{4,5},{5,4},{6,7},{7,6},{8,9},{9,8},{10,11... | collective-permute-start | bytes 589832 | tf_op jit(solution)/shard_map/ppermute | solution.py:29
  94.2 1.6 %collective-permute-start.21 = (bf16[128,768]{1,0:T(8,128)(2,1)S(1)}, bf16[128,768]{1,0:T(8,128)(2,1)S(1)}, u32[]{:S(2)}, u32[]{:S(2)}) collective-permute-start(bf16[128,768]{1,0:T(8,128)(2,1)S(1)} %shard_map.142.refs_1_), channel_id=1, source_target_pairs={{0,1},{1,0},{2,3},{3,2},{4,5},{5,4},{6,7},{7,6},{8,9},{9,8},{10,11... | collective-permute-start | bytes 589832 | tf_op jit(solution)/shard_map/ppermute | solution.py:29
  96.3 3.5 %collective-permute-done.19.a_other = bf16[128,768]{1,0:T(8,128)(2,1)S(1)} collective-permute-done((bf16[128,768]{1,0:T(8,128)(2,1)S(1)}, bf16[128,768]{1,0:T(8,128)(2,1)S(1)}, u32[]{:S(2)}, u32[]{:S(2)}) %collective-permute-start.19) | collective-permute-done | bytes 196640 | tf_op jit(solution)/shard_map/ppermute | solution.py:29
  100.7 4.0 %collective-permute-start.20 = (bf16[128,768]{1,0:T(8,128)(2,1)S(1)}, bf16[128,768]{1,0:T(8,128)(2,1)S(1)}, u32[]{:S(2)}, u32[]{:S(2)}) collective-permute-start(bf16[128,768]{1,0:T(8,128)(2,1)S(1)} %get-tuple-element.123), channel_id=1, source_target_pairs={{2,0},{3,1},{4,2},{5,3},{6,4},{7,5},{8,6},{9,7},{10,8},{11,9},{12,... | collective-permute-start | bytes 589832 | tf_op jit(solution)/shard_map/ppermute | solution.py:29
  105.6 3.8 %collective-permute-start.22 = (bf16[128,768]{1,0:T(8,128)(2,1)S(1)}, bf16[128,768]{1,0:T(8,128)(2,1)S(1)}, u32[]{:S(2)}, u32[]{:S(2)}) collective-permute-start(bf16[128,768]{1,0:T(8,128)(2,1)S(1)} %get-tuple-element.126), channel_id=1, source_target_pairs={{2,0},{3,1},{4,2},{5,3},{6,4},{7,5},{8,6},{9,7},{10,8},{11,9},{12,... | collective-permute-start | bytes 589832 | tf_op jit(solution)/shard_map/ppermute | solution.py:29
  109.5 3.1 %collective-permute-done.22.advanced = bf16[128,768]{1,0:T(8,128)(2,1)S(1)} collective-permute-done((bf16[128,768]{1,0:T(8,128)(2,1)S(1)}, bf16[128,768]{1,0:T(8,128)(2,1)S(1)}, u32[]{:S(2)}, u32[]{:S(2)}) %collective-permute-start.22) | collective-permute-done | bytes 196640 | tf_op jit(solution)/shard_map/ppermute | solution.py:29
  (48 shorter events, 25.9 us)
Async XLA Ops:
  0.6 13.3 %collective-permute-start.5 = (bf16[256,768]{1,0:T(8,128)(2,1)}, bf16[256,768]{1,0:T(8,128)(2,1)S(1)}, u32[]{:S(2)}, u32[]{:S(2)}) collective-permute-start(bf16[256,768]{1,0:T(8,128)(2,1)} %refs_0_.1), channel_id=1, source_target_pairs={{0,1},{1,0},{2,3},{3,2},{4,5},{5,4},{6,7},{7,6},{8,9},{9,8},{10,11... | collective-permute-start | bytes 1179656 | tf_op jit(solution)/shard_map/ppermute | solution.py:29
  3.4 16.7 %collective-permute-start = (bf16[96,1536]{1,0:T(8,128)(2,1)S(1)}, bf16[96,1536]{1,0:T(8,128)(2,1)S(1)}, u32[]{:S(2)}, u32[]{:S(2)}) collective-permute-start(bf16[96,1536]{1,0:T(8,128)(2,1)S(1)} %constant_dynamic-slice_fusion), channel_id=1, source_target_pairs={{0,5},{1,4},{2,7},{3,6},{4,1},{5,0},{6,3},{7,2},{8,13},{9,12},{10,... | collective-permute-start | bytes 884744 | tf_op jit(solution)/shard_map/ppermute | solution.py:29
  5.7 8.3 %collective-permute-start.4 = (bf16[16,768]{1,0:T(8,128)(2,1)S(1)}, bf16[16,768]{1,0:T(8,128)(2,1)S(1)}, u32[]{:S(2)}, u32[]{:S(2)}) collective-permute-start(bf16[16,768]{1,0:T(8,128)(2,1)S(1)} %shard_map.122.rows_mine), channel_id=1, source_target_pairs={{0,1},{1,0},{2,3},{3,2},{4,5},{5,4},{6,7},{7,6},{8,9},{9,8},{10,11... | collective-permute-start | bytes 73736 | tf_op jit(solution)/shard_map/ppermute | solution.py:29
  7.7 8.2 %copy-start = (bf16[256,768]{1,0:T(8,128)(2,1)S(1)}, bf16[256,768]{1,0:T(8,128)(2,1)}, u32[]{:S(2)}) copy-start(bf16[256,768]{1,0:T(8,128)(2,1)} %refs_0_.1) | copy-start | bytes 1179652
  13.9 16.4 %collective-permute-start.7 = (bf16[256,768]{1,0:T(8,128)(2,1)S(1)}, bf16[256,768]{1,0:T(8,128)(2,1)S(1)}, u32[]{:S(2)}, u32[]{:S(2)}) collective-permute-start(bf16[256,768]{1,0:T(8,128)(2,1)S(1)} %collective-permute-done.5.other.refs_1_), channel_id=1, source_target_pairs={{0,2},{1,3},{2,4},{3,5},{4,6},{5,7},{6,8},{7,9},{8,10},{9,11},{10,... | collective-permute-start | bytes 1179656 | tf_op jit(solution)/shard_map/ppermute | solution.py:29
  15.8 14.6 %collective-permute-start.6 = (bf16[256,768]{1,0:T(8,128)(2,1)S(1)}, bf16[256,768]{1,0:T(8,128)(2,1)S(1)}, u32[]{:S(2)}, u32[]{:S(2)}) collective-permute-start(bf16[256,768]{1,0:T(8,128)(2,1)S(1)} %copy-done), channel_id=1, source_target_pairs={{0,2},{1,3},{2,4},{3,5},{4,6},{5,7},{6,8},{7,9},{8,10},{9,11},{10,... | collective-permute-start | bytes 1179656 | tf_op jit(solution)/shard_map/ppermute | solution.py:29
  20.1 16.6 %collective-permute-start.1 = (bf16[96,1536]{1,0:T(8,128)(2,1)S(1)}, bf16[96,1536]{1,0:T(8,128)(2,1)S(1)}, u32[]{:S(2)}, u32[]{:S(2)}) collective-permute-start(bf16[96,1536]{1,0:T(8,128)(2,1)S(1)} %collective-permute-done.own), channel_id=1, source_target_pairs={{0,64},{1,65},{2,66},{3,67},{4,68},{5,69},{6,70},{7,71},{8,72},{9,... | collective-permute-start | bytes 884744 | tf_op jit(solution)/shard_map/ppermute | solution.py:29
  21.7 15.0 %collective-permute-start.2 = (bf16[96,1536]{1,0:T(8,128)(2,1)S(1)}, bf16[96,1536]{1,0:T(8,128)(2,1)S(1)}, u32[]{:S(2)}, u32[]{:S(2)}) collective-permute-start(bf16[96,1536]{1,0:T(8,128)(2,1)S(1)} %collective-permute-done.own), channel_id=1, source_target_pairs={{0,192},{1,193},{2,194},{3,195},{4,196},{5,197},{6,198},{7,199},{8... | collective-permute-start | bytes 884744 | tf_op jit(solution)/shard_map/ppermute | solution.py:29
  22.2 14.5 %collective-permute-start.3 = (bf16[96,1536]{1,0:T(8,128)(2,1)S(1)}, bf16[96,1536]{1,0:T(8,128)(2,1)S(1)}, u32[]{:S(2)}, u32[]{:S(2)}) collective-permute-start(bf16[96,1536]{1,0:T(8,128)(2,1)S(1)} %collective-permute-done.own), channel_id=1, source_target_pairs={{0,56},{1,57},{2,58},{3,59},{4,60},{5,61},{6,62},{7,63},{8,0},{9,1... | collective-permute-start | bytes 884744 | tf_op jit(solution)/shard_map/ppermute | solution.py:29
  30.3 1.8 %copy-start.2 = (s32[128]{0:T(128)S(1)}, s32[128]{0:T(128)}, u32[]{:S(2)}) copy-start(s32[128]{0:T(128)} %starts.11) | copy-start | bytes 1540
  36.7 3.9 %copy-start.1 = (s32[128]{0:T(128)S(1)}, s32[128]{0:T(128)}, u32[]{:S(2)}) copy-start(s32[128]{0:T(128)} %levels.15) | copy-start | bytes 1540
  36.9 9.4 %collective-permute-start.8 = (bf16[4,96,1536]{2,1,0:T(8,128)(2,1)S(1)}, bf16[4,96,1536]{2,1,0:T(8,128)(2,1)S(1)}, u32[]{:S(2)}, u32[]{:S(2)}) collective-permute-start(bf16[4,96,1536]{2,1,0:T(8,128)(2,1)S(1)} %pad_maximum_fusion), channel_id=1, source_target_pairs={{0,2},{1,3},{2,0},{3,1},{4,6},{5,7},{6,4},{7,5},{8,10},{9,11},{10,... | collective-permute-start | bytes 3538952 | tf_op jit(solution)/shard_map/ppermute | solution.py:29
  37.0 9.3 %collective-permute-start.9 = (bf16[128,768]{1,0:T(8,128)(2,1)S(1)}, bf16[128,768]{1,0:T(8,128)(2,1)S(1)}, u32[]{:S(2)}, u32[]{:S(2)}) collective-permute-start(bf16[128,768]{1,0:T(8,128)(2,1)S(1)} %shard_map.126.refs_2_), channel_id=1, source_target_pairs={{0,1},{1,0},{2,3},{3,2},{4,5},{5,4},{6,7},{7,6},{8,9},{9,8},{10,11... | collective-permute-start | bytes 589832 | tf_op jit(solution)/shard_map/ppermute | solution.py:29
  37.8 13.9 %collective-permute-start.12 = (bf16[128,768]{1,0:T(8,128)(2,1)S(1)}, bf16[128,768]{1,0:T(8,128)(2,1)S(1)}, u32[]{:S(2)}, u32[]{:S(2)}) collective-permute-start(bf16[128,768]{1,0:T(8,128)(2,1)S(1)} %shard_map.127.refs_3_), channel_id=1, source_target_pairs={{0,1},{1,0},{2,3},{3,2},{4,5},{5,4},{6,7},{7,6},{8,9},{9,8},{10,11... | collective-permute-start | bytes 589832 | tf_op jit(solution)/shard_map/ppermute | solution.py:29
  47.5 8.6 %collective-permute-start.11 = (bf16[128,1536]{1,0:T(8,128)(2,1)S(1)}, bf16[128,1536]{1,0:T(8,128)(2,1)S(1)}, u32[]{:S(2)}, u32[]{:S(2)}) collective-permute-start(bf16[128,1536]{1,0:T(8,128)(2,1)S(1)} %shard_map.130.refs_0_), channel_id=1, source_target_pairs={{2,0},{3,1},{4,2},{5,3},{6,4},{7,5},{8,6},{9,7},{10,8},{11,9},{12,... | collective-permute-start | bytes 1179656 | tf_op jit(solution)/shard_map/ppermute | solution.py:29
  50.9 7.5 %collective-permute-start.10 = (bf16[256,768]{1,0:T(8,128)(2,1)S(1)}, bf16[256,768]{1,0:T(8,128)(2,1)S(1)}, u32[]{:S(2)}, u32[]{:S(2)}) collective-permute-start(bf16[256,768]{1,0:T(8,128)(2,1)S(1)} %get-tuple-element.85.fresh.refs_0_), channel_id=1, source_target_pairs={{250,255},{251,254}} | collective-permute-start | bytes 1179656 | tf_op jit(solution)/shard_map/ppermute | solution.py:29
  52.8 8.5 %collective-permute-start.13 = (bf16[128,1536]{1,0:T(8,128)(2,1)S(1)}, bf16[128,1536]{1,0:T(8,128)(2,1)S(1)}, u32[]{:S(2)}, u32[]{:S(2)}) collective-permute-start(bf16[128,1536]{1,0:T(8,128)(2,1)S(1)} %shard_map.131.refs_1_), channel_id=1, source_target_pairs={{2,0},{3,1},{4,2},{5,3},{6,4},{7,5},{8,6},{9,7},{10,8},{11,9},{12,... | collective-permute-start | bytes 1179656 | tf_op jit(solution)/shard_map/ppermute | solution.py:29
  57.7 15.5 %collective-permute-start.15 = (bf16[256,768]{1,0:T(8,128)(2,1)S(1)}, bf16[256,768]{1,0:T(8,128)(2,1)S(1)}, u32[]{:S(2)}, u32[]{:S(2)}) collective-permute-start(bf16[256,768]{1,0:T(8,128)(2,1)S(1)} %get-tuple-element.105.fresh.refs_0_), channel_id=1, source_target_pairs={{250,255},{251,254}} | collective-permute-start | bytes 1179656 | tf_op jit(solution)/shard_map/ppermute | solution.py:29
  63.8 9.4 %collective-permute-start.14 = (bf16[128,768]{1,0:T(8,128)(2,1)S(1)}, bf16[128,768]{1,0:T(8,128)(2,1)S(1)}, u32[]{:S(2)}, u32[]{:S(2)}) collective-permute-start(bf16[128,768]{1,0:T(8,128)(2,1)S(1)} %get-tuple-element.97.refs_4_), channel_id=1, source_target_pairs={{0,1},{1,0},{2,3},{3,2},{4,5},{5,4},{6,7},{7,6},{8,9},{9,8},{10,11... | collective-permute-start | bytes 589832 | tf_op jit(solution)/shard_map/ppermute | solution.py:29
  65.9 12.9 %collective-permute-start.17 = (bf16[128,768]{1,0:T(8,128)(2,1)S(1)}, bf16[128,768]{1,0:T(8,128)(2,1)S(1)}, u32[]{:S(2)}, u32[]{:S(2)}) collective-permute-start(bf16[128,768]{1,0:T(8,128)(2,1)S(1)} %shard_map.135.refs_5_), channel_id=1, source_target_pairs={{0,1},{1,0},{2,3},{3,2},{4,5},{5,4},{6,7},{7,6},{8,9},{9,8},{10,11... | collective-permute-start | bytes 589832 | tf_op jit(solution)/shard_map/ppermute | solution.py:29
  74.2 9.9 %collective-permute-start.16 = (bf16[128,1536]{1,0:T(8,128)(2,1)S(1)}, bf16[128,1536]{1,0:T(8,128)(2,1)S(1)}, u32[]{:S(2)}, u32[]{:S(2)}) collective-permute-start(bf16[128,1536]{1,0:T(8,128)(2,1)S(1)} %shard_map.137.refs_0_), channel_id=1, source_target_pairs={{2,0},{3,1},{4,2},{5,3},{6,4},{7,5},{8,6},{9,7},{10,8},{11,9},{12,... | collective-permute-start | bytes 1179656 | tf_op jit(solution)/shard_map/ppermute | solution.py:29
  79.9 8.4 %collective-permute-start.18 = (bf16[128,1536]{1,0:T(8,128)(2,1)S(1)}, bf16[128,1536]{1,0:T(8,128)(2,1)S(1)}, u32[]{:S(2)}, u32[]{:S(2)}) collective-permute-start(bf16[128,1536]{1,0:T(8,128)(2,1)S(1)} %shard_map.138.refs_1_), channel_id=1, source_target_pairs={{2,0},{3,1},{4,2},{5,3},{6,4},{7,5},{8,6},{9,7},{10,8},{11,9},{12,... | collective-permute-start | bytes 1179656 | tf_op jit(solution)/shard_map/ppermute | solution.py:29
  90.8 9.0 %collective-permute-start.19 = (bf16[128,768]{1,0:T(8,128)(2,1)S(1)}, bf16[128,768]{1,0:T(8,128)(2,1)S(1)}, u32[]{:S(2)}, u32[]{:S(2)}) collective-permute-start(bf16[128,768]{1,0:T(8,128)(2,1)S(1)} %get-tuple-element.115.refs_0_), channel_id=1, source_target_pairs={{0,1},{1,0},{2,3},{3,2},{4,5},{5,4},{6,7},{7,6},{8,9},{9,8},{10,11... | collective-permute-start | bytes 589832 | tf_op jit(solution)/shard_map/ppermute | solution.py:29
  94.2 10.5 %collective-permute-start.21 = (bf16[128,768]{1,0:T(8,128)(2,1)S(1)}, bf16[128,768]{1,0:T(8,128)(2,1)S(1)}, u32[]{:S(2)}, u32[]{:S(2)}) collective-permute-start(bf16[128,768]{1,0:T(8,128)(2,1)S(1)} %shard_map.142.refs_1_), channel_id=1, source_target_pairs={{0,1},{1,0},{2,3},{3,2},{4,5},{5,4},{6,7},{7,6},{8,9},{9,8},{10,11... | collective-permute-start | bytes 589832 | tf_op jit(solution)/shard_map/ppermute | solution.py:29
  100.7 8.7 %collective-permute-start.20 = (bf16[128,768]{1,0:T(8,128)(2,1)S(1)}, bf16[128,768]{1,0:T(8,128)(2,1)S(1)}, u32[]{:S(2)}, u32[]{:S(2)}) collective-permute-start(bf16[128,768]{1,0:T(8,128)(2,1)S(1)} %get-tuple-element.123), channel_id=1, source_target_pairs={{2,0},{3,1},{4,2},{5,3},{6,4},{7,5},{8,6},{9,7},{10,8},{11,9},{12,... | collective-permute-start | bytes 589832 | tf_op jit(solution)/shard_map/ppermute | solution.py:29
  105.6 7.0 %collective-permute-start.22 = (bf16[128,768]{1,0:T(8,128)(2,1)S(1)}, bf16[128,768]{1,0:T(8,128)(2,1)S(1)}, u32[]{:S(2)}, u32[]{:S(2)}) collective-permute-start(bf16[128,768]{1,0:T(8,128)(2,1)S(1)} %get-tuple-element.126), channel_id=1, source_target_pairs={{2,0},{3,1},{4,2},{5,3},{6,4},{7,5},{8,6},{9,7},{10,8},{11,9},{12,... | collective-permute-start | bytes 589832 | tf_op jit(solution)/shard_map/ppermute | solution.py:29

commit v8 on v7

--- a/solution.py
+++ b/solution.py
@@ -482,6 +482,7 @@
                 out_products,
                 dtype=jnp.float32,
             )
+            received[1] = swap(after(parts[1], *bases))
         received[0] = after(received[0], *bases, *waits)
         if step == 0:
             w_other = other_projection(piece, parts[1], w_out.shape)

time: 114 us -> 115 us (level)
  no operation moved by 1% of the time
where the time goes in v8:
time: 115 us
  starting transfers between devices  52.6 us (46%)
  Pallas kernels  35 us (30%)
  waiting for transfers between devices  24.8 us (22%)
    ppermute x23, starting transfers between devices, routed(): return lax.ppermute(block, AXES, pairs)  52.6 us
    pallas_call x24, Pallas kernels, kernel_call(): pl.pallas_call(kernel, cost_estimate=pl.CostEstimate(flops=2 * products,...  29.8 us
    ppermute x23, waiting for transfers between devices, routed(): return lax.ppermute(block, AXES, pairs)  24.8 us
    pallas_call x1, Pallas kernels, stage_call(): pl.pallas_call(stage_kernel, out_shape=(pltpu.VMEM(w.shape, w.dtype), plt...  4.05 us
  transfers between devices with their start and end apart: 23, of which 12 were waited for; matrix products, arithmetic and copies ran while one was open for 1% of the time, Pallas kernels for 28%

profile of v8, /device:TPU:12, one launch (start us, length us, event | category | flops | bytes accessed | tf_op | source)
XLA Modules:
  0.0 114.6 jit_solution(18072572769471955053)
XLA Ops:
  3.4 2.2 %collective-permute-start = (bf16[96,1536]{1,0:T(8,128)(2,1)S(1)}, bf16[96,1536]{1,0:T(8,128)(2,1)S(1)}, u32[]{:S(2)}, u32[]{:S(2)}) collective-permute-start(bf16[96,1536]{1,0:T(8,128)(2,1)S(1)} %constant_dynamic-slice_fusion), channel_id=1, source_target_pairs={{0,5},{1,4},{2,7},{3,6},{4,1},{5,0},{6,3},{7,2},{8,13},{9,12},{10,... | collective-permute-start | bytes 884744 | tf_op jit(solution)/shard_map/ppermute | solution.py:29
  5.7 2.0 %collective-permute-start.4 = (bf16[16,768]{1,0:T(8,128)(2,1)S(1)}, bf16[16,768]{1,0:T(8,128)(2,1)S(1)}, u32[]{:S(2)}, u32[]{:S(2)}) collective-permute-start(bf16[16,768]{1,0:T(8,128)(2,1)S(1)} %shard_map.122.rows_mine), channel_id=1, source_target_pairs={{0,1},{1,0},{2,3},{3,2},{4,5},{5,4},{6,7},{7,6},{8,9},{9,8},{10,11... | collective-permute-start | bytes 73736 | tf_op jit(solution)/shard_map/ppermute | solution.py:29
  7.7 4.0 %shard_map.123 = (bf16[3,1536,768]{2,1,0:T(8,128)(2,1)S(1)}, f32[2,768]{1,0:T(2,128)S(1)}, bf16[256,768]{1,0:T(8,128)(2,1)S(1)}, bf16[256,768]{1,0:T(8,128)(2,1)...) custom-call(bf16[3,1536,768]{2,1,0:T(8,128)(2,1)} %bitcast.9, f32[768]{0:T(1024)} %q_hbm.1, f32[768]{0:T(1024)} %k_hbm.1, ...), custom_call_target="tpu_custom_call" | custom-call | tf_op jit(solution)/shard_map/pallas_call | solution.py:134
  11.7 2.2 %collective-permute-done.4.rows_other = bf16[16,768]{1,0:T(8,128)(2,1)S(1)} collective-permute-done((bf16[16,768]{1,0:T(8,128)(2,1)S(1)}, bf16[16,768]{1,0:T(8,128)(2,1)S(1)}, u32[]{:S(2)}, u32[]{:S(2)}) %collective-permute-start.4) | collective-permute-done | bytes 24608 | tf_op jit(solution)/shard_map/ppermute | solution.py:29
  13.9 1.9 %collective-permute-start.7 = (bf16[256,768]{1,0:T(8,128)(2,1)S(1)}, bf16[256,768]{1,0:T(8,128)(2,1)S(1)}, u32[]{:S(2)}, u32[]{:S(2)}) collective-permute-start(bf16[256,768]{1,0:T(8,128)(2,1)S(1)} %collective-permute-done.5.other.refs_1_), channel_id=1, source_target_pairs={{0,2},{1,3},{2,4},{3,5},{4,6},{5,7},{6,8},{7,9},{8,10},{9,11},{10,... | collective-permute-start | bytes 1179656 | tf_op jit(solution)/shard_map/ppermute | solution.py:29
  15.8 3.2 %collective-permute-start.6 = (bf16[256,768]{1,0:T(8,128)(2,1)S(1)}, bf16[256,768]{1,0:T(8,128)(2,1)S(1)}, u32[]{:S(2)}, u32[]{:S(2)}) collective-permute-start(bf16[256,768]{1,0:T(8,128)(2,1)S(1)} %copy-done), channel_id=1, source_target_pairs={{0,2},{1,3},{2,4},{3,5},{4,6},{5,7},{6,8},{7,9},{8,10},{9,11},{10,... | collective-permute-start | bytes 1179656 | tf_op jit(solution)/shard_map/ppermute | solution.py:29
  20.1 1.6 %collective-permute-start.1 = (bf16[96,1536]{1,0:T(8,128)(2,1)S(1)}, bf16[96,1536]{1,0:T(8,128)(2,1)S(1)}, u32[]{:S(2)}, u32[]{:S(2)}) collective-permute-start(bf16[96,1536]{1,0:T(8,128)(2,1)S(1)} %collective-permute-done.own), channel_id=1, source_target_pairs={{0,64},{1,65},{2,66},{3,67},{4,68},{5,69},{6,70},{7,71},{8,72},{9,... | collective-permute-start | bytes 884744 | tf_op jit(solution)/shard_map/ppermute | solution.py:29
  22.2 5.9 %collective-permute-start.3 = (bf16[96,1536]{1,0:T(8,128)(2,1)S(1)}, bf16[96,1536]{1,0:T(8,128)(2,1)S(1)}, u32[]{:S(2)}, u32[]{:S(2)}) collective-permute-start(bf16[96,1536]{1,0:T(8,128)(2,1)S(1)} %collective-permute-done.own), channel_id=1, source_target_pairs={{0,56},{1,57},{2,58},{3,59},{4,60},{5,61},{6,62},{7,63},{8,0},{9,1... | collective-permute-start | bytes 884744 | tf_op jit(solution)/shard_map/ppermute | solution.py:29
  28.0 2.3 %shard_map.124 = (bf16[128,768]{1,0:T(8,128)(2,1)S(1)}, bf16[128,768]{1,0:T(8,128)(2,1)S(1)}, bf16[256,768]{1,0:T(8,128)(2,1)S(1)}, bf16[256,768]{1,0:T(8,128)(2,1)S(1)}) custom-call(bf16[16,768]{1,0:T(8,128)(2,1)S(1)} %shard_map.122.rows_mine, bf16[16,768]{1,0:T(8,128)(2,1)S(1)} %collective-permute-done.4.rows_other, ...), custom_call_target="tpu_custom_call" | custom-call | flops 1811939328 | bytes 7919616 | tf_op jit(solution)/shard_map/pallas_call | solution.py:340
  30.5 1.6 %shard_map.125 = (bf16[256,768]{1,0:T(8,128)(2,1)S(1)}, bf16[256,768]{1,0:T(8,128)(2,1)S(1)}) custom-call(bf16[16,768]{1,0:T(8,128)(2,1)S(1)} %shard_map.122.rows_mine, bf16[16,768]{1,0:T(8,128)(2,1)S(1)} %collective-permute-done.4.rows_other, bf16[3,1536,768]{2,1,0:T(8,128)(2,1)S(1)} %get-tuple-element.68.w, f32[2,768]{1,0:T(2,128)S(1)} %get-tuple-element.69.gains, ...), custom_call_target="tpu_custom_call" | custom-call | flops 1207959552 | bytes 7919616 | tf_op jit(solution)/shard_map/pallas_call | solution.py:340
  34.6 2.1 %collective-permute-done.1.back = bf16[96,1536]{1,0:T(8,128)(2,1)S(1)} collective-permute-done((bf16[96,1536]{1,0:T(8,128)(2,1)S(1)}, bf16[96,1536]{1,0:T(8,128)(2,1)S(1)}, u32[]{:S(2)}, u32[]{:S(2)}) %collective-permute-start.1) | collective-permute-done | bytes 294944 | tf_op jit(solution)/shard_map/ppermute | solution.py:29
  37.8 2.7 %collective-permute-start.12 = (bf16[128,768]{1,0:T(8,128)(2,1)S(1)}, bf16[128,768]{1,0:T(8,128)(2,1)S(1)}, u32[]{:S(2)}, u32[]{:S(2)}) collective-permute-start(bf16[128,768]{1,0:T(8,128)(2,1)S(1)} %shard_map.127.refs_3_), channel_id=1, source_target_pairs={{0,1},{1,0},{2,3},{3,2},{4,5},{5,4},{6,7},{7,6},{8,9},{9,8},{10,11... | collective-permute-start | bytes 589832 | tf_op jit(solution)/shard_map/ppermute | solution.py:29
  41.9 4.3 %collective-permute-done.9.a_other = bf16[128,768]{1,0:T(8,128)(2,1)S(1)} collective-permute-done((bf16[128,768]{1,0:T(8,128)(2,1)S(1)}, bf16[128,768]{1,0:T(8,128)(2,1)S(1)}, u32[]{:S(2)}, u32[]{:S(2)}) %collective-permute-start.9) | collective-permute-done | bytes 196640 | tf_op jit(solution)/shard_map/ppermute | solution.py:29
  47.5 3.4 %collective-permute-start.11 = (bf16[128,1536]{1,0:T(8,128)(2,1)S(1)}, bf16[128,1536]{1,0:T(8,128)(2,1)S(1)}, u32[]{:S(2)}, u32[]{:S(2)}) collective-permute-start(bf16[128,1536]{1,0:T(8,128)(2,1)S(1)} %shard_map.130.refs_0_), channel_id=1, source_target_pairs={{2,0},{3,1},{4,2},{5,3},{6,4},{7,5},{8,6},{9,7},{10,8},{11,9},{12,... | collective-permute-start | bytes 1179656 | tf_op jit(solution)/shard_map/ppermute | solution.py:29
  52.8 3.3 %collective-permute-start.13 = (bf16[128,1536]{1,0:T(8,128)(2,1)S(1)}, bf16[128,1536]{1,0:T(8,128)(2,1)S(1)}, u32[]{:S(2)}, u32[]{:S(2)}) collective-permute-start(bf16[128,1536]{1,0:T(8,128)(2,1)S(1)} %shard_map.131.refs_1_), channel_id=1, source_target_pairs={{2,0},{3,1},{4,2},{5,3},{6,4},{7,5},{8,6},{9,7},{10,8},{11,9},{12,... | collective-permute-start | bytes 1179656 | tf_op jit(solution)/shard_map/ppermute | solution.py:29
  56.1 1.6 %shard_map.132 = (bf16[256,768]{1,0:T(8,128)(2,1)S(1)}, bf16[256,768]{1,0:T(8,128)(2,1)S(1)}) custom-call(bf16[16,768]{1,0:T(8,128)(2,1)S(1)} %shard_map.122.rows_mine, bf16[16,768]{1,0:T(8,128)(2,1)S(1)} %collective-permute-done.4.rows_other, bf16[3,1536,768]{2,1,0:T(8,128)(2,1)S(1)} %get-tuple-element.68.w, f32[2,768]{1,0:T(2,128)S(1)} %get-tuple-element.69.gains, ...), custom_call_target="tpu_custom_call" | custom-call | flops 1207959552 | bytes 7919616 | tf_op jit(solution)/shard_map/pallas_call | solution.py:340
  59.7 1.6 %collective-permute-done.13.rest.refs_3_ = bf16[128,1536]{1,0:T(8,128)(2,1)S(1)} collective-permute-done((bf16[128,1536]{1,0:T(8,128)(2,1)S(1)}, bf16[128,1536]{1,0:T(8,128)(2,1)S(1)}, u32[]{:S(2)}, u32[]{:S(2)}) %collective-permute-start.13) | collective-permute-done | bytes 393248 | tf_op jit(solution)/shard_map/ppermute | solution.py:29
  61.3 2.5 %shard_map.134 = (bf16[128,768]{1,0:T(8,128)(2,1)S(1)}, bf16[128,768]{1,0:T(8,128)(2,1)S(1)}, bf16[256,768]{1,0:T(8,128)(2,1)S(1)}, bf16[256,768]{1,0:T(8,128)(2,1)S(1)}) custom-call(s32[128]{0:T(128)S(1)} %copy-done.2, bf16[16,768]{1,0:T(8,128)(2,1)S(1)} %shard_map.122.rows_mine, bf16[16,768]{1,0:T(8,128)(2,1)S(1)} %collective-permute-done.4.rows_other, ...), custom_call_target="tpu_custom_call" | custom-call | flops 2013265920 | bytes 10082304 | tf_op jit(solution)/shard_map/pallas_call | solution.py:340
  65.9 2.8 %collective-permute-start.17 = (bf16[128,768]{1,0:T(8,128)(2,1)S(1)}, bf16[128,768]{1,0:T(8,128)(2,1)S(1)}, u32[]{:S(2)}, u32[]{:S(2)}) collective-permute-start(bf16[128,768]{1,0:T(8,128)(2,1)S(1)} %shard_map.135.refs_5_), channel_id=1, source_target_pairs={{0,1},{1,0},{2,3},{3,2},{4,5},{5,4},{6,7},{7,6},{8,9},{9,8},{10,11... | collective-permute-start | bytes 589832 | tf_op jit(solution)/shard_map/ppermute | solution.py:29
  68.8 1.4 %shard_map.136 = (f32[128,1536]{1,0:T(8,128)S(1)}, f32[128,1536]{1,0:T(8,128)S(1)}) custom-call(s32[128]{0:T(128)S(1)} %copy-done.1, bf16[16,768]{1,0:T(8,128)(2,1)S(1)} %shard_map.122.rows_mine, bf16[16,768]{1,0:T(8,128)(2,1)S(1)} %collective-permute-done.4.rows_other, bf16[768,1536]{1,0:T(8,128)(2,1)S(1)} %get-tuple-element.84.w_mine, ...), custom_call_target="tpu_custom_call" | custom-call | flops 603979776 | bytes 4374528 | tf_op jit(solution)/shard_map/pallas_call | solution.py:340
  70.1 3.1 %collective-permute-done.14.a_other = bf16[128,768]{1,0:T(8,128)(2,1)S(1)} collective-permute-done((bf16[128,768]{1,0:T(8,128)(2,1)S(1)}, bf16[128,768]{1,0:T(8,128)(2,1)S(1)}, u32[]{:S(2)}, u32[]{:S(2)}) %collective-permute-start.14) | collective-permute-done | bytes 196640 | tf_op jit(solution)/shard_map/ppermute | solution.py:29
  74.2 4.6 %collective-permute-start.16 = (bf16[128,1536]{1,0:T(8,128)(2,1)S(1)}, bf16[128,1536]{1,0:T(8,128)(2,1)S(1)}, u32[]{:S(2)}, u32[]{:S(2)}) collective-permute-start(bf16[128,1536]{1,0:T(8,128)(2,1)S(1)} %shard_map.137.refs_0_), channel_id=1, source_target_pairs={{2,0},{3,1},{4,2},{5,3},{6,4},{7,5},{8,6},{9,7},{10,8},{11,9},{12,... | collective-permute-start | bytes 1179656 | tf_op jit(solution)/shard_map/ppermute | solution.py:29
  79.9 2.1 %collective-permute-start.18 = (bf16[128,1536]{1,0:T(8,128)(2,1)S(1)}, bf16[128,1536]{1,0:T(8,128)(2,1)S(1)}, u32[]{:S(2)}, u32[]{:S(2)}) collective-permute-start(bf16[128,1536]{1,0:T(8,128)(2,1)S(1)} %shard_map.138.refs_1_), channel_id=1, source_target_pairs={{2,0},{3,1},{4,2},{5,3},{6,4},{7,5},{8,6},{9,7},{10,8},{11,9},{12,... | collective-permute-start | bytes 1179656 | tf_op jit(solution)/shard_map/ppermute | solution.py:29
  82.0 2.1 %collective-permute-done.16.chunk.first.refs_2_ = bf16[128,1536]{1,0:T(8,128)(2,1)S(1)} collective-permute-done((bf16[128,1536]{1,0:T(8,128)(2,1)S(1)}, bf16[128,1536]{1,0:T(8,128)(2,1)S(1)}, u32[]{:S(2)}, u32[]{:S(2)}) %collective-permute-start.16) | collective-permute-done | bytes 393248 | tf_op jit(solution)/shard_map/ppermute | solution.py:29
  85.4 1.6 %shard_map.139 = (bf16[256,768]{1,0:T(8,128)(2,1)S(1)}, bf16[256,768]{1,0:T(8,128)(2,1)S(1)}) custom-call(bf16[16,768]{1,0:T(8,128)(2,1)S(1)} %shard_map.122.rows_mine, bf16[16,768]{1,0:T(8,128)(2,1)S(1)} %collective-permute-done.4.rows_other, bf16[3,1536,768]{2,1,0:T(8,128)(2,1)S(1)} %get-tuple-element.68.w, f32[2,768]{1,0:T(2,128)S(1)} %get-tuple-element.69.gains, ...), custom_call_target="tpu_custom_call" | custom-call | flops 1207959552 | bytes 7919616 | tf_op jit(solution)/shard_map/pallas_call | solution.py:340
  88.3 2.5 %shard_map.141 = (bf16[128,768]{1,0:T(8,128)(2,1)S(1)}, bf16[128,768]{1,0:T(8,128)(2,1)S(1)}, bf16[256,768]{1,0:T(8,128)(2,1)S(1)}, bf16[256,768]{1,0:T(8,128)(2,1)S(1)}) custom-call(s32[128]{0:T(128)S(1)} %copy-done.2, bf16[16,768]{1,0:T(8,128)(2,1)S(1)} %shard_map.122.rows_mine, bf16[16,768]{1,0:T(8,128)(2,1)S(1)} %collective-permute-done.4.rows_other, ...), custom_call_target="tpu_custom_call" | custom-call | flops 2013265920 | bytes 10082304 | tf_op jit(solution)/shard_map/pallas_call | solution.py:340
  90.8 2.1 %collective-permute-start.19 = (bf16[128,768]{1,0:T(8,128)(2,1)S(1)}, bf16[128,768]{1,0:T(8,128)(2,1)S(1)}, u32[]{:S(2)}, u32[]{:S(2)}) collective-permute-start(bf16[128,768]{1,0:T(8,128)(2,1)S(1)} %get-tuple-element.116.refs_0_), channel_id=1, source_target_pairs={{0,1},{1,0},{2,3},{3,2},{4,5},{5,4},{6,7},{7,6},{8,9},{9,8},{10,11... | collective-permute-start | bytes 589832 | tf_op jit(solution)/shard_map/ppermute | solution.py:29
  94.7 1.6 %collective-permute-start.21 = (bf16[128,768]{1,0:T(8,128)(2,1)S(1)}, bf16[128,768]{1,0:T(8,128)(2,1)S(1)}, u32[]{:S(2)}, u32[]{:S(2)}) collective-permute-start(bf16[128,768]{1,0:T(8,128)(2,1)S(1)} %shard_map.142.refs_1_), channel_id=1, source_target_pairs={{0,1},{1,0},{2,3},{3,2},{4,5},{5,4},{6,7},{7,6},{8,9},{9,8},{10,11... | collective-permute-start | bytes 589832 | tf_op jit(solution)/shard_map/ppermute | solution.py:29
  96.3 3.6 %collective-permute-done.19.a_other = bf16[128,768]{1,0:T(8,128)(2,1)S(1)} collective-permute-done((bf16[128,768]{1,0:T(8,128)(2,1)S(1)}, bf16[128,768]{1,0:T(8,128)(2,1)S(1)}, u32[]{:S(2)}, u32[]{:S(2)}) %collective-permute-start.19) | collective-permute-done | bytes 196640 | tf_op jit(solution)/shard_map/ppermute | solution.py:29
  100.8 3.9 %collective-permute-start.20 = (bf16[128,768]{1,0:T(8,128)(2,1)S(1)}, bf16[128,768]{1,0:T(8,128)(2,1)S(1)}, u32[]{:S(2)}, u32[]{:S(2)}) collective-permute-start(bf16[128,768]{1,0:T(8,128)(2,1)S(1)} %get-tuple-element.124), channel_id=1, source_target_pairs={{2,0},{3,1},{4,2},{5,3},{6,4},{7,5},{8,6},{9,7},{10,8},{11,9},{12,... | collective-permute-start | bytes 589832 | tf_op jit(solution)/shard_map/ppermute | solution.py:29
  105.6 4.9 %collective-permute-start.22 = (bf16[128,768]{1,0:T(8,128)(2,1)S(1)}, bf16[128,768]{1,0:T(8,128)(2,1)S(1)}, u32[]{:S(2)}, u32[]{:S(2)}) collective-permute-start(bf16[128,768]{1,0:T(8,128)(2,1)S(1)} %get-tuple-element.128), channel_id=1, source_target_pairs={{2,0},{3,1},{4,2},{5,3},{6,4},{7,5},{8,6},{9,7},{10,8},{11,9},{12,... | collective-permute-start | bytes 589832 | tf_op jit(solution)/shard_map/ppermute | solution.py:29
  110.5 3.1 %collective-permute-done.22.advanced = bf16[128,768]{1,0:T(8,128)(2,1)S(1)} collective-permute-done((bf16[128,768]{1,0:T(8,128)(2,1)S(1)}, bf16[128,768]{1,0:T(8,128)(2,1)S(1)}, u32[]{:S(2)}, u32[]{:S(2)}) %collective-permute-start.22) | collective-permute-done | bytes 196640 | tf_op jit(solution)/shard_map/ppermute | solution.py:29
  (48 shorter events, 25.9 us)
Async XLA Ops:
  0.6 13.3 %collective-permute-start.5 = (bf16[256,768]{1,0:T(8,128)(2,1)}, bf16[256,768]{1,0:T(8,128)(2,1)S(1)}, u32[]{:S(2)}, u32[]{:S(2)}) collective-permute-start(bf16[256,768]{1,0:T(8,128)(2,1)} %refs_0_.1), channel_id=1, source_target_pairs={{0,1},{1,0},{2,3},{3,2},{4,5},{5,4},{6,7},{7,6},{8,9},{9,8},{10,11... | collective-permute-start | bytes 1179656 | tf_op jit(solution)/shard_map/ppermute | solution.py:29
  3.4 16.7 %collective-permute-start = (bf16[96,1536]{1,0:T(8,128)(2,1)S(1)}, bf16[96,1536]{1,0:T(8,128)(2,1)S(1)}, u32[]{:S(2)}, u32[]{:S(2)}) collective-permute-start(bf16[96,1536]{1,0:T(8,128)(2,1)S(1)} %constant_dynamic-slice_fusion), channel_id=1, source_target_pairs={{0,5},{1,4},{2,7},{3,6},{4,1},{5,0},{6,3},{7,2},{8,13},{9,12},{10,... | collective-permute-start | bytes 884744 | tf_op jit(solution)/shard_map/ppermute | solution.py:29
  5.7 8.3 %collective-permute-start.4 = (bf16[16,768]{1,0:T(8,128)(2,1)S(1)}, bf16[16,768]{1,0:T(8,128)(2,1)S(1)}, u32[]{:S(2)}, u32[]{:S(2)}) collective-permute-start(bf16[16,768]{1,0:T(8,128)(2,1)S(1)} %shard_map.122.rows_mine), channel_id=1, source_target_pairs={{0,1},{1,0},{2,3},{3,2},{4,5},{5,4},{6,7},{7,6},{8,9},{9,8},{10,11... | collective-permute-start | bytes 73736 | tf_op jit(solution)/shard_map/ppermute | solution.py:29
  7.7 8.2 %copy-start = (bf16[256,768]{1,0:T(8,128)(2,1)S(1)}, bf16[256,768]{1,0:T(8,128)(2,1)}, u32[]{:S(2)}) copy-start(bf16[256,768]{1,0:T(8,128)(2,1)} %refs_0_.1) | copy-start | bytes 1179652
  13.9 16.4 %collective-permute-start.7 = (bf16[256,768]{1,0:T(8,128)(2,1)S(1)}, bf16[256,768]{1,0:T(8,128)(2,1)S(1)}, u32[]{:S(2)}, u32[]{:S(2)}) collective-permute-start(bf16[256,768]{1,0:T(8,128)(2,1)S(1)} %collective-permute-done.5.other.refs_1_), channel_id=1, source_target_pairs={{0,2},{1,3},{2,4},{3,5},{4,6},{5,7},{6,8},{7,9},{8,10},{9,11},{10,... | collective-permute-start | bytes 1179656 | tf_op jit(solution)/shard_map/ppermute | solution.py:29
  15.8 14.6 %collective-permute-start.6 = (bf16[256,768]{1,0:T(8,128)(2,1)S(1)}, bf16[256,768]{1,0:T(8,128)(2,1)S(1)}, u32[]{:S(2)}, u32[]{:S(2)}) collective-permute-start(bf16[256,768]{1,0:T(8,128)(2,1)S(1)} %copy-done), channel_id=1, source_target_pairs={{0,2},{1,3},{2,4},{3,5},{4,6},{5,7},{6,8},{7,9},{8,10},{9,11},{10,... | collective-permute-start | bytes 1179656 | tf_op jit(solution)/shard_map/ppermute | solution.py:29
  20.1 16.6 %collective-permute-start.1 = (bf16[96,1536]{1,0:T(8,128)(2,1)S(1)}, bf16[96,1536]{1,0:T(8,128)(2,1)S(1)}, u32[]{:S(2)}, u32[]{:S(2)}) collective-permute-start(bf16[96,1536]{1,0:T(8,128)(2,1)S(1)} %collective-permute-done.own), channel_id=1, source_target_pairs={{0,64},{1,65},{2,66},{3,67},{4,68},{5,69},{6,70},{7,71},{8,72},{9,... | collective-permute-start | bytes 884744 | tf_op jit(solution)/shard_map/ppermute | solution.py:29
  21.7 15.0 %collective-permute-start.2 = (bf16[96,1536]{1,0:T(8,128)(2,1)S(1)}, bf16[96,1536]{1,0:T(8,128)(2,1)S(1)}, u32[]{:S(2)}, u32[]{:S(2)}) collective-permute-start(bf16[96,1536]{1,0:T(8,128)(2,1)S(1)} %collective-permute-done.own), channel_id=1, source_target_pairs={{0,192},{1,193},{2,194},{3,195},{4,196},{5,197},{6,198},{7,199},{8... | collective-permute-start | bytes 884744 | tf_op jit(solution)/shard_map/ppermute | solution.py:29
  22.2 14.5 %collective-permute-start.3 = (bf16[96,1536]{1,0:T(8,128)(2,1)S(1)}, bf16[96,1536]{1,0:T(8,128)(2,1)S(1)}, u32[]{:S(2)}, u32[]{:S(2)}) collective-permute-start(bf16[96,1536]{1,0:T(8,128)(2,1)S(1)} %collective-permute-done.own), channel_id=1, source_target_pairs={{0,56},{1,57},{2,58},{3,59},{4,60},{5,61},{6,62},{7,63},{8,0},{9,1... | collective-permute-start | bytes 884744 | tf_op jit(solution)/shard_map/ppermute | solution.py:29
  30.3 1.8 %copy-start.2 = (s32[128]{0:T(128)S(1)}, s32[128]{0:T(128)}, u32[]{:S(2)}) copy-start(s32[128]{0:T(128)} %starts.11) | copy-start | bytes 1540
  36.7 3.9 %copy-start.1 = (s32[128]{0:T(128)S(1)}, s32[128]{0:T(128)}, u32[]{:S(2)}) copy-start(s32[128]{0:T(128)} %levels.15) | copy-start | bytes 1540
  36.9 9.4 %collective-permute-start.8 = (bf16[4,96,1536]{2,1,0:T(8,128)(2,1)S(1)}, bf16[4,96,1536]{2,1,0:T(8,128)(2,1)S(1)}, u32[]{:S(2)}, u32[]{:S(2)}) collective-permute-start(bf16[4,96,1536]{2,1,0:T(8,128)(2,1)S(1)} %pad_maximum_fusion), channel_id=1, source_target_pairs={{0,2},{1,3},{2,0},{3,1},{4,6},{5,7},{6,4},{7,5},{8,10},{9,11},{10,... | collective-permute-start | bytes 3538952 | tf_op jit(solution)/shard_map/ppermute | solution.py:29
  37.0 9.3 %collective-permute-start.9 = (bf16[128,768]{1,0:T(8,128)(2,1)S(1)}, bf16[128,768]{1,0:T(8,128)(2,1)S(1)}, u32[]{:S(2)}, u32[]{:S(2)}) collective-permute-start(bf16[128,768]{1,0:T(8,128)(2,1)S(1)} %shard_map.126.refs_2_), channel_id=1, source_target_pairs={{0,1},{1,0},{2,3},{3,2},{4,5},{5,4},{6,7},{7,6},{8,9},{9,8},{10,11... | collective-permute-start | bytes 589832 | tf_op jit(solution)/shard_map/ppermute | solution.py:29
  37.8 13.9 %collective-permute-start.12 = (bf16[128,768]{1,0:T(8,128)(2,1)S(1)}, bf16[128,768]{1,0:T(8,128)(2,1)S(1)}, u32[]{:S(2)}, u32[]{:S(2)}) collective-permute-start(bf16[128,768]{1,0:T(8,128)(2,1)S(1)} %shard_map.127.refs_3_), channel_id=1, source_target_pairs={{0,1},{1,0},{2,3},{3,2},{4,5},{5,4},{6,7},{7,6},{8,9},{9,8},{10,11... | collective-permute-start | bytes 589832 | tf_op jit(solution)/shard_map/ppermute | solution.py:29
  47.5 8.6 %collective-permute-start.11 = (bf16[128,1536]{1,0:T(8,128)(2,1)S(1)}, bf16[128,1536]{1,0:T(8,128)(2,1)S(1)}, u32[]{:S(2)}, u32[]{:S(2)}) collective-permute-start(bf16[128,1536]{1,0:T(8,128)(2,1)S(1)} %shard_map.130.refs_0_), channel_id=1, source_target_pairs={{2,0},{3,1},{4,2},{5,3},{6,4},{7,5},{8,6},{9,7},{10,8},{11,9},{12,... | collective-permute-start | bytes 1179656 | tf_op jit(solution)/shard_map/ppermute | solution.py:29
  50.9 7.5 %collective-permute-start.10 = (bf16[256,768]{1,0:T(8,128)(2,1)S(1)}, bf16[256,768]{1,0:T(8,128)(2,1)S(1)}, u32[]{:S(2)}, u32[]{:S(2)}) collective-permute-start(bf16[256,768]{1,0:T(8,128)(2,1)S(1)} %get-tuple-element.86.fresh.refs_0_), channel_id=1, source_target_pairs={{250,255},{251,254}} | collective-permute-start | bytes 1179656 | tf_op jit(solution)/shard_map/ppermute | solution.py:29
  52.8 8.5 %collective-permute-start.13 = (bf16[128,1536]{1,0:T(8,128)(2,1)S(1)}, bf16[128,1536]{1,0:T(8,128)(2,1)S(1)}, u32[]{:S(2)}, u32[]{:S(2)}) collective-permute-start(bf16[128,1536]{1,0:T(8,128)(2,1)S(1)} %shard_map.131.refs_1_), channel_id=1, source_target_pairs={{2,0},{3,1},{4,2},{5,3},{6,4},{7,5},{8,6},{9,7},{10,8},{11,9},{12,... | collective-permute-start | bytes 1179656 | tf_op jit(solution)/shard_map/ppermute | solution.py:29
  57.7 15.5 %collective-permute-start.15 = (bf16[256,768]{1,0:T(8,128)(2,1)S(1)}, bf16[256,768]{1,0:T(8,128)(2,1)S(1)}, u32[]{:S(2)}, u32[]{:S(2)}) collective-permute-start(bf16[256,768]{1,0:T(8,128)(2,1)S(1)} %get-tuple-element.106.fresh.refs_0_), channel_id=1, source_target_pairs={{250,255},{251,254}} | collective-permute-start | bytes 1179656 | tf_op jit(solution)/shard_map/ppermute | solution.py:29
  63.8 9.4 %collective-permute-start.14 = (bf16[128,768]{1,0:T(8,128)(2,1)S(1)}, bf16[128,768]{1,0:T(8,128)(2,1)S(1)}, u32[]{:S(2)}, u32[]{:S(2)}) collective-permute-start(bf16[128,768]{1,0:T(8,128)(2,1)S(1)} %get-tuple-element.98.refs_4_), channel_id=1, source_target_pairs={{0,1},{1,0},{2,3},{3,2},{4,5},{5,4},{6,7},{7,6},{8,9},{9,8},{10,11... | collective-permute-start | bytes 589832 | tf_op jit(solution)/shard_map/ppermute | solution.py:29
  65.9 12.9 %collective-permute-start.17 = (bf16[128,768]{1,0:T(8,128)(2,1)S(1)}, bf16[128,768]{1,0:T(8,128)(2,1)S(1)}, u32[]{:S(2)}, u32[]{:S(2)}) collective-permute-start(bf16[128,768]{1,0:T(8,128)(2,1)S(1)} %shard_map.135.refs_5_), channel_id=1, source_target_pairs={{0,1},{1,0},{2,3},{3,2},{4,5},{5,4},{6,7},{7,6},{8,9},{9,8},{10,11... | collective-permute-start | bytes 589832 | tf_op jit(solution)/shard_map/ppermute | solution.py:29
  74.2 9.9 %collective-permute-start.16 = (bf16[128,1536]{1,0:T(8,128)(2,1)S(1)}, bf16[128,1536]{1,0:T(8,128)(2,1)S(1)}, u32[]{:S(2)}, u32[]{:S(2)}) collective-permute-start(bf16[128,1536]{1,0:T(8,128)(2,1)S(1)} %shard_map.137.refs_0_), channel_id=1, source_target_pairs={{2,0},{3,1},{4,2},{5,3},{6,4},{7,5},{8,6},{9,7},{10,8},{11,9},{12,... | collective-permute-start | bytes 1179656 | tf_op jit(solution)/shard_map/ppermute | solution.py:29
  79.9 8.4 %collective-permute-start.18 = (bf16[128,1536]{1,0:T(8,128)(2,1)S(1)}, bf16[128,1536]{1,0:T(8,128)(2,1)S(1)}, u32[]{:S(2)}, u32[]{:S(2)}) collective-permute-start(bf16[128,1536]{1,0:T(8,128)(2,1)S(1)} %shard_map.138.refs_1_), channel_id=1, source_target_pairs={{2,0},{3,1},{4,2},{5,3},{6,4},{7,5},{8,6},{9,7},{10,8},{11,9},{12,... | collective-permute-start | bytes 1179656 | tf_op jit(solution)/shard_map/ppermute | solution.py:29
  90.8 9.1 %collective-permute-start.19 = (bf16[128,768]{1,0:T(8,128)(2,1)S(1)}, bf16[128,768]{1,0:T(8,128)(2,1)S(1)}, u32[]{:S(2)}, u32[]{:S(2)}) collective-permute-start(bf16[128,768]{1,0:T(8,128)(2,1)S(1)} %get-tuple-element.116.refs_0_), channel_id=1, source_target_pairs={{0,1},{1,0},{2,3},{3,2},{4,5},{5,4},{6,7},{7,6},{8,9},{9,8},{10,11... | collective-permute-start | bytes 589832 | tf_op jit(solution)/shard_map/ppermute | solution.py:29
  94.7 10.0 %collective-permute-start.21 = (bf16[128,768]{1,0:T(8,128)(2,1)S(1)}, bf16[128,768]{1,0:T(8,128)(2,1)S(1)}, u32[]{:S(2)}, u32[]{:S(2)}) collective-permute-start(bf16[128,768]{1,0:T(8,128)(2,1)S(1)} %shard_map.142.refs_1_), channel_id=1, source_target_pairs={{0,1},{1,0},{2,3},{3,2},{4,5},{5,4},{6,7},{7,6},{8,9},{9,8},{10,11... | collective-permute-start | bytes 589832 | tf_op jit(solution)/shard_map/ppermute | solution.py:29
  100.8 9.7 %collective-permute-start.20 = (bf16[128,768]{1,0:T(8,128)(2,1)S(1)}, bf16[128,768]{1,0:T(8,128)(2,1)S(1)}, u32[]{:S(2)}, u32[]{:S(2)}) collective-permute-start(bf16[128,768]{1,0:T(8,128)(2,1)S(1)} %get-tuple-element.124), channel_id=1, source_target_pairs={{2,0},{3,1},{4,2},{5,3},{6,4},{7,5},{8,6},{9,7},{10,8},{11,9},{12,... | collective-permute-start | bytes 589832 | tf_op jit(solution)/shard_map/ppermute | solution.py:29
  105.6 8.0 %collective-permute-start.22 = (bf16[128,768]{1,0:T(8,128)(2,1)S(1)}, bf16[128,768]{1,0:T(8,128)(2,1)S(1)}, u32[]{:S(2)}, u32[]{:S(2)}) collective-permute-start(bf16[128,768]{1,0:T(8,128)(2,1)S(1)} %get-tuple-element.128), channel_id=1, source_target_pairs={{2,0},{3,1},{4,2},{5,3},{6,4},{7,5},{8,6},{9,7},{10,8},{11,9},{12,... | collective-permute-start | bytes 589832 | tf_op jit(solution)/shard_map/ppermute | solution.py:29
